TPU v7x, 32 devices: a whole 2x2x4 slice. The times are simulated.
32 devices in a mesh: energy: 16 (over z, y, x), slab: 2 (over core).
Axes of the slice: x: 2, y: 2, z: 4, core: 2. Of those that a mesh axis runs over, the one named last changes fastest.
Arguments:
- lesser_free: float32 [32, 144, 256], P('energy', None, 'slab'), may hold values from -6 to 6
- greater_free: float32 [32, 144, 256], P('energy', None, 'slab'), may hold values from -6 to 6
- retarded: float32 [32, 144, 256], P('energy', None, 'slab'), may hold values from -1.75 to 1.75
- coupling: float32 [12, 144, 256], P(None, None, 'slab'), may hold values from -0.875 to 0.875
- neighbour_offsets: int32 [12, 256], P(None, 'slab'), may hold values from -32 to 32, as said below
- phonon_shift: int32 [64], replicated, may hold values from 1 to 16, as said below
- phonon_coupling: float32 [64], replicated, may hold values from 0.01 to 0.1
- phonon_occupation: float32 [64], replicated, may hold values from 0.05 to 5
Outputs:
- green_lesser: float32 [32, 144, 256], P('energy', None, 'slab')
- green_greater: float32 [32, 144, 256], P('energy', None, 'slab')
Inputs may be any that keep to these rules, and one draw needn't show every extreme that they name: `neighbour_offsets`: each atom's 12 offsets are distinct and nonzero. `phonon_shift`: several frequencies may share a shift.
All inputs are finite; a program needn't handle non-finite values.
Results may differ from a plain program's by a relative error of at most 0.0003.
Values sent between devices are 32-bit elements; how exact they have to be, the bound alone decides.
No kernel may reach another device: no remote copies, remote signals or barrier semaphores. Data moves between devices by JAX's collectives and lax.ppermute only.
A program may use at most 64 MiB of HBM per device.

v0:
```python
import functools

import jax
import jax.numpy as jnp
from jax import lax
from jax.experimental import pallas as pl
from jax.experimental.pallas import tpu as pltpu
from jax.sharding import PartitionSpec as P

NORB = 12
NB = 12
HW = 32
ITERS = 2
ROWS = 8
FUSED = 1

TOP_RANK = lax.Precision.HIGHEST
PARAMS = pltpu.CompilerParams(vmem_limit_bytes=24 * 1024 * 1024)


def tiles(count):
    return [(at, min(ROWS, count - at)) for at in range(0, count, ROWS)]


def spread_rows(target, base, row, source, first, count):
    for at, size in tiles(count):
        rows = pl.ds((base + at) * ROWS + row, size, stride=ROWS)
        target[rows, :] = source(first + at, size)


def prep_coupling_kernel(rows, coupling, inside, out):
    group = ROWS // rows
    pairs = coupling.shape[1]
    for n in range(NB):
        valid = inside[n : n + 1, :]
        for row in range(rows):
            spread_rows(
                out,
                (n // group) * pairs,
                (n % group) * rows + row,
                lambda at, size: coupling[n, at : at + size, :] * valid,
                0,
                pairs,
            )


def prep_dressing_kernel(rows, retarded, shifts, coupled, occupied, left, right, mixing):
    energies, pairs, _ = retarded.shape
    total = mixing.shape[1]
    share = pairs * rows // ROWS
    for row in range(ROWS):
        read = lambda at, size: retarded[row % energies, at : at + size, :]
        spread_rows(left, 0, row, read, row // rows * share, share)
        spread_rows(right, 0, row, read, 0, pairs)
    places = lax.broadcasted_iota(jnp.int32, (total, total), 0)
    gap = lax.broadcasted_iota(jnp.int32, (total, total), 1) - places

    def add_mode(mode, kernels):
        lesser, greater = kernels
        shift = shifts[mode]
        absorb = coupled[mode] * occupied[mode]
        emit = coupled[mode] * (occupied[mode] + 1.0)
        ahead = gap == shift
        behind = gap == -shift
        lesser = lesser + jnp.where(ahead, emit, 0.0) + jnp.where(behind, absorb, 0.0)
        greater = greater + jnp.where(ahead, absorb, 0.0) + jnp.where(behind, emit, 0.0)
        return lesser, greater

    empty = jnp.zeros((total, total), jnp.float32)
    lesser, greater = lax.fori_loop(0, shifts.shape[0], add_mode, (empty, empty))
    mixing[0] = lesser
    mixing[1] = greater


def couple_kernel(fused, *refs):
    near, far = refs[:fused], refs[fused : 2 * fused]
    lanes, is_near, links_hbm, out = refs[2 * fused : 2 * fused + 4]
    own, other, gathered_a, gathered_b, total, links, sems = refs[2 * fused + 4 :]
    energies, pairs, atoms = near[0].shape
    rows = fused * energies
    group = ROWS // rows
    groups = NB // group
    copies = [
        pltpu.make_async_copy(links_hbm.at[g], links.at[g], sems.at[g]) for g in range(groups)
    ]
    for copy in copies:
        copy.start()
    for row in range(ROWS):
        function, energy = row % rows // energies, row % energies
        for target, sources in ((own, near), (other, far)):
            source = sources[function]
            spread_rows(
                target, 0, row, lambda at, size: source[energy, at : at + size, :], 0, pairs
            )
    buffers = (gathered_a, gathered_b)

    def gather(g, first, count):
        target = buffers[g % 2]
        lane, mine = lanes[g], is_near[g] != 0
        for at in range(count):
            pair = first + at
            rows_at = pl.ds(pl.multiple_of(pair * ROWS, ROWS), ROWS)
            inner = jnp.take_along_axis(own[rows_at, :], lane, axis=1, mode="promise_in_bounds")
            outer = jnp.take_along_axis(other[rows_at, :], lane, axis=1, mode="promise_in_bounds")
            target[pair] = jnp.where(mine, inner, outer)

    blocked = 2
    steps = NORB // blocked
    chunk = pairs // steps
    lax.fori_loop(0, steps, lambda step, _: gather(0, step * chunk, chunk), None)
    for g in range(groups):
        copies[g].wait()
        source = buffers[g % 2]

        def block_row(step, _):
            first = step * blocked
            inner = [[None] * NORB for _ in range(blocked)]
            for j in range(NORB):
                left = [links[g, (first + b) * NORB + j] for b in range(blocked)]
                for l in range(NORB):
                    value = source[j * NORB + l]
                    for b in range(blocked):
                        term = left[b] * value
                        inner[b][l] = term if j == 0 else inner[b][l] + term
            for k in range(NORB):
                sums = [None] * blocked
                for l in range(NORB):
                    right = links[g, k * NORB + l]
                    for b in range(blocked):
                        term = inner[b][l] * right
                        sums[b] = term if l == 0 else sums[b] + term
                for b in range(blocked):
                    at = (first + b) * NORB + k
                    value = sums[b] if g == 0 else total[at] + sums[b]
                    if g < groups - 1:
                        total[at] = value
                    else:
                        width = ROWS // 2
                        while width >= rows:
                            value = value + pltpu.roll(value, width, 0)
                            width //= 2
                        out[at] = value[:rows]
            if g < groups - 1:
                gather(g + 1, step * chunk, chunk)

        lax.fori_loop(0, steps, block_row, None)
    for at in range(pairs, out.shape[0]):
        out[at] = jnp.zeros((rows, atoms), jnp.float32)


def mix_kernel(fused, mixing, blocks, out, before, after):
    parts, share, rows, atoms = blocks.shape
    energies = rows // fused
    for f in range(fused):
        some = slice(f * energies, (f + 1) * energies)
        for part in range(parts):
            for pair in range(share):
                before[part * energies : (part + 1) * energies, pair * atoms : (pair + 1) * atoms] = (
                    blocks[part, pair, some, :]
                )
        after[...] = jnp.dot(
            mixing[f], before[...], precision=TOP_RANK, preferred_element_type=jnp.float32
        )
        for part in range(parts):
            for pair in range(share):
                out[part, pair, some, :] = after[
                    part * energies : (part + 1) * energies, pair * atoms : (pair + 1) * atoms
                ]


def dress_kernel(fused, *refs):
    sigma, left, right = refs[:3]
    free, out = refs[3 : 3 + fused], refs[3 + fused : 3 + 2 * fused]
    copied, dressed = refs[3 + 2 * fused :]
    energies, pairs, atoms = free[0].shape
    rows = fused * energies
    parts = ROWS // rows
    share = pairs // parts
    for pair in range(pairs):
        value = sigma[pair]
        for part in range(parts):
            copied[pair, part * rows : (part + 1) * rows, :] = value
    for i in range(NORB // parts):
        inner = [None] * NORB
        for j in range(NORB):
            factor = left[i * NORB + j]
            for l in range(NORB):
                term = factor * copied[j * NORB + l]
                inner[l] = term if j == 0 else inner[l] + term
        for k in range(NORB):
            value = inner[0] * right[k * NORB]
            for l in range(1, NORB):
                value = value + inner[l] * right[k * NORB + l]
            at = (i * NORB + k) * ROWS
            dressed[at : at + ROWS, :] = value
    for row in range(ROWS):
        function, energy, part = row % rows // energies, row % energies, row // rows
        for at, size in tiles(share):
            first = part * share + at
            piece = dressed[pl.ds(at * ROWS + row, size, stride=ROWS), :]
            out[function][energy, first : first + size, :] = (
                free[function][energy, first : first + size, :] + piece
            )


def call(kernel, outs, scratch, flops, *operands, spaces=None):
    shapes = [jax.ShapeDtypeStruct(dims, jnp.float32) for dims in outs]
    vmem = pl.BlockSpec(memory_space=pltpu.VMEM)
    moved = sum(x.size for x in operands) + sum(x.size for x in shapes)
    return pl.pallas_call(
        kernel,
        out_shape=shapes,
        in_specs=spaces or [vmem] * len(operands),
        out_specs=[vmem] * len(shapes),
        scratch_shapes=scratch,
        compiler_params=PARAMS,
        cost_estimate=pl.CostEstimate(
            flops=flops, bytes_accessed=4 * moved, transcendentals=0
        ),
    )(*operands)


def beside(block):
    count = lax.axis_size("slab")
    if count == 2:
        return lax.ppermute(block, "slab", [(0, 1), (1, 0)])
    forward = [(i, i + 1) for i in range(count - 1)]
    backward = [(target, source) for source, target in forward]
    axis = block.ndim - 1
    atoms = block.shape[axis]
    low = lax.ppermute(lax.slice_in_dim(block, atoms - HW, atoms, axis=axis), "slab", forward)
    high = lax.ppermute(lax.slice_in_dim(block, 0, HW, axis=axis), "slab", backward)
    gap = jnp.zeros(block.shape[:-1] + (atoms - 2 * HW,), block.dtype)
    return jnp.concatenate([high, gap, low], axis=axis)


def body(
    lesser_free,
    greater_free,
    retarded,
    coupling,
    neighbour_offsets,
    phonon_shift,
    phonon_coupling,
    phonon_occupation,
):
    energies, pairs, atoms = lesser_free.shape
    fused = FUSED
    rows = fused * energies
    group = ROWS // rows
    groups = NB // group
    parts = lax.axis_size("energy")
    share = -(-pairs // parts)
    total = energies * parts
    vmem = pl.BlockSpec(memory_space=pltpu.VMEM)
    smem = pl.BlockSpec(memory_space=pltpu.SMEM)
    away = pl.BlockSpec(memory_space=pl.ANY)

    targets = neighbour_offsets + jnp.arange(atoms, dtype=jnp.int32)[None, :]
    placed = targets + lax.axis_index("slab") * atoms
    inside = (placed >= 0) & (placed < lax.axis_size("slab") * atoms)

    def widened(values):
        return jnp.broadcast_to(values[:, None, :], (NB, rows, atoms)).reshape(groups, ROWS, atoms)

    lanes = widened(jnp.remainder(targets, atoms))
    is_near = widened(((targets >= 0) & (targets < atoms)).astype(jnp.int32))

    free = (lesser_free, greater_free)
    chains = [free[at : at + fused] for at in range(0, 2, fused)]
    greens = list(chains)
    halos = [tuple(beside(g) for g in chain) for chain in greens]

    (links,) = call(
        functools.partial(prep_coupling_kernel, rows),
        [(groups * pairs * ROWS, atoms)],
        [],
        coupling.size * rows,
        coupling,
        inside.astype(jnp.float32),
    )
    links = links.reshape(groups, pairs, ROWS, atoms)
    left, right, mixing = call(
        functools.partial(prep_dressing_kernel, rows),
        [(pairs * rows, atoms), (pairs * ROWS, atoms), (2, total, total)],
        [],
        retarded.size * ROWS,
        retarded,
        phonon_shift,
        phonon_coupling,
        phonon_occupation,
        spaces=[vmem, smem, smem, smem],
    )
    left = left.reshape(pairs * rows // ROWS, ROWS, atoms)
    right = right.reshape(pairs, ROWS, atoms)

    wide = pltpu.VMEM((pairs * ROWS, atoms), jnp.float32)
    deep = pltpu.VMEM((pairs, ROWS, atoms), jnp.float32)
    flat = pltpu.VMEM((total, share * atoms), jnp.float32)
    work = 4 * NORB * rows * pairs * atoms

    for step in range(ITERS):
        coupled = [
            call(
                functools.partial(couple_kernel, fused),
                [(parts * share, rows, atoms)],
                [
                    wide,
                    wide,
                    deep,
                    deep,
                    deep,
                    pltpu.VMEM(links.shape, jnp.float32),
                    pltpu.SemaphoreType.DMA((groups,)),
                ],
                NB * work,
                *green,
                *halo,
                lanes,
                is_near,
                links,
                spaces=[vmem] * (2 * fused + 2) + [away],
            )[0]
            for green, halo in zip(greens, halos)
        ]
        gathered = [
            lax.all_to_all(x.reshape(parts, share, rows, atoms), "energy", 0, 0) for x in coupled
        ]
        mixed = [
            call(
                functools.partial(mix_kernel, fused),
                [x.shape],
                [flat, flat],
                2 * total * x.size,
                mixing[at * fused : (at + 1) * fused],
                x,
            )[0]
            for at, x in enumerate(gathered)
        ]
        sigma = [
            lax.all_to_all(x, "energy", 0, 0).reshape(parts * share, rows, atoms) for x in mixed
        ]
        greens = [
            call(
                functools.partial(dress_kernel, fused),
                [lesser_free.shape] * fused,
                [deep, pltpu.VMEM((pairs * rows, atoms), jnp.float32)],
                work,
                x,
                left,
                right,
                *chain,
            )
            for x, chain in zip(sigma, chains)
        ]
        if step < ITERS - 1:
            halos = [tuple(beside(g) for g in chain) for chain in greens]
    return tuple(g for chain in greens for g in chain)


def solution(mesh):
    placed = (
        P("energy", None, "slab"),
        P("energy", None, "slab"),
        P("energy", None, "slab"),
        P(None, None, "slab"),
        P(None, "slab"),
        P(),
        P(),
        P(),
    )
    return jax.shard_map(
        body,
        mesh=mesh,
        in_specs=placed,
        out_specs=(P("energy", None, "slab"), P("energy", None, "slab")),
        check_vma=False,
    )
```

profile of v0, /device:TPU:0, one launch (start us, length us, event | category | flops | bytes accessed | tf_op | source)
XLA Modules:
  0.0 112.0 jit_solution(12813686914872673784)
XLA Ops:
  1.9 1.2 %copy-done.2 = f32[12,144,128]{2,1,0:T(8,128)S(1)} copy-done((f32[12,144,128]{2,1,0:T(8,128)S(1)}, f32[12,144,128]{2,1,0:T(8,128)}, u32[]{:S(2)}) %copy-start.2) | copy-done | bytes 884760
  3.8 4.9 %shard_map.103 = f32[144,2,128]{2,1,0:T(2,128)} custom-call(f32[2,144,128]{2,1,0:T(8,128)S(1)} %copy-done, f32[2,144,128]{2,1,0:T(8,128)S(1)} %collective-permute-done.2.refs_1_, s32[3,8,128]{2,1,0:T(8,128)S(1)} %bitcast.33, s32[3,8,128]{2,1,0:T(8,128)S(1)} %bitcast.29, f32[3,144,8,128]{3,2,1,0:T(8,128)S(1)} %bitcast.13), custom_call_target="tpu_custom_call" | custom-call | flops 21233664 | bytes 2236416 | tf_op jit(solution)/shard_map/pallas_call | solution.py:210
  8.8 8.0 %all-to-all-start.4 = ((f32[16,9,2,128]{3,2,1,0:T(2,128)}), f32[16,9,2,128]{3,2,1,0:T(2,128)S(1)}, u32[]{:S(2)}, u32[]{:S(2)}) async-start(f32[16,9,2,128]{3,2,1,0:T(2,128)} %bitcast.9), calls=%async_computation.4 | async-start | bytes 294912 | tf_op jit(solution)/shard_map/all_to_all | solution.py:327
  17.1 1.2 %collective-permute-done.refs_1_ = f32[2,144,128]{2,1,0:T(8,128)S(1)} collective-permute-done((f32[2,144,128]{2,1,0:T(8,128)S(1)}, f32[2,144,128]{2,1,0:T(8,128)S(1)}, u32[]{:S(2)}, u32[]{:S(2)}) %collective-permute-start) | collective-permute-done | bytes 147488 | tf_op jit(solution)/shard_map/ppermute | solution.py:226
  18.2 4.9 %shard_map.97 = f32[144,2,128]{2,1,0:T(2,128)} custom-call(f32[2,144,128]{2,1,0:T(8,128)S(1)} %copy-done.1, f32[2,144,128]{2,1,0:T(8,128)S(1)} %collective-permute-done.refs_1_, s32[3,8,128]{2,1,0:T(8,128)S(1)} %bitcast.34, s32[3,8,128]{2,1,0:T(8,128)S(1)} %bitcast.30, f32[3,144,8,128]{3,2,1,0:T(8,128)S(1)} %bitcast.14), custom_call_target="tpu_custom_call" | custom-call | flops 21233664 | bytes 2236416 | tf_op jit(solution)/shard_map/pallas_call | solution.py:210
  23.2 1.9 %all-to-all-done.4.blocks = f32[16,9,2,128]{3,2,1,0:T(2,128)S(1)} async-done(((f32[16,9,2,128]{3,2,1,0:T(2,128)}), f32[16,9,2,128]{3,2,1,0:T(2,128)S(1)}, u32[]{:S(2)}, u32[]{:S(2)}) %all-to-all-start.4) | async-done | bytes 147488 | tf_op jit(solution)/shard_map/all_to_all | solution.py:327
  25.1 5.0 %all-to-all-start = ((f32[16,9,2,128]{3,2,1,0:T(2,128)}), f32[16,9,2,128]{3,2,1,0:T(2,128)S(1)}, u32[]{:S(2)}, u32[]{:S(2)}) async-start(f32[16,9,2,128]{3,2,1,0:T(2,128)} %bitcast.3), calls=%async_computation | async-start | bytes 294912 | tf_op jit(solution)/shard_map/all_to_all | solution.py:327
  30.1 1.4 %shard_map.95 = (f32[288,128]{1,0:T(8,128)S(1)}, f32[1152,128]{1,0:T(8,128)S(1)}, f32[2,32,32]{2,1,0:T(8,128)S(1)}) custom-call(f32[2,144,128]{2,1,0:T(8,128)S(1)} %copy-done.3, s32[64]{0:T(128)S(1)} %copy-done.4, f32[64]{0:T(128)S(1)} %copy-done.5, f32[64]{0:T(128)S(1)} %copy-done.6), custom_call_target="tpu_custom_call" | custom-call | flops 294912 | bytes 893696 | tf_op jit(solution)/shard_map/pallas_call | solution.py:210
  32.5 5.5 %all-to-all-done.blocks = f32[16,9,2,128]{3,2,1,0:T(2,128)S(1)} async-done(((f32[16,9,2,128]{3,2,1,0:T(2,128)}), f32[16,9,2,128]{3,2,1,0:T(2,128)S(1)}, u32[]{:S(2)}, u32[]{:S(2)}) %all-to-all-start) | async-done | bytes 147488 | tf_op jit(solution)/shard_map/all_to_all | solution.py:327
  38.0 3.5 %all-to-all-start.5 = ((f32[16,9,2,128]{3,2,1,0:T(2,128)}), f32[16,9,2,128]{3,2,1,0:T(2,128)S(1)}, u32[]{:S(2)}, u32[]{:S(2)}) async-start(f32[16,9,2,128]{3,2,1,0:T(2,128)} %shard_map.104), calls=%async_computation.5 | async-start | bytes 294912 | tf_op jit(solution)/shard_map/all_to_all | solution.py:341
  42.5 6.9 %all-to-all-done.5 = f32[16,9,2,128]{3,2,1,0:T(2,128)S(1)} async-done(((f32[16,9,2,128]{3,2,1,0:T(2,128)}), f32[16,9,2,128]{3,2,1,0:T(2,128)S(1)}, u32[]{:S(2)}, u32[]{:S(2)}) %all-to-all-start.5) | async-done | bytes 147488 | tf_op jit(solution)/shard_map/all_to_all | solution.py:341
  49.4 3.5 %all-to-all-start.1 = ((f32[16,9,2,128]{3,2,1,0:T(2,128)}), f32[16,9,2,128]{3,2,1,0:T(2,128)S(1)}, u32[]{:S(2)}, u32[]{:S(2)}) async-start(f32[16,9,2,128]{3,2,1,0:T(2,128)} %shard_map.98), calls=%async_computation.1 | async-start | bytes 294912 | tf_op jit(solution)/shard_map/all_to_all | solution.py:341
  53.4 1.4 %collective-permute-done.3.refs_1_ = f32[2,144,128]{2,1,0:T(8,128)S(1)} collective-permute-done((f32[2,144,128]{2,1,0:T(8,128)S(1)}, f32[2,144,128]{2,1,0:T(8,128)S(1)}, u32[]{:S(2)}, u32[]{:S(2)}) %collective-permute-start.3) | collective-permute-done | bytes 147488 | tf_op jit(solution)/shard_map/ppermute | solution.py:226
  54.8 4.9 %shard_map.106 = f32[144,2,128]{2,1,0:T(2,128)} custom-call(f32[2,144,128]{2,1,0:T(8,128)S(1)} %shard_map.105.refs_0_, f32[2,144,128]{2,1,0:T(8,128)S(1)} %collective-permute-done.3.refs_1_, s32[3,8,128]{2,1,0:T(8,128)S(1)} %bitcast.35, s32[3,8,128]{2,1,0:T(8,128)S(1)} %bitcast.31, f32[3,144,8,128]{3,2,1,0:T(8,128)S(1)} %bitcast.15), custom_call_target="tpu_custom_call" | custom-call | flops 21233664 | bytes 2236416 | tf_op jit(solution)/shard_map/pallas_call | solution.py:210
  60.8 5.8 %all-to-all-start.6 = ((f32[16,9,2,128]{3,2,1,0:T(2,128)}), f32[16,9,2,128]{3,2,1,0:T(2,128)S(1)}, u32[]{:S(2)}, u32[]{:S(2)}) async-start(f32[16,9,2,128]{3,2,1,0:T(2,128)} %bitcast.11), calls=%async_computation.6 | async-start | bytes 294912 | tf_op jit(solution)/shard_map/all_to_all | solution.py:327
  67.1 1.4 %collective-permute-done.1.refs_1_ = f32[2,144,128]{2,1,0:T(8,128)S(1)} collective-permute-done((f32[2,144,128]{2,1,0:T(8,128)S(1)}, f32[2,144,128]{2,1,0:T(8,128)S(1)}, u32[]{:S(2)}, u32[]{:S(2)}) %collective-permute-start.1) | collective-permute-done | bytes 147488 | tf_op jit(solution)/shard_map/ppermute | solution.py:226
  68.4 4.9 %shard_map.100 = f32[144,2,128]{2,1,0:T(2,128)} custom-call(f32[2,144,128]{2,1,0:T(8,128)S(1)} %shard_map.99.refs_0_, f32[2,144,128]{2,1,0:T(8,128)S(1)} %collective-permute-done.1.refs_1_, s32[3,8,128]{2,1,0:T(8,128)S(1)} %bitcast.36, s32[3,8,128]{2,1,0:T(8,128)S(1)} %bitcast.32, f32[3,144,8,128]{3,2,1,0:T(8,128)S(1)} %bitcast.16), custom_call_target="tpu_custom_call" | custom-call | flops 21233664 | bytes 2236416 | tf_op jit(solution)/shard_map/pallas_call | solution.py:210
  73.3 1.2 %all-to-all-done.6.blocks = f32[16,9,2,128]{3,2,1,0:T(2,128)S(1)} async-done(((f32[16,9,2,128]{3,2,1,0:T(2,128)}), f32[16,9,2,128]{3,2,1,0:T(2,128)S(1)}, u32[]{:S(2)}, u32[]{:S(2)}) %all-to-all-start.6) | async-done | bytes 147488 | tf_op jit(solution)/shard_map/all_to_all | solution.py:327
  74.5 5.7 %all-to-all-start.2 = ((f32[16,9,2,128]{3,2,1,0:T(2,128)}), f32[16,9,2,128]{3,2,1,0:T(2,128)S(1)}, u32[]{:S(2)}, u32[]{:S(2)}) async-start(f32[16,9,2,128]{3,2,1,0:T(2,128)} %bitcast.7), calls=%async_computation.2 | async-start | bytes 294912 | tf_op jit(solution)/shard_map/all_to_all | solution.py:327
  81.2 7.0 %all-to-all-done.2.blocks = f32[16,9,2,128]{3,2,1,0:T(2,128)S(1)} async-done(((f32[16,9,2,128]{3,2,1,0:T(2,128)}), f32[16,9,2,128]{3,2,1,0:T(2,128)S(1)}, u32[]{:S(2)}, u32[]{:S(2)}) %all-to-all-start.2) | async-done | bytes 147488 | tf_op jit(solution)/shard_map/all_to_all | solution.py:327
  88.2 3.5 %all-to-all-start.7 = ((f32[16,9,2,128]{3,2,1,0:T(2,128)}), f32[16,9,2,128]{3,2,1,0:T(2,128)S(1)}, u32[]{:S(2)}, u32[]{:S(2)}) async-start(f32[16,9,2,128]{3,2,1,0:T(2,128)} %shard_map.107), calls=%async_computation.7 | async-start | bytes 294912 | tf_op jit(solution)/shard_map/all_to_all | solution.py:341
  92.7 6.9 %all-to-all-done.7 = f32[16,9,2,128]{3,2,1,0:T(2,128)S(1)} async-done(((f32[16,9,2,128]{3,2,1,0:T(2,128)}), f32[16,9,2,128]{3,2,1,0:T(2,128)S(1)}, u32[]{:S(2)}, u32[]{:S(2)}) %all-to-all-start.7) | async-done | bytes 147488 | tf_op jit(solution)/shard_map/all_to_all | solution.py:341
  99.6 3.5 %all-to-all-start.3 = ((f32[16,9,2,128]{3,2,1,0:T(2,128)}), f32[16,9,2,128]{3,2,1,0:T(2,128)S(1)}, u32[]{:S(2)}, u32[]{:S(2)}) async-start(f32[16,9,2,128]{3,2,1,0:T(2,128)} %shard_map.101), calls=%async_computation.3 | async-start | bytes 294912 | tf_op jit(solution)/shard_map/all_to_all | solution.py:341
  104.1 6.8 %all-to-all-done.3 = f32[16,9,2,128]{3,2,1,0:T(2,128)S(1)} async-done(((f32[16,9,2,128]{3,2,1,0:T(2,128)}), f32[16,9,2,128]{3,2,1,0:T(2,128)S(1)}, u32[]{:S(2)}, u32[]{:S(2)}) %all-to-all-start.3) | async-done | bytes 147488 | tf_op jit(solution)/shard_map/all_to_all | solution.py:341
  (35 shorter events, 10.2 us)
Async XLA Ops:
  0.6 3.2 %copy-start = (f32[2,144,128]{2,1,0:T(8,128)S(1)}, f32[2,144,128]{2,1,0:T(8,128)}, u32[]{:S(2)}) copy-start(f32[2,144,128]{2,1,0:T(8,128)} %refs_3_.7) | copy-start | bytes 442372
  0.6 3.1 %collective-permute-start.2 = (f32[2,144,128]{2,1,0:T(8,128)}, f32[2,144,128]{2,1,0:T(8,128)S(1)}, u32[]{:S(2)}, u32[]{:S(2)}) collective-permute-start(f32[2,144,128]{2,1,0:T(8,128)} %refs_3_.7), channel_id=1, source_target_pairs={{0,1},{1,0},{2,3},{3,2},{4,5},{5,4},{6,7},{7,6},{8,9},{9,8},{10,11... | collective-permute-start | bytes 442376 | tf_op jit(solution)/shard_map/ppermute | solution.py:226
  1.9 1.2 %copy-start.2 = (f32[12,144,128]{2,1,0:T(8,128)S(1)}, f32[12,144,128]{2,1,0:T(8,128)}, u32[]{:S(2)}) copy-start(f32[12,144,128]{2,1,0:T(8,128)} %coupling.1) | copy-start | bytes 2654212
  3.0 0.7 copy-start.7
  3.7 13.1 %copy-start.1 = (f32[2,144,128]{2,1,0:T(8,128)S(1)}, f32[2,144,128]{2,1,0:T(8,128)}, u32[]{:S(2)}) copy-start(f32[2,144,128]{2,1,0:T(8,128)} %refs_3_.5) | copy-start | bytes 442372
  8.7 21.4 %copy-start.3 = (f32[2,144,128]{2,1,0:T(8,128)S(1)}, f32[2,144,128]{2,1,0:T(8,128)}, u32[]{:S(2)}) copy-start(f32[2,144,128]{2,1,0:T(8,128)} %retarded.1) | copy-start | bytes 442372
  8.7 21.4 %copy-start.4 = (s32[64]{0:T(128)S(1)}, s32[64]{0:T(128)}, u32[]{:S(2)}) copy-start(s32[64]{0:T(128)} %shifts.1) | copy-start | bytes 772
  8.7 21.4 %copy-start.5 = (f32[64]{0:T(128)S(1)}, f32[64]{0:T(128)}, u32[]{:S(2)}) copy-start(f32[64]{0:T(128)} %coupled.1) | copy-start | bytes 772
  8.8 21.4 %copy-start.6 = (f32[64]{0:T(128)S(1)}, f32[64]{0:T(128)}, u32[]{:S(2)}) copy-start(f32[64]{0:T(128)} %occupied.1) | copy-start | bytes 772
  8.8 16.3 %all-to-all-start.4 = ((f32[16,9,2,128]{3,2,1,0:T(2,128)}), f32[16,9,2,128]{3,2,1,0:T(2,128)S(1)}, u32[]{:S(2)}, u32[]{:S(2)}) async-start(f32[16,9,2,128]{3,2,1,0:T(2,128)} %bitcast.9), calls=%async_computation.4 | async-start | bytes 294912 | tf_op jit(solution)/shard_map/all_to_all | solution.py:327
  16.8 1.4 %collective-permute-start = (f32[2,144,128]{2,1,0:T(8,128)S(1)}, f32[2,144,128]{2,1,0:T(8,128)S(1)}, u32[]{:S(2)}, u32[]{:S(2)}) collective-permute-start(f32[2,144,128]{2,1,0:T(8,128)S(1)} %copy-done.1), channel_id=1, source_target_pairs={{0,1},{1,0},{2,3},{3,2},{4,5},{5,4},{6,7},{7,6},{8,9},{9,8},{10,11... | collective-permute-start | bytes 442376 | tf_op jit(solution)/shard_map/ppermute | solution.py:226
  25.1 13.0 %all-to-all-start = ((f32[16,9,2,128]{3,2,1,0:T(2,128)}), f32[16,9,2,128]{3,2,1,0:T(2,128)S(1)}, u32[]{:S(2)}, u32[]{:S(2)}) async-start(f32[16,9,2,128]{3,2,1,0:T(2,128)} %bitcast.3), calls=%async_computation | async-start | bytes 294912 | tf_op jit(solution)/shard_map/all_to_all | solution.py:327
  38.0 11.4 %all-to-all-start.5 = ((f32[16,9,2,128]{3,2,1,0:T(2,128)}), f32[16,9,2,128]{3,2,1,0:T(2,128)S(1)}, u32[]{:S(2)}, u32[]{:S(2)}) async-start(f32[16,9,2,128]{3,2,1,0:T(2,128)} %shard_map.104), calls=%async_computation.5 | async-start | bytes 294912 | tf_op jit(solution)/shard_map/all_to_all | solution.py:341
  49.4 11.4 %all-to-all-start.1 = ((f32[16,9,2,128]{3,2,1,0:T(2,128)}), f32[16,9,2,128]{3,2,1,0:T(2,128)S(1)}, u32[]{:S(2)}, u32[]{:S(2)}) async-start(f32[16,9,2,128]{3,2,1,0:T(2,128)} %shard_map.98), calls=%async_computation.1 | async-start | bytes 294912 | tf_op jit(solution)/shard_map/all_to_all | solution.py:341
  53.3 1.4 %collective-permute-start.3 = (f32[2,144,128]{2,1,0:T(8,128)S(1)}, f32[2,144,128]{2,1,0:T(8,128)S(1)}, u32[]{:S(2)}, u32[]{:S(2)}) collective-permute-start(f32[2,144,128]{2,1,0:T(8,128)S(1)} %shard_map.105.refs_0_), channel_id=1, source_target_pairs={{0,1},{1,0},{2,3},{3,2},{4,5},{5,4},{6,7},{7,6},{8,9},{9,8},{10,11... | collective-permute-start | bytes 442376 | tf_op jit(solution)/shard_map/ppermute | solution.py:226
  60.8 13.8 %all-to-all-start.6 = ((f32[16,9,2,128]{3,2,1,0:T(2,128)}), f32[16,9,2,128]{3,2,1,0:T(2,128)S(1)}, u32[]{:S(2)}, u32[]{:S(2)}) async-start(f32[16,9,2,128]{3,2,1,0:T(2,128)} %bitcast.11), calls=%async_computation.6 | async-start | bytes 294912 | tf_op jit(solution)/shard_map/all_to_all | solution.py:327
  67.0 1.4 %collective-permute-start.1 = (f32[2,144,128]{2,1,0:T(8,128)S(1)}, f32[2,144,128]{2,1,0:T(8,128)S(1)}, u32[]{:S(2)}, u32[]{:S(2)}) collective-permute-start(f32[2,144,128]{2,1,0:T(8,128)S(1)} %shard_map.99.refs_0_), channel_id=1, source_target_pairs={{0,1},{1,0},{2,3},{3,2},{4,5},{5,4},{6,7},{7,6},{8,9},{9,8},{10,11... | collective-permute-start | bytes 442376 | tf_op jit(solution)/shard_map/ppermute | solution.py:226
  74.5 13.7 %all-to-all-start.2 = ((f32[16,9,2,128]{3,2,1,0:T(2,128)}), f32[16,9,2,128]{3,2,1,0:T(2,128)S(1)}, u32[]{:S(2)}, u32[]{:S(2)}) async-start(f32[16,9,2,128]{3,2,1,0:T(2,128)} %bitcast.7), calls=%async_computation.2 | async-start | bytes 294912 | tf_op jit(solution)/shard_map/all_to_all | solution.py:327
  88.2 11.4 %all-to-all-start.7 = ((f32[16,9,2,128]{3,2,1,0:T(2,128)}), f32[16,9,2,128]{3,2,1,0:T(2,128)S(1)}, u32[]{:S(2)}, u32[]{:S(2)}) async-start(f32[16,9,2,128]{3,2,1,0:T(2,128)} %shard_map.107), calls=%async_computation.7 | async-start | bytes 294912 | tf_op jit(solution)/shard_map/all_to_all | solution.py:341
  99.6 11.4 %all-to-all-start.3 = ((f32[16,9,2,128]{3,2,1,0:T(2,128)}), f32[16,9,2,128]{3,2,1,0:T(2,128)S(1)}, u32[]{:S(2)}, u32[]{:S(2)}) async-start(f32[16,9,2,128]{3,2,1,0:T(2,128)} %shard_map.101), calls=%async_computation.3 | async-start | bytes 294912 | tf_op jit(solution)/shard_map/all_to_all | solution.py:341
where the time goes:
time: 113 us; the launch traced here: 112 us
  waiting for transfers between devices  41 us (36%)
  starting transfers between devices  39.6 us (35%)
  Pallas kernels  28.1 us (25%)
  local copies, waits for them, and re-layouts  1.6 us (1%)
    pallas_call x14, Pallas kernels, call(): pl.pallas_call(kernel, out_shape=shapes, in_specs=spaces or [vmem] * len(...  28.1 us
    all_to_all x4, starting transfers between devices, body(): lax.all_to_all(x.reshape(parts, share, rows, atoms), 'energy', 0, 0)  24.6 us
    all_to_all x4, waiting for transfers between devices, body(): lax.all_to_all(x, 'energy', 0, 0).reshape(parts * share, rows, atoms)  21.6 us
    all_to_all x4, waiting for transfers between devices, body(): lax.all_to_all(x.reshape(parts, share, rows, atoms), 'energy', 0, 0)  15.6 us
    all_to_all x4, starting transfers between devices, body(): lax.all_to_all(x, 'energy', 0, 0).reshape(parts * share, rows, atoms)  14.1 us
    ppermute x4, waiting for transfers between devices, beside(): return lax.ppermute(block, 'slab', [(0, 1), (1, 0)])  3.88 us
  transfers between devices with their start and end apart: 12, of which 11 were waited for; matrix products, arithmetic and copies ran while one was open for 1% of the time, Pallas kernels for 20%

commit v1 on v0

--- a/solution.py
+++ b/solution.py
@@ -12,7 +12,7 @@
 HW = 32
 ITERS = 2
 ROWS = 8
-FUSED = 1
+FUSED = 2
 
 TOP_RANK = lax.Precision.HIGHEST
 PARAMS = pltpu.CompilerParams(vmem_limit_bytes=24 * 1024 * 1024)

time: 113 us -> 93.8 us (0.83)
  blocking collectives: 0 us -> 41.3 us
  waiting for transfers between devices: 41 us -> 7.51 us
  starting transfers between devices: 39.6 us -> 9.5 us
  local copies, waits for them, and re-layouts: 1.6 us -> 11.3 us
  Pallas kernels: 28.1 us -> 21.8 us
    all_to_all x0 -> x3, blocking collectives: none -> 41.3 us  [the longest x2 27 us: body(): lax.all_to_all(x, 'energy', 0, 0).reshape(parts * share, rows, atoms)]
    all_to_all x4 -> x0, waiting for transfers between devices: 21.6 us -> none  [body(): lax.all_to_all(x, 'energy', 0, 0).reshape(parts * share, rows, atoms)]
    all_to_all x4 -> x1, starting transfers between devices: 24.6 us -> 8.33 us  [body(): lax.all_to_all(x.reshape(parts, share, rows, atoms), 'energy', 0, 0)]
    all_to_all x4 -> x0, starting transfers between devices: 14.1 us -> none  [body(): lax.all_to_all(x, 'energy', 0, 0).reshape(parts * share, rows, atoms)]
    unnamed x16 -> x48, local copies, waits for them, and re-layouts: 1.58 us -> 11.3 us
    all_to_all x4 -> x1, waiting for transfers between devices: 15.6 us -> 6.44 us  [body(): lax.all_to_all(x.reshape(parts, share, rows, atoms), 'energy', 0, 0)]
    pallas_call x14 -> x8, Pallas kernels: 28.1 us -> 21.8 us  [call(): pl.pallas_call(kernel, out_shape=shapes, in_specs=spaces or [vmem] * len(...]
    ppermute x4, waiting for transfers between devices: 3.88 us -> 1.08 us  [beside(): return lax.ppermute(block, 'slab', [(0, 1), (1, 0)])]
  transfers between devices with their start and end apart: 12 -> 5, of which waited for: 11 -> 3; matrix products, arithmetic and copies ran while one was open for 1% -> 1% of each run, Pallas kernels for 20% -> 2%
where the time goes in v1:
time: 93.8 us; the launch traced here: 93 us
  blocking collectives  41.3 us (44%)
  Pallas kernels  21.8 us (23%)
  local copies, waits for them, and re-layouts  11.3 us (12%)
  starting transfers between devices  9.5 us (10%)
  waiting for transfers between devices  7.51 us (8%)
    all_to_all x2, blocking collectives, body(): lax.all_to_all(x, 'energy', 0, 0).reshape(parts * share, rows, atoms)  27 us
    pallas_call x8, Pallas kernels, call(): pl.pallas_call(kernel, out_shape=shapes, in_specs=spaces or [vmem] * len(...  21.8 us
    all_to_all x1, blocking collectives, body(): lax.all_to_all(x.reshape(parts, share, rows, atoms), 'energy', 0, 0)  14.4 us
    unnamed x48, local copies, waits for them, and re-layouts  11.3 us
    all_to_all x1, starting transfers between devices, body(): lax.all_to_all(x.reshape(parts, share, rows, atoms), 'energy', 0, 0)  8.33 us
    all_to_all x1, waiting for transfers between devices, body(): lax.all_to_all(x.reshape(parts, share, rows, atoms), 'energy', 0, 0)  6.44 us
  transfers between devices with their start and end apart: 5, of which 3 were waited for; matrix products, arithmetic and copies ran while one was open for 1% of the time, Pallas kernels for 2%

profile of v1, /device:TPU:0, one launch (start us, length us, event | category | flops | bytes accessed | tf_op | source)
XLA Modules:
  0.0 93.0 jit_solution(17948137765862265853)
XLA Ops:
  1.2 0.7 and_convert_fusion
  2.0 1.2 %copy-done.11 = f32[12,144,128]{2,1,0:T(8,128)S(1)} copy-done((f32[12,144,128]{2,1,0:T(8,128)S(1)}, f32[12,144,128]{2,1,0:T(8,128)}, u32[]{:S(2)}) %copy-start.11) | copy-done | bytes 884760
  4.0 8.5 %shard_map.97 = f32[144,4,128]{2,1,0:T(4,128)S(1)} custom-call(f32[2,144,128]{2,1,0:T(8,128)S(1)} %copy-done.3, f32[2,144,128]{2,1,0:T(8,128)S(1)} %copy-done.5, f32[2,144,128]{2,1,0:T(8,128)} %collective-permute-done.refs_2_, f32[2,144,128]{2,1,0:T(8,128)} %collective-permute-done.1.refs_3_, s32[6,8,128]{2,1,0:T(8,128)S(1)} %bitcast.19, ...), custom_call_target="tpu_custom_call" | custom-call | flops 42467328 | bytes 4472832 | tf_op jit(solution)/shard_map/pallas_call | solution.py:210
  12.5 0.7 copy-done.7
  13.2 8.3 %all-to-all-start = ((f32[16,9,4,128]{3,2,1,0:T(4,128)}), f32[16,9,4,128]{3,2,1,0:T(4,128)}, u32[]{:S(2)}, u32[]{:S(2)}) async-start(f32[16,9,4,128]{3,2,1,0:T(4,128)} %bitcast.13), calls=%async_computation | async-start | bytes 589824 | tf_op jit(solution)/shard_map/all_to_all | solution.py:327
  21.6 0.9 copy-done.16
  22.5 1.4 %shard_map.95 = (f32[576,128]{1,0:T(8,128)S(1)}, f32[1152,128]{1,0:T(8,128)S(1)}, f32[2,32,32]{2,1,0:T(8,128)S(1)}) custom-call(f32[2,144,128]{2,1,0:T(8,128)S(1)} %copy-done.16, s32[64]{0:T(128)S(1)} %copy-done.20, f32[64]{0:T(128)S(1)} %copy-done.21, f32[64]{0:T(128)S(1)} %copy-done.22), custom_call_target="tpu_custom_call" | custom-call | flops 294912 | bytes 1041152 | tf_op jit(solution)/shard_map/pallas_call | solution.py:210
  23.9 0.8 copy-done
  24.8 0.7 copy-done.8
  26.1 6.4 %all-to-all-done.blocks = f32[16,9,4,128]{3,2,1,0:T(4,128)} async-done(((f32[16,9,4,128]{3,2,1,0:T(4,128)}), f32[16,9,4,128]{3,2,1,0:T(4,128)}, u32[]{:S(2)}, u32[]{:S(2)}) %all-to-all-start) | async-done | bytes 294944 | tf_op jit(solution)/shard_map/all_to_all | solution.py:327
  32.5 0.8 copy-done.18
  33.3 1.5 %shard_map.98 = f32[16,9,4,128]{3,2,1,0:T(4,128)S(1)} custom-call(f32[2,32,32]{2,1,0:T(8,128)S(1)} %copy-done.18, f32[16,9,4,128]{3,2,1,0:T(4,128)} %all-to-all-done.blocks), custom_call_target="tpu_custom_call" | custom-call | flops 4718592 | bytes 598016 | tf_op jit(solution)/shard_map/pallas_call | solution.py:210
  34.8 13.5 %all_to_all.20 = f32[16,9,4,128]{3,2,1,0:T(4,128)S(1)} all-to-all(f32[16,9,4,128]{3,2,1,0:T(4,128)S(1)} %shard_map.98), channel_id=1, replica_groups=mesh['energy'=16,'slab'=2] {'energy'}, dimensions={0} | all-to-all | bytes 589824 | tf_op jit(solution)/shard_map/all_to_all | solution.py:341
  48.2 1.1 %copy-done.1 = f32[1152,128]{1,0:T(8,128)S(1)} copy-done((f32[1152,128]{1,0:T(8,128)S(1)}, f32[1152,128]{1,0:T(8,128)}, u32[]{:S(2)}) %copy-start.1) | copy-done | bytes 589848
  49.3 0.9 copy-done.4
  50.2 0.9 copy-done.6
  51.1 1.0 %copy-done.9 = f32[576,128]{1,0:T(8,128)S(1)} copy-done((f32[576,128]{1,0:T(8,128)S(1)}, f32[576,128]{1,0:T(8,128)}, u32[]{:S(2)}) %copy-start.9) | copy-done | bytes 294936
  53.2 0.9 collective-permute-done.2.refs_2_
  54.3 0.7 copy-done.13
  55.1 0.7 copy-done.15
  55.8 7.5 %shard_map.100 = f32[144,4,128]{2,1,0:T(4,128)S(1)} custom-call(f32[2,144,128]{2,1,0:T(8,128)S(1)} %get-tuple-element.10.refs_0_, f32[2,144,128]{2,1,0:T(8,128)S(1)} %get-tuple-element.11.refs_1_, f32[2,144,128]{2,1,0:T(8,128)S(1)} %collective-permute-done.2.refs_2_, f32[2,144,128]{2,1,0:T(8,128)S(1)} %collective-permute-done.3.refs_3_, ...), custom_call_target="tpu_custom_call" | custom-call | flops 42467328 | bytes 4472832 | tf_op jit(solution)/shard_map/pallas_call | solution.py:210
  63.3 14.4 %all_to_all.21.blocks = f32[16,9,4,128]{3,2,1,0:T(4,128)S(1)} all-to-all(f32[16,9,4,128]{3,2,1,0:T(4,128)S(1)} %bitcast.14), channel_id=1, replica_groups=mesh['energy'=16,'slab'=2] {'energy'}, dimensions={0} | all-to-all | bytes 589824 | tf_op jit(solution)/shard_map/all_to_all | solution.py:327
  78.2 13.5 %all_to_all.22 = f32[16,9,4,128]{3,2,1,0:T(4,128)S(1)} all-to-all(f32[16,9,4,128]{3,2,1,0:T(4,128)S(1)} %shard_map.101), channel_id=1, replica_groups=mesh['energy'=16,'slab'=2] {'energy'}, dimensions={0} | all-to-all | bytes 589824 | tf_op jit(solution)/shard_map/all_to_all | solution.py:341
  91.7 1.3 %shard_map.102 = (f32[2,144,128]{2,1,0:T(8,128)}, f32[2,144,128]{2,1,0:T(8,128)}) custom-call(f32[144,4,128]{2,1,0:T(4,128)S(1)} %bitcast.15, f32[72,8,128]{2,1,0:T(8,128)S(1)} %bitcast.18, f32[144,8,128]{2,1,0:T(8,128)S(1)} %bitcast.12, f32[2,144,128]{2,1,0:T(8,128)S(1)} %copy-done.4, f32[2,144,128]{2,1,0:T(8,128)S(1)} %copy-done.6), custom_call_target="tpu_custom_call" | custom-call | flops 3538944 | bytes 1769472 | tf_op jit(solution)/shard_map/pallas_call | solution.py:210
  (49 shorter events, 3.9 us)
Async XLA Ops:
  0.6 3.2 %collective-permute-start = (f32[2,144,128]{2,1,0:T(8,128)}, f32[2,144,128]{2,1,0:T(8,128)}, u32[]{:S(2)}, u32[]{:S(2)}) collective-permute-start(f32[2,144,128]{2,1,0:T(8,128)} %refs_3_.3), channel_id=1, source_target_pairs={{0,1},{1,0},{2,3},{3,2},{4,5},{5,4},{6,7},{7,6},{8,9},{9,8},{10,11... | collective-permute-start | bytes 442376 | tf_op jit(solution)/shard_map/ppermute | solution.py:226
  1.1 2.7 %collective-permute-start.1 = (f32[2,144,128]{2,1,0:T(8,128)}, f32[2,144,128]{2,1,0:T(8,128)}, u32[]{:S(2)}, u32[]{:S(2)}) collective-permute-start(f32[2,144,128]{2,1,0:T(8,128)} %refs_4_.3), channel_id=1, source_target_pairs={{0,1},{1,0},{2,3},{3,2},{4,5},{5,4},{6,7},{7,6},{8,9},{9,8},{10,11... | collective-permute-start | bytes 442376 | tf_op jit(solution)/shard_map/ppermute | solution.py:226
  1.2 2.7 %copy-start.3 = (f32[2,144,128]{2,1,0:T(8,128)S(1)}, f32[2,144,128]{2,1,0:T(8,128)}, u32[]{:S(2)}) copy-start(f32[2,144,128]{2,1,0:T(8,128)} %refs_3_.3) | copy-start | bytes 442372
  1.2 2.7 %copy-start.5 = (f32[2,144,128]{2,1,0:T(8,128)S(1)}, f32[2,144,128]{2,1,0:T(8,128)}, u32[]{:S(2)}) copy-start(f32[2,144,128]{2,1,0:T(8,128)} %refs_4_.3) | copy-start | bytes 442372
  2.0 1.2 %copy-start.11 = (f32[12,144,128]{2,1,0:T(8,128)S(1)}, f32[12,144,128]{2,1,0:T(8,128)}, u32[]{:S(2)}) copy-start(f32[12,144,128]{2,1,0:T(8,128)} %coupling.1) | copy-start | bytes 2654212
  3.8 17.7 %copy-start.20 = (s32[64]{0:T(128)S(1)}, s32[64]{0:T(128)}, u32[]{:S(2)}) copy-start(s32[64]{0:T(128)} %shifts.1) | copy-start | bytes 772
  3.9 17.7 %copy-start.21 = (f32[64]{0:T(128)S(1)}, f32[64]{0:T(128)}, u32[]{:S(2)}) copy-start(f32[64]{0:T(128)} %coupled.1) | copy-start | bytes 772
  3.9 17.7 %copy-start.22 = (f32[64]{0:T(128)S(1)}, f32[64]{0:T(128)}, u32[]{:S(2)}) copy-start(f32[64]{0:T(128)} %occupied.1) | copy-start | bytes 772
  3.9 8.6 %copy-start.12 = (s32[12,4,128]{2,1,0:T(4,128)}, s32[12,4,128]{2,1,0:T(4,128)S(1)}, u32[]{:S(2)}) copy-start(s32[12,4,128]{2,1,0:T(4,128)S(1)} %broadcast_in_dim.4) | copy-start | bytes 73732
  3.9 8.5 %copy-start.14 = (s32[12,4,128]{2,1,0:T(4,128)}, s32[12,4,128]{2,1,0:T(4,128)S(1)}, u32[]{:S(2)}) copy-start(s32[12,4,128]{2,1,0:T(4,128)S(1)} %broadcast_in_dim.5) | copy-start | bytes 73732
  13.2 19.3 %all-to-all-start = ((f32[16,9,4,128]{3,2,1,0:T(4,128)}), f32[16,9,4,128]{3,2,1,0:T(4,128)}, u32[]{:S(2)}, u32[]{:S(2)}) async-start(f32[16,9,4,128]{3,2,1,0:T(4,128)} %bitcast.13), calls=%async_computation | async-start | bytes 589824 | tf_op jit(solution)/shard_map/all_to_all | solution.py:327
  21.6 0.9 copy-start.16
  23.9 0.8 copy-start
  32.5 0.8 copy-start.18
  34.8 42.9 %copy-start.19 = (f32[2,32,32]{2,1,0:T(8,128)S(1)}, f32[2,32,32]{2,1,0:T(8,128)}, u32[]{:S(2)}) copy-start(f32[2,32,32]{2,1,0:T(8,128)} %copy-done.17) | copy-start | bytes 24580
  48.2 1.1 %copy-start.1 = (f32[1152,128]{1,0:T(8,128)S(1)}, f32[1152,128]{1,0:T(8,128)}, u32[]{:S(2)}) copy-start(f32[1152,128]{1,0:T(8,128)} %copy-done) | copy-start | bytes 1769476
  49.3 0.9 copy-start.4
  50.2 0.9 copy-start.6
  51.1 1.0 %copy-start.9 = (f32[576,128]{1,0:T(8,128)S(1)}, f32[576,128]{1,0:T(8,128)}, u32[]{:S(2)}) copy-start(f32[576,128]{1,0:T(8,128)} %copy-done.8) | copy-start | bytes 884740
  52.1 39.6 %copy-start.2 = (f32[1152,128]{1,0:T(8,128)S(1)}, f32[1152,128]{1,0:T(8,128)}, u32[]{:S(2)}) copy-start(f32[1152,128]{1,0:T(8,128)} %copy-done) | copy-start | bytes 1769476
  52.1 39.6 %copy-start.10 = (f32[576,128]{1,0:T(8,128)S(1)}, f32[576,128]{1,0:T(8,128)}, u32[]{:S(2)}) copy-start(f32[576,128]{1,0:T(8,128)} %copy-done.8) | copy-start | bytes 884740
  52.7 1.4 %collective-permute-start.2 = (f32[2,144,128]{2,1,0:T(8,128)S(1)}, f32[2,144,128]{2,1,0:T(8,128)S(1)}, u32[]{:S(2)}, u32[]{:S(2)}) collective-permute-start(f32[2,144,128]{2,1,0:T(8,128)S(1)} %get-tuple-element.10.refs_0_), channel_id=1, source_target_pairs={{0,1},{1,0},{2,3},{3,2},{4,5},{5,4},{6,7},{7,6},{8,9},{9,8},{10,11... | collective-permute-start | bytes 442376 | tf_op jit(solution)/shard_map/ppermute | solution.py:226
  52.7 1.6 %collective-permute-start.3 = (f32[2,144,128]{2,1,0:T(8,128)S(1)}, f32[2,144,128]{2,1,0:T(8,128)S(1)}, u32[]{:S(2)}, u32[]{:S(2)}) collective-permute-start(f32[2,144,128]{2,1,0:T(8,128)S(1)} %get-tuple-element.11.refs_1_), channel_id=1, source_target_pairs={{0,1},{1,0},{2,3},{3,2},{4,5},{5,4},{6,7},{7,6},{8,9},{9,8},{10,11... | collective-permute-start | bytes 442376 | tf_op jit(solution)/shard_map/ppermute | solution.py:226
  54.3 0.7 copy-start.13
  (5 other events, 3.5 us)

commit v2 on v1

--- a/solution.py
+++ b/solution.py
@@ -28,11 +28,21 @@
         target[rows, :] = source(first + at, size)
 
 
-def prep_coupling_kernel(rows, coupling, inside, out):
+def prep_coupling_kernel(rows, coupling, offsets, out, lanes, is_near):
     group = ROWS // rows
-    pairs = coupling.shape[1]
+    _, pairs, atoms = coupling.shape
+    slab, slabs = lax.axis_index("slab"), lax.axis_size("slab")
+    targets = offsets[...] + lax.broadcasted_iota(jnp.int32, (NB, atoms), 1)
+    placed = targets + slab * atoms
+    inside = ((placed >= 0) & (placed < slabs * atoms)).astype(jnp.float32)
+    near = ((targets >= 0) & (targets < atoms)).astype(jnp.int32)
+    lane = jnp.where(targets < 0, targets + atoms, targets)
+    lane = jnp.where(lane >= atoms, lane - atoms, lane)
     for n in range(NB):
         valid = inside[n : n + 1, :]
+        some = slice(n % group * rows, (n % group + 1) * rows)
+        lanes[n // group, some, :] = jnp.broadcast_to(lane[n : n + 1, :], (rows, atoms))
+        is_near[n // group, some, :] = jnp.broadcast_to(near[n : n + 1, :], (rows, atoms))
         for row in range(rows):
             spread_rows(
                 out,
@@ -44,16 +54,47 @@
             )
 
 
+def partner(device, slot, parts):
+    if parts & (parts - 1) == 0:
+        return device ^ slot
+    return (device + slot) % parts
+
+
+def origin(device, slot, parts):
+    if parts & (parts - 1) == 0:
+        return device ^ slot
+    return (device + parts - slot) % parts
+
+
+def exchanged(shares):
+    parts = len(shares)
+    received = [shares[0]]
+    for slot in range(1, parts):
+        route = [(i, partner(i, slot, parts)) for i in range(parts)]
+        received.append(lax.ppermute(shares[slot], "energy", route))
+    return received
+
+
 def prep_dressing_kernel(rows, retarded, shifts, coupled, occupied, left, right, mixing):
     energies, pairs, _ = retarded.shape
     total = mixing.shape[1]
+    parts = total // energies
+    device = lax.axis_index("energy")
     share = pairs * rows // ROWS
     for row in range(ROWS):
         read = lambda at, size: retarded[row % energies, at : at + size, :]
         spread_rows(left, 0, row, read, row // rows * share, share)
         spread_rows(right, 0, row, read, 0, pairs)
-    places = lax.broadcasted_iota(jnp.int32, (total, total), 0)
-    gap = lax.broadcasted_iota(jnp.int32, (total, total), 1) - places
+    row_at = lax.broadcasted_iota(jnp.int32, (total, total), 0)
+    column_at = lax.broadcasted_iota(jnp.int32, (total, total), 1)
+    sent = jnp.zeros((total, total), jnp.int32)
+    came = jnp.zeros((total, total), jnp.int32)
+    for slot in range(parts):
+        first = slot * energies
+        for at in range(energies):
+            sent = jnp.where(row_at == first + at, partner(device, slot, parts) * energies + at, sent)
+            came = jnp.where(column_at == first + at, origin(device, slot, parts) * energies + at, came)
+    gap = came - sent
 
     def add_mode(mode, kernels):
         lesser, greater = kernels
@@ -74,17 +115,13 @@
 
 def couple_kernel(fused, *refs):
     near, far = refs[:fused], refs[fused : 2 * fused]
-    lanes, is_near, links_hbm, out = refs[2 * fused : 2 * fused + 4]
-    own, other, gathered_a, gathered_b, total, links, sems = refs[2 * fused + 4 :]
+    lanes, is_near, links = refs[2 * fused : 2 * fused + 3]
+    outs = refs[2 * fused + 3 : -6]
+    own, other, gathered_a, gathered_b, total, staged = refs[-6:]
     energies, pairs, atoms = near[0].shape
     rows = fused * energies
     group = ROWS // rows
     groups = NB // group
-    copies = [
-        pltpu.make_async_copy(links_hbm.at[g], links.at[g], sems.at[g]) for g in range(groups)
-    ]
-    for copy in copies:
-        copy.start()
     for row in range(ROWS):
         function, energy = row % rows // energies, row % energies
         for target, sources in ((own, near), (other, far)):
@@ -104,12 +141,11 @@
             outer = jnp.take_along_axis(other[rows_at, :], lane, axis=1, mode="promise_in_bounds")
             target[pair] = jnp.where(mine, inner, outer)
 
-    blocked = 2
+    blocked = 3
     steps = NORB // blocked
     chunk = pairs // steps
     lax.fori_loop(0, steps, lambda step, _: gather(0, step * chunk, chunk), None)
     for g in range(groups):
-        copies[g].wait()
         source = buffers[g % 2]
 
         def block_row(step, _):
@@ -139,47 +175,58 @@
                         while width >= rows:
                             value = value + pltpu.roll(value, width, 0)
                             width //= 2
-                        out[at] = value[:rows]
+                        staged[at] = value[:rows]
             if g < groups - 1:
                 gather(g + 1, step * chunk, chunk)
 
         lax.fori_loop(0, steps, block_row, None)
-    for at in range(pairs, out.shape[0]):
-        out[at] = jnp.zeros((rows, atoms), jnp.float32)
-
-
-def mix_kernel(fused, mixing, blocks, out, before, after):
-    parts, share, rows, atoms = blocks.shape
+    for at in range(pairs, staged.shape[0]):
+        staged[at] = jnp.zeros((rows, atoms), jnp.float32)
+    device = lax.axis_index("energy")
+    share = outs[0].shape[0]
+    for slot, out in enumerate(outs):
+        first = partner(device, slot, len(outs)) * share
+        for at in range(share):
+            out[at] = staged[first + at]
+
+
+def mix_kernel(fused, parts, mixing, *refs):
+    blocks, outs = refs[:parts], refs[parts : 2 * parts]
+    before, after = refs[2 * parts :]
+    share, rows, atoms = blocks[0].shape
     energies = rows // fused
     for f in range(fused):
         some = slice(f * energies, (f + 1) * energies)
-        for part in range(parts):
+        for slot in range(parts):
+            held = slice(slot * energies, (slot + 1) * energies)
             for pair in range(share):
-                before[part * energies : (part + 1) * energies, pair * atoms : (pair + 1) * atoms] = (
-                    blocks[part, pair, some, :]
-                )
-        after[...] = jnp.dot(
-            mixing[f], before[...], precision=TOP_RANK, preferred_element_type=jnp.float32
+                before[f, held, pair * atoms : (pair + 1) * atoms] = blocks[slot][pair, some, :]
+        after[f] = jnp.dot(
+            mixing[f], before[f], precision=TOP_RANK, preferred_element_type=jnp.float32
         )
-        for part in range(parts):
+        for slot in range(parts):
+            held = slice(slot * energies, (slot + 1) * energies)
             for pair in range(share):
-                out[part, pair, some, :] = after[
-                    part * energies : (part + 1) * energies, pair * atoms : (pair + 1) * atoms
-                ]
-
-
-def dress_kernel(fused, *refs):
-    sigma, left, right = refs[:3]
-    free, out = refs[3 : 3 + fused], refs[3 + fused : 3 + 2 * fused]
-    copied, dressed = refs[3 + 2 * fused :]
+                outs[slot][pair, some, :] = after[f, held, pair * atoms : (pair + 1) * atoms]
+
+
+def dress_kernel(fused, slots, *refs):
+    sigma, refs = refs[:slots], refs[slots:]
+    left, right = refs[:2]
+    free, out = refs[2 : 2 + fused], refs[2 + fused : 2 + 2 * fused]
+    copied, dressed = refs[2 + 2 * fused :]
     energies, pairs, atoms = free[0].shape
     rows = fused * energies
     parts = ROWS // rows
     share = pairs // parts
-    for pair in range(pairs):
-        value = sigma[pair]
-        for part in range(parts):
-            copied[pair, part * rows : (part + 1) * rows, :] = value
+    device = lax.axis_index("energy")
+    width = sigma[0].shape[0]
+    for slot in range(slots):
+        first = origin(device, slot, slots) * width
+        for at in range(width):
+            value = sigma[slot][at]
+            for part in range(parts):
+                copied[first + at, part * rows : (part + 1) * rows, :] = value
     for i in range(NORB // parts):
         inner = [None] * NORB
         for j in range(NORB):
@@ -204,7 +251,10 @@
 
 
 def call(kernel, outs, scratch, flops, *operands, spaces=None):
-    shapes = [jax.ShapeDtypeStruct(dims, jnp.float32) for dims in outs]
+    shapes = [
+        x if isinstance(x, jax.ShapeDtypeStruct) else jax.ShapeDtypeStruct(x, jnp.float32)
+        for x in outs
+    ]
     vmem = pl.BlockSpec(memory_space=pltpu.VMEM)
     moved = sum(x.size for x in operands) + sum(x.size for x in shapes)
     return pl.pallas_call(
@@ -254,30 +304,20 @@
     total = energies * parts
     vmem = pl.BlockSpec(memory_space=pltpu.VMEM)
     smem = pl.BlockSpec(memory_space=pltpu.SMEM)
-    away = pl.BlockSpec(memory_space=pl.ANY)
-
-    targets = neighbour_offsets + jnp.arange(atoms, dtype=jnp.int32)[None, :]
-    placed = targets + lax.axis_index("slab") * atoms
-    inside = (placed >= 0) & (placed < lax.axis_size("slab") * atoms)
-
-    def widened(values):
-        return jnp.broadcast_to(values[:, None, :], (NB, rows, atoms)).reshape(groups, ROWS, atoms)
-
-    lanes = widened(jnp.remainder(targets, atoms))
-    is_near = widened(((targets >= 0) & (targets < atoms)).astype(jnp.int32))
+    indices = jax.ShapeDtypeStruct((groups, ROWS, atoms), jnp.int32)
 
     free = (lesser_free, greater_free)
     chains = [free[at : at + fused] for at in range(0, 2, fused)]
     greens = list(chains)
     halos = [tuple(beside(g) for g in chain) for chain in greens]
 
-    (links,) = call(
+    links, lanes, is_near = call(
         functools.partial(prep_coupling_kernel, rows),
-        [(groups * pairs * ROWS, atoms)],
+        [(groups * pairs * ROWS, atoms), indices, indices],
         [],
         coupling.size * rows,
         coupling,
-        inside.astype(jnp.float32),
+        neighbour_offsets,
     )
     links = links.reshape(groups, pairs, ROWS, atoms)
     left, right, mixing = call(
@@ -296,57 +336,49 @@
 
     wide = pltpu.VMEM((pairs * ROWS, atoms), jnp.float32)
     deep = pltpu.VMEM((pairs, ROWS, atoms), jnp.float32)
-    flat = pltpu.VMEM((total, share * atoms), jnp.float32)
+    flat = pltpu.VMEM((fused, total, share * atoms), jnp.float32)
+    staged = pltpu.VMEM((parts * share, rows, atoms), jnp.float32)
+    shares = [(share, rows, atoms)] * parts
     work = 4 * NORB * rows * pairs * atoms
 
     for step in range(ITERS):
         coupled = [
             call(
                 functools.partial(couple_kernel, fused),
-                [(parts * share, rows, atoms)],
-                [
-                    wide,
-                    wide,
-                    deep,
-                    deep,
-                    deep,
-                    pltpu.VMEM(links.shape, jnp.float32),
-                    pltpu.SemaphoreType.DMA((groups,)),
-                ],
+                shares,
+                [wide, wide, deep, deep, deep, staged],
                 NB * work,
                 *green,
                 *halo,
                 lanes,
                 is_near,
                 links,
-                spaces=[vmem] * (2 * fused + 2) + [away],
-            )[0]
+            )
             for green, halo in zip(greens, halos)
         ]
-        gathered = [
-            lax.all_to_all(x.reshape(parts, share, rows, atoms), "energy", 0, 0) for x in coupled
-        ]
+        gathered = [exchanged(x) for x in coupled]
         mixed = [
             call(
-                functools.partial(mix_kernel, fused),
-                [x.shape],
+                functools.partial(mix_kernel, fused, parts),
+                shares,
                 [flat, flat],
-                2 * total * x.size,
+                2 * total * rows * share * parts * atoms,
                 mixing[at * fused : (at + 1) * fused],
-                x,
-            )[0]
+                *x,
+            )
             for at, x in enumerate(gathered)
         ]
-        sigma = [
-            lax.all_to_all(x, "energy", 0, 0).reshape(parts * share, rows, atoms) for x in mixed
-        ]
+        sigma = [exchanged(x) for x in mixed]
         greens = [
             call(
-                functools.partial(dress_kernel, fused),
+                functools.partial(dress_kernel, fused, parts),
                 [lesser_free.shape] * fused,
-                [deep, pltpu.VMEM((pairs * rows, atoms), jnp.float32)],
+                [
+                    pltpu.VMEM((parts * share, ROWS, atoms), jnp.float32),
+                    pltpu.VMEM((pairs * rows, atoms), jnp.float32),
+                ],
                 work,
-                x,
+                *x,
                 left,
                 right,
                 *chain,

time: 93.8 us -> 151 us (1.61)
  starting transfers between devices: 9.5 us -> 108 us
  blocking collectives: 41.3 us -> 0 us
  waiting for transfers between devices: 7.51 us -> 18.3 us
  local copies, waits for them, and re-layouts: 11.3 us -> 3.71 us
  Pallas kernels: 21.8 us -> 19.9 us
    ppermute x0 -> x60, starting transfers between devices: none -> 107 us  [exchanged(): received.append(lax.ppermute(shares[slot], 'energy', route))]
    all_to_all x3 -> x0, blocking collectives: 41.3 us -> none  [the longest x2 27 us: body(): lax.all_to_all(x, 'energy', 0, 0).reshape(parts * share, rows, atoms)]
    ppermute x0 -> x60, waiting for transfers between devices: none -> 17.3 us  [exchanged(): received.append(lax.ppermute(shares[slot], 'energy', route))]
    all_to_all x1 -> x0, starting transfers between devices: 8.33 us -> none  [body(): lax.all_to_all(x.reshape(parts, share, rows, atoms), 'energy', 0, 0)]
    unnamed x48 -> x20, local copies, waits for them, and re-layouts: 11.3 us -> 3.71 us
    all_to_all x1 -> x0, waiting for transfers between devices: 6.44 us -> none  [body(): lax.all_to_all(x.reshape(parts, share, rows, atoms), 'energy', 0, 0)]
    pallas_call x8, Pallas kernels: 21.8 us -> 19.9 us  [call(): pl.pallas_call(kernel, out_shape=shapes, in_specs=spaces or [vmem] * len(...]
  transfers between devices with their start and end apart: 5 -> 64, of which waited for: 3 -> 11; matrix products, arithmetic and copies ran while one was open for 1% -> 0% of each run, Pallas kernels for 2% -> 1%
where the time goes in v2:
time: 151 us
  starting transfers between devices  108 us (72%)
  Pallas kernels  19.9 us (13%)
  waiting for transfers between devices  18.3 us (12%)
  local copies, waits for them, and re-layouts  3.71 us (2%)
    ppermute x60, starting transfers between devices, exchanged(): received.append(lax.ppermute(shares[slot], 'energy', route))  107 us
    pallas_call x8, Pallas kernels, call(): pl.pallas_call(kernel, out_shape=shapes, in_specs=spaces or [vmem] * len(...  19.9 us
    ppermute x60, waiting for transfers between devices, exchanged(): received.append(lax.ppermute(shares[slot], 'energy', route))  17.3 us
    unnamed x20, local copies, waits for them, and re-layouts  3.71 us
  transfers between devices with their start and end apart: 64, of which 11 were waited for; matrix products, arithmetic and copies ran while one was open for 0% of the time, Pallas kernels for 1%

profile of v2, /device:TPU:0, one launch (start us, length us, event | category | flops | bytes accessed | tf_op | source)
XLA Modules:
  0.0 151.2 jit_solution(16083973662621878301)
XLA Ops:
  5.5 7.6 %shard_map.97 = (f32[9,4,128]{2,1,0:T(4,128)S(1)}, f32[9,4,128]{2,1,0:T(4,128)S(1)}, f32[9,4,128]{2,1,0:T(4,128)S(1)}, f32[9,4,128]{2,1,0:T(4,128)S(1)}, f32[9,4...) custom-call(f32[2,144,128]{2,1,0:T(8,128)S(1)} %copy-done, ...), custom_call_target="tpu_custom_call" | custom-call | flops 42467328 | bytes 4472832 | tf_op jit(solution)/shard_map/pallas_call | solution.py:260
  13.1 3.0 %collective-permute-start.2 = (f32[9,4,128]{2,1,0:T(4,128)S(1)}, f32[9,4,128]{2,1,0:T(4,128)S(1)}, u32[]{:S(2)}, u32[]{:S(2)}) collective-permute-start(f32[9,4,128]{2,1,0:T(4,128)S(1)} %get-tuple-element.79), channel_id=1, source_target_pairs={{0,2},{2,0},{4,6},{6,4},{8,10},{10,8},{12,14},{14,12},{16,18},{18,... | collective-permute-start | bytes 55304 | tf_op jit(solution)/shard_map/ppermute | solution.py:74
  23.6 2.9 %collective-permute-start.9 = (f32[9,4,128]{2,1,0:T(4,128)S(1)}, f32[9,4,128]{2,1,0:T(4,128)S(1)}, u32[]{:S(2)}, u32[]{:S(2)}) collective-permute-start(f32[9,4,128]{2,1,0:T(4,128)S(1)} %get-tuple-element.86), channel_id=1, source_target_pairs={{0,16},{2,18},{4,20},{6,22},{8,24},{10,26},{12,28},{14,30},{16,0},... | collective-permute-start | bytes 55304 | tf_op jit(solution)/shard_map/ppermute | solution.py:74
  27.8 3.5 %collective-permute-start.11 = (f32[9,4,128]{2,1,0:T(4,128)S(1)}, f32[9,4,128]{2,1,0:T(4,128)S(1)}, u32[]{:S(2)}, u32[]{:S(2)}) collective-permute-start(f32[9,4,128]{2,1,0:T(4,128)S(1)} %get-tuple-element.88), channel_id=1, source_target_pairs={{0,20},{2,22},{4,16},{6,18},{8,28},{10,30},{12,24},{14,26},{16,4},... | collective-permute-start | bytes 55304 | tf_op jit(solution)/shard_map/ppermute | solution.py:74
  31.4 3.8 %collective-permute-start.13 = (f32[9,4,128]{2,1,0:T(4,128)S(1)}, f32[9,4,128]{2,1,0:T(4,128)S(1)}, u32[]{:S(2)}, u32[]{:S(2)}) collective-permute-start(f32[9,4,128]{2,1,0:T(4,128)S(1)} %get-tuple-element.90), channel_id=1, source_target_pairs={{0,24},{2,26},{4,28},{6,30},{8,16},{10,18},{12,20},{14,22},{16,8},... | collective-permute-start | bytes 55304 | tf_op jit(solution)/shard_map/ppermute | solution.py:74
  36.4 4.6 %collective-permute-start.15 = (f32[9,4,128]{2,1,0:T(4,128)S(1)}, f32[9,4,128]{2,1,0:T(4,128)S(1)}, u32[]{:S(2)}, u32[]{:S(2)}) collective-permute-start(f32[9,4,128]{2,1,0:T(4,128)S(1)} %get-tuple-element.92), channel_id=1, source_target_pairs={{0,28},{2,30},{4,24},{6,26},{8,20},{10,22},{12,16},{14,18},{16,12}... | collective-permute-start | bytes 55304 | tf_op jit(solution)/shard_map/ppermute | solution.py:74
  43.0 5.4 %collective-permute-done.16.refs_15_ = f32[9,4,128]{2,1,0:T(4,128)S(1)} collective-permute-done((f32[9,4,128]{2,1,0:T(4,128)S(1)}, f32[9,4,128]{2,1,0:T(4,128)S(1)}, u32[]{:S(2)}, u32[]{:S(2)}) %collective-permute-start.16) | collective-permute-done | bytes 18464 | tf_op jit(solution)/shard_map/ppermute | solution.py:74
  54.3 4.0 %collective-permute-start.23 = (f32[9,4,128]{2,1,0:T(4,128)S(1)}, f32[9,4,128]{2,1,0:T(4,128)S(1)}, u32[]{:S(2)}, u32[]{:S(2)}) collective-permute-start(f32[9,4,128]{2,1,0:T(4,128)S(1)} %get-tuple-element.101), channel_id=1, source_target_pairs={{0,14},{2,12},{4,10},{6,8},{8,6},{10,4},{12,2},{14,0},{16,30},{18,... | collective-permute-start | bytes 55304 | tf_op jit(solution)/shard_map/ppermute | solution.py:74
  58.3 2.8 %collective-permute-start.25 = (f32[9,4,128]{2,1,0:T(4,128)S(1)}, f32[9,4,128]{2,1,0:T(4,128)S(1)}, u32[]{:S(2)}, u32[]{:S(2)}) collective-permute-start(f32[9,4,128]{2,1,0:T(4,128)S(1)} %get-tuple-element.103), channel_id=1, source_target_pairs={{0,18},{2,16},{4,22},{6,20},{8,26},{10,24},{12,30},{14,28},{16,2},... | collective-permute-start | bytes 55304 | tf_op jit(solution)/shard_map/ppermute | solution.py:74
  61.1 4.8 %collective-permute-start.27 = (f32[9,4,128]{2,1,0:T(4,128)S(1)}, f32[9,4,128]{2,1,0:T(4,128)S(1)}, u32[]{:S(2)}, u32[]{:S(2)}) collective-permute-start(f32[9,4,128]{2,1,0:T(4,128)S(1)} %get-tuple-element.105), channel_id=1, source_target_pairs={{0,22},{2,20},{4,18},{6,16},{8,30},{10,28},{12,26},{14,24},{16,6},... | collective-permute-start | bytes 55304 | tf_op jit(solution)/shard_map/ppermute | solution.py:74
  66.0 3.6 %collective-permute-start.29 = (f32[9,4,128]{2,1,0:T(4,128)S(1)}, f32[9,4,128]{2,1,0:T(4,128)S(1)}, u32[]{:S(2)}, u32[]{:S(2)}) collective-permute-start(f32[9,4,128]{2,1,0:T(4,128)S(1)} %get-tuple-element.107), channel_id=1, source_target_pairs={{0,26},{2,24},{4,30},{6,28},{8,18},{10,16},{12,22},{14,20},{16,10}... | collective-permute-start | bytes 55304 | tf_op jit(solution)/shard_map/ppermute | solution.py:74
  69.8 5.5 %collective-permute-start.31 = (f32[9,4,128]{2,1,0:T(4,128)S(1)}, f32[9,4,128]{2,1,0:T(4,128)S(1)}, u32[]{:S(2)}, u32[]{:S(2)}) collective-permute-start(f32[9,4,128]{2,1,0:T(4,128)S(1)} %get-tuple-element.109), channel_id=1, source_target_pairs={{0,30},{2,28},{4,26},{6,24},{8,22},{10,20},{12,18},{14,16},{16,14}... | collective-permute-start | bytes 55304 | tf_op jit(solution)/shard_map/ppermute | solution.py:74
  79.5 7.6 %shard_map.100 = (f32[9,4,128]{2,1,0:T(4,128)S(1)}, f32[9,4,128]{2,1,0:T(4,128)S(1)}, f32[9,4,128]{2,1,0:T(4,128)S(1)}, f32[9,4,128]{2,1,0:T(4,128)S(1)}, f32[9,...) custom-call(f32[2,144,128]{2,1,0:T(8,128)S(1)} %get-tuple-element.11, ...), custom_call_target="tpu_custom_call" | custom-call | flops 42467328 | bytes 4472832 | tf_op jit(solution)/shard_map/pallas_call | solution.py:260
  90.7 2.8 %collective-permute-start.38 = (f32[9,4,128]{2,1,0:T(4,128)S(1)}, f32[9,4,128]{2,1,0:T(4,128)S(1)}, u32[]{:S(2)}, u32[]{:S(2)}) collective-permute-start(f32[9,4,128]{2,1,0:T(4,128)S(1)} %get-tuple-element.119), channel_id=1, source_target_pairs={{0,10},{2,8},{4,14},{6,12},{8,2},{10,0},{12,6},{14,4},{16,26},{18,... | collective-permute-start | bytes 55304 | tf_op jit(solution)/shard_map/ppermute | solution.py:74
  100.2 3.2 %collective-permute-start.43 = (f32[9,4,128]{2,1,0:T(4,128)S(1)}, f32[9,4,128]{2,1,0:T(4,128)S(1)}, u32[]{:S(2)}, u32[]{:S(2)}) collective-permute-start(f32[9,4,128]{2,1,0:T(4,128)S(1)} %get-tuple-element.124), channel_id=1, source_target_pairs={{0,20},{2,22},{4,16},{6,18},{8,28},{10,30},{12,24},{14,26},{16,4},... | collective-permute-start | bytes 55304 | tf_op jit(solution)/shard_map/ppermute | solution.py:74
  104.2 3.4 %collective-permute-start.45 = (f32[9,4,128]{2,1,0:T(4,128)S(1)}, f32[9,4,128]{2,1,0:T(4,128)S(1)}, u32[]{:S(2)}, u32[]{:S(2)}) collective-permute-start(f32[9,4,128]{2,1,0:T(4,128)S(1)} %get-tuple-element.126), channel_id=1, source_target_pairs={{0,24},{2,26},{4,28},{6,30},{8,16},{10,18},{12,20},{14,22},{16,8},... | collective-permute-start | bytes 55304 | tf_op jit(solution)/shard_map/ppermute | solution.py:74
  108.8 4.7 %collective-permute-start.47 = (f32[9,4,128]{2,1,0:T(4,128)S(1)}, f32[9,4,128]{2,1,0:T(4,128)S(1)}, u32[]{:S(2)}, u32[]{:S(2)}) collective-permute-start(f32[9,4,128]{2,1,0:T(4,128)S(1)} %get-tuple-element.128), channel_id=1, source_target_pairs={{0,28},{2,30},{4,24},{6,26},{8,20},{10,22},{12,16},{14,18},{16,12}... | collective-permute-start | bytes 55304 | tf_op jit(solution)/shard_map/ppermute | solution.py:74
  115.6 5.4 %collective-permute-done.48.refs_15_ = f32[9,4,128]{2,1,0:T(4,128)S(1)} collective-permute-done((f32[9,4,128]{2,1,0:T(4,128)S(1)}, f32[9,4,128]{2,1,0:T(4,128)S(1)}, u32[]{:S(2)}, u32[]{:S(2)}) %collective-permute-start.48) | collective-permute-done | bytes 18464 | tf_op jit(solution)/shard_map/ppermute | solution.py:74
  122.4 2.7 %collective-permute-start.51 = (f32[9,4,128]{2,1,0:T(4,128)S(1)}, f32[9,4,128]{2,1,0:T(4,128)S(1)}, u32[]{:S(2)}, u32[]{:S(2)}) collective-permute-start(f32[9,4,128]{2,1,0:T(4,128)S(1)} %get-tuple-element.133), channel_id=1, source_target_pairs={{0,6},{2,4},{4,2},{6,0},{8,14},{10,12},{12,10},{14,8},{16,22},{18,... | collective-permute-start | bytes 55304 | tf_op jit(solution)/shard_map/ppermute | solution.py:74
  126.8 4.1 %collective-permute-start.55 = (f32[9,4,128]{2,1,0:T(4,128)S(1)}, f32[9,4,128]{2,1,0:T(4,128)S(1)}, u32[]{:S(2)}, u32[]{:S(2)}) collective-permute-start(f32[9,4,128]{2,1,0:T(4,128)S(1)} %get-tuple-element.137), channel_id=1, source_target_pairs={{0,14},{2,12},{4,10},{6,8},{8,6},{10,4},{12,2},{14,0},{16,30},{18,... | collective-permute-start | bytes 55304 | tf_op jit(solution)/shard_map/ppermute | solution.py:74
  130.9 2.6 %collective-permute-start.57 = (f32[9,4,128]{2,1,0:T(4,128)S(1)}, f32[9,4,128]{2,1,0:T(4,128)S(1)}, u32[]{:S(2)}, u32[]{:S(2)}) collective-permute-start(f32[9,4,128]{2,1,0:T(4,128)S(1)} %get-tuple-element.139), channel_id=1, source_target_pairs={{0,18},{2,16},{4,22},{6,20},{8,26},{10,24},{12,30},{14,28},{16,2},... | collective-permute-start | bytes 55304 | tf_op jit(solution)/shard_map/ppermute | solution.py:74
  133.6 5.0 %collective-permute-start.59 = (f32[9,4,128]{2,1,0:T(4,128)S(1)}, f32[9,4,128]{2,1,0:T(4,128)S(1)}, u32[]{:S(2)}, u32[]{:S(2)}) collective-permute-start(f32[9,4,128]{2,1,0:T(4,128)S(1)} %get-tuple-element.141), channel_id=1, source_target_pairs={{0,22},{2,20},{4,18},{6,16},{8,30},{10,28},{12,26},{14,24},{16,6},... | collective-permute-start | bytes 55304 | tf_op jit(solution)/shard_map/ppermute | solution.py:74
  138.6 3.5 %collective-permute-start.61 = (f32[9,4,128]{2,1,0:T(4,128)S(1)}, f32[9,4,128]{2,1,0:T(4,128)S(1)}, u32[]{:S(2)}, u32[]{:S(2)}) collective-permute-start(f32[9,4,128]{2,1,0:T(4,128)S(1)} %get-tuple-element.143), channel_id=1, source_target_pairs={{0,26},{2,24},{4,30},{6,28},{8,18},{10,16},{12,22},{14,20},{16,10}... | collective-permute-start | bytes 55304 | tf_op jit(solution)/shard_map/ppermute | solution.py:74
  142.5 5.6 %collective-permute-start.63 = (f32[9,4,128]{2,1,0:T(4,128)S(1)}, f32[9,4,128]{2,1,0:T(4,128)S(1)}, u32[]{:S(2)}, u32[]{:S(2)}) collective-permute-start(f32[9,4,128]{2,1,0:T(4,128)S(1)} %get-tuple-element.145), channel_id=1, source_target_pairs={{0,30},{2,28},{4,26},{6,24},{8,22},{10,20},{12,18},{14,16},{16,14}... | collective-permute-start | bytes 55304 | tf_op jit(solution)/shard_map/ppermute | solution.py:74
  (132 shorter events, 48.4 us)
Async XLA Ops:
  21.0 10.3 %collective-permute-start.7 = (f32[9,4,128]{2,1,0:T(4,128)S(1)}, f32[9,4,128]{2,1,0:T(4,128)S(1)}, u32[]{:S(2)}, u32[]{:S(2)}) collective-permute-start(f32[9,4,128]{2,1,0:T(4,128)S(1)} %get-tuple-element.84), channel_id=1, source_target_pairs={{0,12},{2,14},{4,8},{6,10},{8,4},{10,6},{12,0},{14,2},{16,28},{18,... | collective-permute-start | bytes 55304 | tf_op jit(solution)/shard_map/ppermute | solution.py:74
  23.6 11.6 %collective-permute-start.9 = (f32[9,4,128]{2,1,0:T(4,128)S(1)}, f32[9,4,128]{2,1,0:T(4,128)S(1)}, u32[]{:S(2)}, u32[]{:S(2)}) collective-permute-start(f32[9,4,128]{2,1,0:T(4,128)S(1)} %get-tuple-element.86), channel_id=1, source_target_pairs={{0,16},{2,18},{4,20},{6,22},{8,24},{10,26},{12,28},{14,30},{16,0},... | collective-permute-start | bytes 55304 | tf_op jit(solution)/shard_map/ppermute | solution.py:74
  26.5 9.8 %collective-permute-start.10 = (f32[9,4,128]{2,1,0:T(4,128)S(1)}, f32[9,4,128]{2,1,0:T(4,128)S(1)}, u32[]{:S(2)}, u32[]{:S(2)}) collective-permute-start(f32[9,4,128]{2,1,0:T(4,128)S(1)} %get-tuple-element.87), channel_id=1, source_target_pairs={{0,18},{2,16},{4,22},{6,20},{8,26},{10,24},{12,30},{14,28},{16,2},... | collective-permute-start | bytes 55304 | tf_op jit(solution)/shard_map/ppermute | solution.py:74
  27.8 13.1 %collective-permute-start.11 = (f32[9,4,128]{2,1,0:T(4,128)S(1)}, f32[9,4,128]{2,1,0:T(4,128)S(1)}, u32[]{:S(2)}, u32[]{:S(2)}) collective-permute-start(f32[9,4,128]{2,1,0:T(4,128)S(1)} %get-tuple-element.88), channel_id=1, source_target_pairs={{0,20},{2,22},{4,16},{6,18},{8,28},{10,30},{12,24},{14,26},{16,4},... | collective-permute-start | bytes 55304 | tf_op jit(solution)/shard_map/ppermute | solution.py:74
  31.3 11.1 %collective-permute-start.12 = (f32[9,4,128]{2,1,0:T(4,128)S(1)}, f32[9,4,128]{2,1,0:T(4,128)S(1)}, u32[]{:S(2)}, u32[]{:S(2)}) collective-permute-start(f32[9,4,128]{2,1,0:T(4,128)S(1)} %get-tuple-element.89), channel_id=1, source_target_pairs={{0,22},{2,20},{4,18},{6,16},{8,30},{10,28},{12,26},{14,24},{16,6},... | collective-permute-start | bytes 55304 | tf_op jit(solution)/shard_map/ppermute | solution.py:74
  31.4 11.1 %collective-permute-start.13 = (f32[9,4,128]{2,1,0:T(4,128)S(1)}, f32[9,4,128]{2,1,0:T(4,128)S(1)}, u32[]{:S(2)}, u32[]{:S(2)}) collective-permute-start(f32[9,4,128]{2,1,0:T(4,128)S(1)} %get-tuple-element.90), channel_id=1, source_target_pairs={{0,24},{2,26},{4,28},{6,30},{8,16},{10,18},{12,20},{14,22},{16,8},... | collective-permute-start | bytes 55304 | tf_op jit(solution)/shard_map/ppermute | solution.py:74
  54.3 11.6 %collective-permute-start.23 = (f32[9,4,128]{2,1,0:T(4,128)S(1)}, f32[9,4,128]{2,1,0:T(4,128)S(1)}, u32[]{:S(2)}, u32[]{:S(2)}) collective-permute-start(f32[9,4,128]{2,1,0:T(4,128)S(1)} %get-tuple-element.101), channel_id=1, source_target_pairs={{0,14},{2,12},{4,10},{6,8},{8,6},{10,4},{12,2},{14,0},{16,30},{18,... | collective-permute-start | bytes 55304 | tf_op jit(solution)/shard_map/ppermute | solution.py:74
  58.3 11.4 %collective-permute-start.25 = (f32[9,4,128]{2,1,0:T(4,128)S(1)}, f32[9,4,128]{2,1,0:T(4,128)S(1)}, u32[]{:S(2)}, u32[]{:S(2)}) collective-permute-start(f32[9,4,128]{2,1,0:T(4,128)S(1)} %get-tuple-element.103), channel_id=1, source_target_pairs={{0,18},{2,16},{4,22},{6,20},{8,26},{10,24},{12,30},{14,28},{16,2},... | collective-permute-start | bytes 55304 | tf_op jit(solution)/shard_map/ppermute | solution.py:74
  61.1 14.3 %collective-permute-start.27 = (f32[9,4,128]{2,1,0:T(4,128)S(1)}, f32[9,4,128]{2,1,0:T(4,128)S(1)}, u32[]{:S(2)}, u32[]{:S(2)}) collective-permute-start(f32[9,4,128]{2,1,0:T(4,128)S(1)} %get-tuple-element.105), channel_id=1, source_target_pairs={{0,22},{2,20},{4,18},{6,16},{8,30},{10,28},{12,26},{14,24},{16,6},... | collective-permute-start | bytes 55304 | tf_op jit(solution)/shard_map/ppermute | solution.py:74
  65.9 9.5 %collective-permute-start.28 = (f32[9,4,128]{2,1,0:T(4,128)S(1)}, f32[9,4,128]{2,1,0:T(4,128)S(1)}, u32[]{:S(2)}, u32[]{:S(2)}) collective-permute-start(f32[9,4,128]{2,1,0:T(4,128)S(1)} %get-tuple-element.106), channel_id=1, source_target_pairs={{0,24},{2,26},{4,28},{6,30},{8,16},{10,18},{12,20},{14,22},{16,8},... | collective-permute-start | bytes 55304 | tf_op jit(solution)/shard_map/ppermute | solution.py:74
  66.0 9.3 %collective-permute-start.29 = (f32[9,4,128]{2,1,0:T(4,128)S(1)}, f32[9,4,128]{2,1,0:T(4,128)S(1)}, u32[]{:S(2)}, u32[]{:S(2)}) collective-permute-start(f32[9,4,128]{2,1,0:T(4,128)S(1)} %get-tuple-element.107), channel_id=1, source_target_pairs={{0,26},{2,24},{4,30},{6,28},{8,18},{10,16},{12,22},{14,20},{16,10}... | collective-permute-start | bytes 55304 | tf_op jit(solution)/shard_map/ppermute | solution.py:74
  90.7 9.6 %collective-permute-start.38 = (f32[9,4,128]{2,1,0:T(4,128)S(1)}, f32[9,4,128]{2,1,0:T(4,128)S(1)}, u32[]{:S(2)}, u32[]{:S(2)}) collective-permute-start(f32[9,4,128]{2,1,0:T(4,128)S(1)} %get-tuple-element.119), channel_id=1, source_target_pairs={{0,10},{2,8},{4,14},{6,12},{8,2},{10,0},{12,6},{14,4},{16,26},{18,... | collective-permute-start | bytes 55304 | tf_op jit(solution)/shard_map/ppermute | solution.py:74
  93.5 10.0 %collective-permute-start.39 = (f32[9,4,128]{2,1,0:T(4,128)S(1)}, f32[9,4,128]{2,1,0:T(4,128)S(1)}, u32[]{:S(2)}, u32[]{:S(2)}) collective-permute-start(f32[9,4,128]{2,1,0:T(4,128)S(1)} %get-tuple-element.120), channel_id=1, source_target_pairs={{0,12},{2,14},{4,8},{6,10},{8,4},{10,6},{12,0},{14,2},{16,28},{18,... | collective-permute-start | bytes 55304 | tf_op jit(solution)/shard_map/ppermute | solution.py:74
  94.4 9.8 %collective-permute-start.40 = (f32[9,4,128]{2,1,0:T(4,128)S(1)}, f32[9,4,128]{2,1,0:T(4,128)S(1)}, u32[]{:S(2)}, u32[]{:S(2)}) collective-permute-start(f32[9,4,128]{2,1,0:T(4,128)S(1)} %get-tuple-element.121), channel_id=1, source_target_pairs={{0,14},{2,12},{4,10},{6,8},{8,6},{10,4},{12,2},{14,0},{16,30},{18,... | collective-permute-start | bytes 55304 | tf_op jit(solution)/shard_map/ppermute | solution.py:74
  96.5 11.1 %collective-permute-start.41 = (f32[9,4,128]{2,1,0:T(4,128)S(1)}, f32[9,4,128]{2,1,0:T(4,128)S(1)}, u32[]{:S(2)}, u32[]{:S(2)}) collective-permute-start(f32[9,4,128]{2,1,0:T(4,128)S(1)} %get-tuple-element.122), channel_id=1, source_target_pairs={{0,16},{2,18},{4,20},{6,22},{8,24},{10,26},{12,28},{14,30},{16,0},... | collective-permute-start | bytes 55304 | tf_op jit(solution)/shard_map/ppermute | solution.py:74
  98.8 10.0 %collective-permute-start.42 = (f32[9,4,128]{2,1,0:T(4,128)S(1)}, f32[9,4,128]{2,1,0:T(4,128)S(1)}, u32[]{:S(2)}, u32[]{:S(2)}) collective-permute-start(f32[9,4,128]{2,1,0:T(4,128)S(1)} %get-tuple-element.123), channel_id=1, source_target_pairs={{0,18},{2,16},{4,22},{6,20},{8,26},{10,24},{12,30},{14,28},{16,2},... | collective-permute-start | bytes 55304 | tf_op jit(solution)/shard_map/ppermute | solution.py:74
  100.2 13.2 %collective-permute-start.43 = (f32[9,4,128]{2,1,0:T(4,128)S(1)}, f32[9,4,128]{2,1,0:T(4,128)S(1)}, u32[]{:S(2)}, u32[]{:S(2)}) collective-permute-start(f32[9,4,128]{2,1,0:T(4,128)S(1)} %get-tuple-element.124), channel_id=1, source_target_pairs={{0,20},{2,22},{4,16},{6,18},{8,28},{10,30},{12,24},{14,26},{16,4},... | collective-permute-start | bytes 55304 | tf_op jit(solution)/shard_map/ppermute | solution.py:74
  103.4 10.2 %collective-permute-start.44 = (f32[9,4,128]{2,1,0:T(4,128)S(1)}, f32[9,4,128]{2,1,0:T(4,128)S(1)}, u32[]{:S(2)}, u32[]{:S(2)}) collective-permute-start(f32[9,4,128]{2,1,0:T(4,128)S(1)} %get-tuple-element.125), channel_id=1, source_target_pairs={{0,22},{2,20},{4,18},{6,16},{8,30},{10,28},{12,26},{14,24},{16,6},... | collective-permute-start | bytes 55304 | tf_op jit(solution)/shard_map/ppermute | solution.py:74
  104.2 9.5 %collective-permute-start.45 = (f32[9,4,128]{2,1,0:T(4,128)S(1)}, f32[9,4,128]{2,1,0:T(4,128)S(1)}, u32[]{:S(2)}, u32[]{:S(2)}) collective-permute-start(f32[9,4,128]{2,1,0:T(4,128)S(1)} %get-tuple-element.126), channel_id=1, source_target_pairs={{0,24},{2,26},{4,28},{6,30},{8,16},{10,18},{12,20},{14,22},{16,8},... | collective-permute-start | bytes 55304 | tf_op jit(solution)/shard_map/ppermute | solution.py:74
  126.8 11.8 %collective-permute-start.55 = (f32[9,4,128]{2,1,0:T(4,128)S(1)}, f32[9,4,128]{2,1,0:T(4,128)S(1)}, u32[]{:S(2)}, u32[]{:S(2)}) collective-permute-start(f32[9,4,128]{2,1,0:T(4,128)S(1)} %get-tuple-element.137), channel_id=1, source_target_pairs={{0,14},{2,12},{4,10},{6,8},{8,6},{10,4},{12,2},{14,0},{16,30},{18,... | collective-permute-start | bytes 55304 | tf_op jit(solution)/shard_map/ppermute | solution.py:74
  130.9 11.2 %collective-permute-start.57 = (f32[9,4,128]{2,1,0:T(4,128)S(1)}, f32[9,4,128]{2,1,0:T(4,128)S(1)}, u32[]{:S(2)}, u32[]{:S(2)}) collective-permute-start(f32[9,4,128]{2,1,0:T(4,128)S(1)} %get-tuple-element.139), channel_id=1, source_target_pairs={{0,18},{2,16},{4,22},{6,20},{8,26},{10,24},{12,30},{14,28},{16,2},... | collective-permute-start | bytes 55304 | tf_op jit(solution)/shard_map/ppermute | solution.py:74
  133.6 14.4 %collective-permute-start.59 = (f32[9,4,128]{2,1,0:T(4,128)S(1)}, f32[9,4,128]{2,1,0:T(4,128)S(1)}, u32[]{:S(2)}, u32[]{:S(2)}) collective-permute-start(f32[9,4,128]{2,1,0:T(4,128)S(1)} %get-tuple-element.141), channel_id=1, source_target_pairs={{0,22},{2,20},{4,18},{6,16},{8,30},{10,28},{12,26},{14,24},{16,6},... | collective-permute-start | bytes 55304 | tf_op jit(solution)/shard_map/ppermute | solution.py:74
  138.6 9.5 %collective-permute-start.60 = (f32[9,4,128]{2,1,0:T(4,128)S(1)}, f32[9,4,128]{2,1,0:T(4,128)S(1)}, u32[]{:S(2)}, u32[]{:S(2)}) collective-permute-start(f32[9,4,128]{2,1,0:T(4,128)S(1)} %get-tuple-element.142), channel_id=1, source_target_pairs={{0,24},{2,26},{4,28},{6,30},{8,16},{10,18},{12,20},{14,22},{16,8},... | collective-permute-start | bytes 55304 | tf_op jit(solution)/shard_map/ppermute | solution.py:74
  138.6 9.5 %collective-permute-start.61 = (f32[9,4,128]{2,1,0:T(4,128)S(1)}, f32[9,4,128]{2,1,0:T(4,128)S(1)}, u32[]{:S(2)}, u32[]{:S(2)}) collective-permute-start(f32[9,4,128]{2,1,0:T(4,128)S(1)} %get-tuple-element.143), channel_id=1, source_target_pairs={{0,26},{2,24},{4,30},{6,28},{8,18},{10,16},{12,22},{14,20},{16,10}... | collective-permute-start | bytes 55304 | tf_op jit(solution)/shard_map/ppermute | solution.py:74
  (50 other events, 694.0 us)

commit v3 on v1

--- a/solution.py
+++ b/solution.py
@@ -28,14 +28,73 @@
         target[rows, :] = source(first + at, size)
 
 
-def prep_coupling_kernel(rows, coupling, inside, out):
+def prep_kernel(fused, chains, *refs):
+    coupling_hbm, retarded_hbm, *free_hbm = refs[: 2 + 2]
+    offsets, shifts, coupled, occupied = refs[4:8]
+    links, lanes, is_near, left, right, mixing = refs[8:14]
+    owns = refs[14 : 14 + chains]
+    coupling, retarded, free, sems = refs[14 + chains :]
+    energies, pairs, atoms = retarded.shape
+    rows = fused * energies
     group = ROWS // rows
-    pairs = coupling.shape[1]
+    copies = [pltpu.make_async_copy(free_hbm[f], free.at[f], sems.at[f]) for f in range(2)]
+    copies.append(pltpu.make_async_copy(retarded_hbm, retarded, sems.at[2]))
     for n in range(NB):
+        copies.append(
+            pltpu.make_async_copy(coupling_hbm.at[n], coupling.at[n], sems.at[3 + n])
+        )
+    for copy in copies:
+        copy.start()
+
+    total = mixing.shape[1]
+    gap = lax.broadcasted_iota(jnp.int32, (total, total), 1) - lax.broadcasted_iota(
+        jnp.int32, (total, total), 0
+    )
+    lesser = jnp.zeros((total, total), jnp.float32)
+    greater = jnp.zeros((total, total), jnp.float32)
+    for mode in range(shifts.shape[0]):
+        shift = shifts[mode]
+        absorb = coupled[mode] * occupied[mode]
+        emit = coupled[mode] * (occupied[mode] + 1.0)
+        ahead = gap == shift
+        behind = gap == -shift
+        lesser = lesser + jnp.where(ahead, emit, jnp.where(behind, absorb, 0.0))
+        greater = greater + jnp.where(ahead, absorb, jnp.where(behind, emit, 0.0))
+    mixing[0] = lesser
+    mixing[1] = greater
+
+    slab, slabs = lax.axis_index("slab"), lax.axis_size("slab")
+    targets = offsets[...] + lax.broadcasted_iota(jnp.int32, (NB, atoms), 1)
+    placed = targets + slab * atoms
+    inside = ((placed >= 0) & (placed < slabs * atoms)).astype(jnp.float32)
+    near = ((targets >= 0) & (targets < atoms)).astype(jnp.int32)
+    lane = jnp.where(targets < 0, targets + atoms, targets)
+    lane = jnp.where(lane >= atoms, lane - atoms, lane)
+    for n in range(NB):
+        some = slice(n % group * rows, (n % group + 1) * rows)
+        lanes[n // group, some, :] = jnp.broadcast_to(lane[n : n + 1, :], (rows, atoms))
+        is_near[n // group, some, :] = jnp.broadcast_to(near[n : n + 1, :], (rows, atoms))
+
+    copies[0].wait()
+    copies[1].wait()
+    for chain, own in enumerate(owns):
+        for row in range(ROWS):
+            function, energy = chain * fused + row % rows // energies, row % energies
+            spread_rows(
+                own, 0, row, lambda at, size: free[function, energy, at : at + size, :], 0, pairs
+            )
+    copies[2].wait()
+    share = pairs * rows // ROWS
+    for row in range(ROWS):
+        read = lambda at, size: retarded[row % energies, at : at + size, :]
+        spread_rows(left, 0, row, read, row // rows * share, share)
+        spread_rows(right, 0, row, read, 0, pairs)
+    for n in range(NB):
+        copies[3 + n].wait()
         valid = inside[n : n + 1, :]
         for row in range(rows):
             spread_rows(
-                out,
+                links,
                 (n // group) * pairs,
                 (n % group) * rows + row,
                 lambda at, size: coupling[n, at : at + size, :] * valid,
@@ -44,53 +103,24 @@
             )
 
 
-def prep_dressing_kernel(rows, retarded, shifts, coupled, occupied, left, right, mixing):
-    energies, pairs, _ = retarded.shape
-    total = mixing.shape[1]
-    share = pairs * rows // ROWS
-    for row in range(ROWS):
-        read = lambda at, size: retarded[row % energies, at : at + size, :]
-        spread_rows(left, 0, row, read, row // rows * share, share)
-        spread_rows(right, 0, row, read, 0, pairs)
-    places = lax.broadcasted_iota(jnp.int32, (total, total), 0)
-    gap = lax.broadcasted_iota(jnp.int32, (total, total), 1) - places
-
-    def add_mode(mode, kernels):
-        lesser, greater = kernels
-        shift = shifts[mode]
-        absorb = coupled[mode] * occupied[mode]
-        emit = coupled[mode] * (occupied[mode] + 1.0)
-        ahead = gap == shift
-        behind = gap == -shift
-        lesser = lesser + jnp.where(ahead, emit, 0.0) + jnp.where(behind, absorb, 0.0)
-        greater = greater + jnp.where(ahead, absorb, 0.0) + jnp.where(behind, emit, 0.0)
-        return lesser, greater
-
-    empty = jnp.zeros((total, total), jnp.float32)
-    lesser, greater = lax.fori_loop(0, shifts.shape[0], add_mode, (empty, empty))
-    mixing[0] = lesser
-    mixing[1] = greater
-
-
-def couple_kernel(fused, *refs):
-    near, far = refs[:fused], refs[fused : 2 * fused]
-    lanes, is_near, links_hbm, out = refs[2 * fused : 2 * fused + 4]
-    own, other, gathered_a, gathered_b, total, links, sems = refs[2 * fused + 4 :]
-    energies, pairs, atoms = near[0].shape
+def couple_kernel(fused, energies, own, *refs):
+    far, refs = refs[:-8], refs[-8:]
+    lanes, is_near, links, out = refs[:4]
+    other, gathered_a, gathered_b, total = refs[4:]
+    _, pairs, _, atoms = links.shape
     rows = fused * energies
     group = ROWS // rows
     groups = NB // group
-    copies = [
-        pltpu.make_async_copy(links_hbm.at[g], links.at[g], sems.at[g]) for g in range(groups)
-    ]
-    for copy in copies:
-        copy.start()
-    for row in range(ROWS):
-        function, energy = row % rows // energies, row % energies
-        for target, sources in ((own, near), (other, far)):
-            source = sources[function]
+    if len(far) == 1:
+        for pair in range(pairs):
+            value = far[0][pair]
+            for at in range(0, ROWS, rows):
+                other[pair * ROWS + at : pair * ROWS + at + rows, :] = value
+    else:
+        for row in range(ROWS):
+            source = far[row % rows // energies]
             spread_rows(
-                target, 0, row, lambda at, size: source[energy, at : at + size, :], 0, pairs
+                other, 0, row, lambda at, size: source[row % energies, at : at + size, :], 0, pairs
             )
     buffers = (gathered_a, gathered_b)
 
@@ -109,7 +139,6 @@
     chunk = pairs // steps
     lax.fori_loop(0, steps, lambda step, _: gather(0, step * chunk, chunk), None)
     for g in range(groups):
-        copies[g].wait()
         source = buffers[g % 2]
 
         def block_row(step, _):
@@ -168,15 +197,9 @@
                 ]
 
 
-def dress_kernel(fused, *refs):
-    sigma, left, right = refs[:3]
-    free, out = refs[3 : 3 + fused], refs[3 + fused : 3 + 2 * fused]
-    copied, dressed = refs[3 + 2 * fused :]
-    energies, pairs, atoms = free[0].shape
-    rows = fused * energies
+def dress(rows, sigma, left, right, copied, keep):
     parts = ROWS // rows
-    share = pairs // parts
-    for pair in range(pairs):
+    for pair in range(NORB * NORB):
         value = sigma[pair]
         for part in range(parts):
             copied[pair, part * rows : (part + 1) * rows, :] = value
@@ -191,8 +214,42 @@
             value = inner[0] * right[k * NORB]
             for l in range(1, NORB):
                 value = value + inner[l] * right[k * NORB + l]
-            at = (i * NORB + k) * ROWS
-            dressed[at : at + ROWS, :] = value
+            keep(i * NORB + k, value)
+
+
+def dress_between_kernel(rows, sigma, left, right, free, own, compact, copied):
+    pairs, _, atoms = sigma.shape[0], rows, sigma.shape[2]
+    share = left.shape[0]
+    row_at = lax.broadcasted_iota(jnp.int32, (ROWS, atoms), 0)
+
+    def keep(at, value):
+        for part in range(ROWS // rows):
+            held = (row_at >= part * rows) & (row_at < (part + 1) * rows)
+            piece = jnp.where(held, value, 0.0)
+            width = ROWS // 2
+            while width >= rows:
+                piece = piece + pltpu.roll(piece, width, 0)
+                width //= 2
+            pair = part * share + at
+            piece = piece + free[pair * ROWS : (pair + 1) * ROWS, :]
+            own[pair * ROWS : (pair + 1) * ROWS, :] = piece
+            compact[pair] = piece[:rows]
+
+    dress(rows, sigma, left, right, copied, keep)
+
+
+def dress_last_kernel(fused, *refs):
+    sigma, left, right = refs[:3]
+    free, out = refs[3 : 3 + fused], refs[3 + fused : 3 + 2 * fused]
+    copied, dressed = refs[3 + 2 * fused :]
+    energies = free[0].shape[0]
+    rows = fused * energies
+    share = left.shape[0]
+
+    def keep(at, value):
+        dressed[at * ROWS : (at + 1) * ROWS, :] = value
+
+    dress(rows, sigma, left, right, copied, keep)
     for row in range(ROWS):
         function, energy, part = row % rows // energies, row % energies, row // rows
         for at, size in tiles(share):
@@ -204,7 +261,10 @@
 
 
 def call(kernel, outs, scratch, flops, *operands, spaces=None):
-    shapes = [jax.ShapeDtypeStruct(dims, jnp.float32) for dims in outs]
+    shapes = [
+        x if isinstance(x, jax.ShapeDtypeStruct) else jax.ShapeDtypeStruct(x, jnp.float32)
+        for x in outs
+    ]
     vmem = pl.BlockSpec(memory_space=pltpu.VMEM)
     moved = sum(x.size for x in operands) + sum(x.size for x in shapes)
     return pl.pallas_call(
@@ -254,74 +314,61 @@
     total = energies * parts
     vmem = pl.BlockSpec(memory_space=pltpu.VMEM)
     smem = pl.BlockSpec(memory_space=pltpu.SMEM)
-    away = pl.BlockSpec(memory_space=pl.ANY)
-
-    targets = neighbour_offsets + jnp.arange(atoms, dtype=jnp.int32)[None, :]
-    placed = targets + lax.axis_index("slab") * atoms
-    inside = (placed >= 0) & (placed < lax.axis_size("slab") * atoms)
-
-    def widened(values):
-        return jnp.broadcast_to(values[:, None, :], (NB, rows, atoms)).reshape(groups, ROWS, atoms)
-
-    lanes = widened(jnp.remainder(targets, atoms))
-    is_near = widened(((targets >= 0) & (targets < atoms)).astype(jnp.int32))
+    away = pl.BlockSpec(memory_space=pltpu.HBM)
+    indices = jax.ShapeDtypeStruct((groups, ROWS, atoms), jnp.int32)
+    wide = (pairs * ROWS, atoms)
+    deep = (pairs, ROWS, atoms)
+    work = 4 * NORB * rows * pairs * atoms
 
     free = (lesser_free, greater_free)
     chains = [free[at : at + fused] for at in range(0, 2, fused)]
-    greens = list(chains)
-    halos = [tuple(beside(g) for g in chain) for chain in greens]
-
-    (links,) = call(
-        functools.partial(prep_coupling_kernel, rows),
-        [(groups * pairs * ROWS, atoms)],
-        [],
+    halos = [tuple(beside(g) for g in chain) for chain in chains]
+    links, lanes, is_near, left, right, mixing, *frees = call(
+        functools.partial(prep_kernel, fused, len(chains)),
+        [
+            (groups * pairs * ROWS, atoms),
+            indices,
+            indices,
+            (pairs * rows, atoms),
+            wide,
+            (2, total, total),
+        ]
+        + [wide] * len(chains),
+        [
+            pltpu.VMEM(coupling.shape, jnp.float32),
+            pltpu.VMEM(retarded.shape, jnp.float32),
+            pltpu.VMEM((2,) + retarded.shape, jnp.float32),
+            pltpu.SemaphoreType.DMA((3 + NB,)),
+        ],
         coupling.size * rows,
         coupling,
-        inside.astype(jnp.float32),
-    )
-    links = links.reshape(groups, pairs, ROWS, atoms)
-    left, right, mixing = call(
-        functools.partial(prep_dressing_kernel, rows),
-        [(pairs * rows, atoms), (pairs * ROWS, atoms), (2, total, total)],
-        [],
-        retarded.size * ROWS,
         retarded,
+        *free,
+        neighbour_offsets,
         phonon_shift,
         phonon_coupling,
         phonon_occupation,
-        spaces=[vmem, smem, smem, smem],
+        spaces=[away] * 4 + [vmem] + [smem] * 3,
     )
+    links = links.reshape(groups, pairs, ROWS, atoms)
     left = left.reshape(pairs * rows // ROWS, ROWS, atoms)
     right = right.reshape(pairs, ROWS, atoms)
-
-    wide = pltpu.VMEM((pairs * ROWS, atoms), jnp.float32)
-    deep = pltpu.VMEM((pairs, ROWS, atoms), jnp.float32)
-    flat = pltpu.VMEM((total, share * atoms), jnp.float32)
-    work = 4 * NORB * rows * pairs * atoms
+    owns = frees
 
     for step in range(ITERS):
         coupled = [
             call(
-                functools.partial(couple_kernel, fused),
+                functools.partial(couple_kernel, fused, energies),
                 [(parts * share, rows, atoms)],
-                [
-                    wide,
-                    wide,
-                    deep,
-                    deep,
-                    deep,
-                    pltpu.VMEM(links.shape, jnp.float32),
-                    pltpu.SemaphoreType.DMA((groups,)),
-                ],
+                [pltpu.VMEM(wide, jnp.float32)] + [pltpu.VMEM(deep, jnp.float32)] * 3,
                 NB * work,
-                *green,
+                own,
                 *halo,
                 lanes,
                 is_near,
                 links,
-                spaces=[vmem] * (2 * fused + 2) + [away],
             )[0]
-            for green, halo in zip(greens, halos)
+            for own, halo in zip(owns, halos)
         ]
         gathered = [
             lax.all_to_all(x.reshape(parts, share, rows, atoms), "energy", 0, 0) for x in coupled
@@ -330,9 +377,9 @@
             call(
                 functools.partial(mix_kernel, fused),
                 [x.shape],
-                [flat, flat],
+                [pltpu.VMEM((total, share * atoms), jnp.float32)] * 2,
                 2 * total * x.size,
-                mixing[at * fused : (at + 1) * fused],
+                mixing if len(chains) == 1 else mixing[at * fused : (at + 1) * fused],
                 x,
             )[0]
             for at, x in enumerate(gathered)
@@ -340,22 +387,36 @@
         sigma = [
             lax.all_to_all(x, "energy", 0, 0).reshape(parts * share, rows, atoms) for x in mixed
         ]
-        greens = [
-            call(
-                functools.partial(dress_kernel, fused),
-                [lesser_free.shape] * fused,
-                [deep, pltpu.VMEM((pairs * rows, atoms), jnp.float32)],
-                work,
-                x,
-                left,
-                right,
-                *chain,
-            )
-            for x, chain in zip(sigma, chains)
-        ]
         if step < ITERS - 1:
-            halos = [tuple(beside(g) for g in chain) for chain in greens]
-    return tuple(g for chain in greens for g in chain)
+            pieces = [
+                call(
+                    functools.partial(dress_between_kernel, rows),
+                    [wide, (pairs, rows, atoms)],
+                    [pltpu.VMEM(deep, jnp.float32)],
+                    work,
+                    x,
+                    left,
+                    right,
+                    start,
+                )
+                for x, start in zip(sigma, frees)
+            ]
+            owns = [own for own, _ in pieces]
+            halos = [(beside(compact),) for _, compact in pieces]
+    outs = [
+        call(
+            functools.partial(dress_last_kernel, fused),
+            [lesser_free.shape] * fused,
+            [pltpu.VMEM(deep, jnp.float32), pltpu.VMEM((pairs * rows, atoms), jnp.float32)],
+            work,
+            x,
+            left,
+            right,
+            *chain,
+        )
+        for x, chain in zip(sigma, chains)
+    ]
+    return tuple(g for chain in outs for g in chain)
 
 
 def solution(mesh):

time: 93.8 us -> 90.4 us (0.964)
  blocking collectives: 41.3 us -> 60.2 us
  starting transfers between devices: 9.5 us -> 0.67 us
  waiting for transfers between devices: 7.51 us -> 1.57 us
  local copies, waits for them, and re-layouts: 11.3 us -> 6.56 us
  Pallas kernels: 21.8 us -> 20.3 us
    all_to_all x1 -> x2, blocking collectives: 14.4 us -> 33.2 us  [body(): lax.all_to_all(x.reshape(parts, share, rows, atoms), 'energy', 0, 0)]
    all_to_all x1 -> x0, starting transfers between devices: 8.33 us -> none  [body(): lax.all_to_all(x.reshape(parts, share, rows, atoms), 'energy', 0, 0)]
    all_to_all x1 -> x0, waiting for transfers between devices: 6.44 us -> none  [body(): lax.all_to_all(x.reshape(parts, share, rows, atoms), 'energy', 0, 0)]
    unnamed x48 -> x16, local copies, waits for them, and re-layouts: 11.3 us -> 6.56 us
    pallas_call x8 -> x7, Pallas kernels: 21.8 us -> 20.3 us  [call(): pl.pallas_call(kernel, out_shape=shapes, in_specs=spaces or [vmem] * len(...]
  transfers between devices with their start and end apart: 5 -> 3, of which waited for: 3 -> 1; matrix products, arithmetic and copies ran while one was open for 1% -> 0% of each run, Pallas kernels for 2% -> 4%
where the time goes in v3:
time: 90.4 us; the launch traced here: 90 us
  blocking collectives  60.2 us (67%)
  Pallas kernels  20.3 us (22%)
  local copies, waits for them, and re-layouts  6.56 us (7%)
  waiting for transfers between devices  1.57 us (2%)
    all_to_all x2, blocking collectives, body(): lax.all_to_all(x.reshape(parts, share, rows, atoms), 'energy', 0, 0)  33.2 us
    all_to_all x2, blocking collectives, body(): lax.all_to_all(x, 'energy', 0, 0).reshape(parts * share, rows, atoms)  26.9 us
    pallas_call x7, Pallas kernels, call(): pl.pallas_call(kernel, out_shape=shapes, in_specs=spaces or [vmem] * len(...  20.3 us
    unnamed x16, local copies, waits for them, and re-layouts  6.56 us
  transfers between devices with their start and end apart: 3, of which 1 were waited for; matrix products, arithmetic and copies ran while one was open for 0% of the time, Pallas kernels for 4%

profile of v3, /device:TPU:0, one launch (start us, length us, event | category | flops | bytes accessed | tf_op | source)
XLA Modules:
  0.0 90.0 jit_solution(11912277882189382627)
XLA Ops:
  0.6 0.5 collective-permute-start
  1.2 0.1 collective-permute-start.1
  1.2 1.2 %copy-done = f32[12,144,128]{2,1,0:T(8,128)S(1)} copy-done((f32[12,144,128]{2,1,0:T(8,128)S(1)}, f32[12,144,128]{2,1,0:T(8,128)}, u32[]{:S(2)}) %copy-start) | copy-done | bytes 884760
  2.4 0.9 %copy-done.1 = f32[2,144,128]{2,1,0:T(8,128)S(1)} copy-done((f32[2,144,128]{2,1,0:T(8,128)S(1)}, f32[2,144,128]{2,1,0:T(8,128)}, u32[]{:S(2)}) %copy-start.1) | copy-done | bytes 147480
  3.3 0.9 %copy-done.2 = f32[2,144,128]{2,1,0:T(8,128)S(1)} copy-done((f32[2,144,128]{2,1,0:T(8,128)S(1)}, f32[2,144,128]{2,1,0:T(8,128)}, u32[]{:S(2)}) %copy-start.2) | copy-done | bytes 147480
  4.2 0.9 %copy-done.3 = f32[2,144,128]{2,1,0:T(8,128)S(1)} copy-done((f32[2,144,128]{2,1,0:T(8,128)S(1)}, f32[2,144,128]{2,1,0:T(8,128)}, u32[]{:S(2)}) %copy-start.3) | copy-done | bytes 147480
  5.1 0.7 copy-done.4
  5.8 0.7 copy-done.5
  6.5 0.7 copy-done.6
  7.1 0.7 copy-done.7
  7.8 3.6 %shard_map.95 = (f32[6912,128]{1,0:T(8,128)S(1)}, s32[6,8,128]{2,1,0:T(8,128)S(1)}, s32[6,8,128]{2,1,0:T(8,128)S(1)}, f32[576,128]{1,0:T(8,128)S(1)}, f32[1152,1...) custom-call(f32[12,144,128]{2,1,0:T(8,128)S(1)} %copy-done, f32[2,144,128]{2,1,0:T(8,128)S(1)} %copy-done.3, ...), custom_call_target="tpu_custom_call" | custom-call | flops 884736 | bytes 6404864 | tf_op jit(solution)/shard_map/pallas_call | solution.py:270
  11.4 0.0 collective-permute-done.1.refs_1_
  11.4 6.9 %shard_map.96 = f32[144,4,128]{2,1,0:T(4,128)S(1)} custom-call(f32[1152,128]{1,0:T(8,128)S(1)} %get-tuple-element.12.own.free, f32[2,144,128]{2,1,0:T(8,128)S(1)} %collective-permute-done.refs_0_, f32[2,144,128]{2,1,0:T(8,128)S(1)} %collective-permute-done.1.refs_1_, s32[6,8,128]{2,1,0:T(8,128)S(1)} %get-tuple-element.13.refs_2_.refs_1_, ...), custom_call_target="tpu_custom_call" | custom-call | flops 42467328 | bytes 4767744 | tf_op jit(solution)/shard_map/pallas_call | solution.py:270
  18.3 19.0 %all_to_all.20.blocks = f32[16,9,4,128]{3,2,1,0:T(4,128)S(1)} all-to-all(f32[16,9,4,128]{3,2,1,0:T(4,128)S(1)} %bitcast.12), channel_id=1, replica_groups=mesh['energy'=16,'slab'=2] {'energy'}, dimensions={0} | all-to-all | bytes 589824 | tf_op jit(solution)/shard_map/all_to_all | solution.py:374
  37.3 0.5 shard_map.97
  37.8 13.5 %all_to_all.21 = f32[16,9,4,128]{3,2,1,0:T(4,128)S(1)} all-to-all(f32[16,9,4,128]{3,2,1,0:T(4,128)S(1)} %shard_map.97), channel_id=1, replica_groups=mesh['energy'=16,'slab'=2] {'energy'}, dimensions={0} | all-to-all | bytes 589824 | tf_op jit(solution)/shard_map/all_to_all | solution.py:388
  51.3 0.6 shard_map.98
  51.9 0.1 collective-permute-start.2
  52.0 1.6 %collective-permute-done.2.refs_0_ = f32[144,4,128]{2,1,0:T(4,128)S(1)} collective-permute-done((f32[144,4,128]{2,1,0:T(4,128)S(1)}, f32[144,4,128]{2,1,0:T(4,128)S(1)}, u32[]{:S(2)}, u32[]{:S(2)}) %collective-permute-start.2) | collective-permute-done | bytes 294944 | tf_op jit(solution)/shard_map/ppermute | solution.py:286
  53.6 6.9 %shard_map.99 = f32[144,4,128]{2,1,0:T(4,128)S(1)} custom-call(f32[1152,128]{1,0:T(8,128)S(1)} %get-tuple-element.18.own, f32[144,4,128]{2,1,0:T(4,128)S(1)} %collective-permute-done.2.refs_0_, s32[6,8,128]{2,1,0:T(8,128)S(1)} %get-tuple-element.13.refs_2_.refs_1_, s32[6,8,128]{2,1,0:T(8,128)S(1)} %get-tuple-element.14.refs_3_.refs_2_, ...), custom_call_target="tpu_custom_call" | custom-call | flops 42467328 | bytes 4767744 | tf_op jit(solution)/shard_map/pallas_call | solution.py:270
  60.5 14.2 %all_to_all.22.blocks = f32[16,9,4,128]{3,2,1,0:T(4,128)S(1)} all-to-all(f32[16,9,4,128]{3,2,1,0:T(4,128)S(1)} %bitcast.11), channel_id=1, replica_groups=mesh['energy'=16,'slab'=2] {'energy'}, dimensions={0} | all-to-all | bytes 589824 | tf_op jit(solution)/shard_map/all_to_all | solution.py:374
  74.7 0.5 shard_map.100
  75.2 13.5 %all_to_all.23 = f32[16,9,4,128]{3,2,1,0:T(4,128)S(1)} all-to-all(f32[16,9,4,128]{3,2,1,0:T(4,128)S(1)} %shard_map.100), channel_id=1, replica_groups=mesh['energy'=16,'slab'=2] {'energy'}, dimensions={0} | all-to-all | bytes 589824 | tf_op jit(solution)/shard_map/all_to_all | solution.py:388
  88.7 1.3 %shard_map.101 = (f32[2,144,128]{2,1,0:T(8,128)}, f32[2,144,128]{2,1,0:T(8,128)}) custom-call(f32[144,4,128]{2,1,0:T(4,128)S(1)} %bitcast.16, f32[72,8,128]{2,1,0:T(8,128)S(1)} %bitcast.15, f32[144,8,128]{2,1,0:T(8,128)S(1)} %bitcast.10, f32[2,144,128]{2,1,0:T(8,128)S(1)} %copy-done.1, f32[2,144,128]{2,1,0:T(8,128)S(1)} %copy-done.2), custom_call_target="tpu_custom_call" | custom-call | flops 3538944 | bytes 1769472 | tf_op jit(solution)/shard_map/pallas_call | solution.py:270
  (9 shorter events, 0.0 us)
Async XLA Ops:
  0.6 10.7 %collective-permute-start = (f32[2,144,128]{2,1,0:T(8,128)}, f32[2,144,128]{2,1,0:T(8,128)S(1)}, u32[]{:S(2)}, u32[]{:S(2)}) collective-permute-start(f32[2,144,128]{2,1,0:T(8,128)} %refs_3_.3), channel_id=1, source_target_pairs={{0,1},{1,0},{2,3},{3,2},{4,5},{5,4},{6,7},{7,6},{8,9},{9,8},{10,11... | collective-permute-start | bytes 442376 | tf_op jit(solution)/shard_map/ppermute | solution.py:286
  1.2 10.2 %collective-permute-start.1 = (f32[2,144,128]{2,1,0:T(8,128)}, f32[2,144,128]{2,1,0:T(8,128)S(1)}, u32[]{:S(2)}, u32[]{:S(2)}) collective-permute-start(f32[2,144,128]{2,1,0:T(8,128)} %refs_4_.3), channel_id=1, source_target_pairs={{0,1},{1,0},{2,3},{3,2},{4,5},{5,4},{6,7},{7,6},{8,9},{9,8},{10,11... | collective-permute-start | bytes 442376 | tf_op jit(solution)/shard_map/ppermute | solution.py:286
  1.2 1.2 %copy-start = (f32[12,144,128]{2,1,0:T(8,128)S(1)}, f32[12,144,128]{2,1,0:T(8,128)}, u32[]{:S(2)}) copy-start(f32[12,144,128]{2,1,0:T(8,128)} %refs_0_.1) | copy-start | bytes 2654212
  2.4 0.9 %copy-start.1 = (f32[2,144,128]{2,1,0:T(8,128)S(1)}, f32[2,144,128]{2,1,0:T(8,128)}, u32[]{:S(2)}) copy-start(f32[2,144,128]{2,1,0:T(8,128)} %refs_3_.3) | copy-start | bytes 442372
  3.3 0.9 %copy-start.2 = (f32[2,144,128]{2,1,0:T(8,128)S(1)}, f32[2,144,128]{2,1,0:T(8,128)}, u32[]{:S(2)}) copy-start(f32[2,144,128]{2,1,0:T(8,128)} %refs_4_.3) | copy-start | bytes 442372
  4.2 0.9 %copy-start.3 = (f32[2,144,128]{2,1,0:T(8,128)S(1)}, f32[2,144,128]{2,1,0:T(8,128)}, u32[]{:S(2)}) copy-start(f32[2,144,128]{2,1,0:T(8,128)} %refs_1_.1) | copy-start | bytes 442372
  5.1 0.7 copy-start.4
  5.8 0.7 copy-start.5
  6.5 0.7 copy-start.6
  7.1 0.7 copy-start.7
  51.9 1.6 %collective-permute-start.2 = (f32[144,4,128]{2,1,0:T(4,128)S(1)}, f32[144,4,128]{2,1,0:T(4,128)S(1)}, u32[]{:S(2)}, u32[]{:S(2)}) collective-permute-start(f32[144,4,128]{2,1,0:T(4,128)S(1)} %get-tuple-element.19), channel_id=1, source_target_pairs={{0,1},{1,0},{2,3},{3,2},{4,5},{5,4},{6,7},{7,6},{8,9},{9,8},{10,11... | collective-permute-start | bytes 884744 | tf_op jit(solution)/shard_map/ppermute | solution.py:286

commit v4 on v1

v4 whole, which is shorter than its diff:
```python
import functools

import jax
import jax.numpy as jnp
from jax import lax
from jax.experimental import pallas as pl
from jax.experimental.pallas import tpu as pltpu
from jax.sharding import PartitionSpec as P

NORB = 12
NB = 12
HW = 32
ITERS = 2
ROWS = 8
BLOCKED = 2

TOP_RANK = lax.Precision.HIGHEST
PARAMS = pltpu.CompilerParams(vmem_limit_bytes=24 * 1024 * 1024)
ALONE = pltpu.CompilerParams(vmem_limit_bytes=60 * 1024 * 1024)


def spread_rows(target, base, row, source, first, count):
    for at in range(0, count, ROWS):
        size = min(ROWS, count - at)
        rows = pl.ds((base + at) * ROWS + row, size, stride=ROWS)
        target[rows, :] = source(first + at, size)


def index_neighbours(rows, offsets, lanes, is_near, inside):
    atoms = offsets.shape[1]
    group = ROWS // rows
    slab, slabs = lax.axis_index("slab"), lax.axis_size("slab")
    targets = offsets[...] + lax.broadcasted_iota(jnp.int32, (NB, atoms), 1)
    placed = targets + slab * atoms
    inside[...] = ((placed >= 0) & (placed < slabs * atoms)).astype(jnp.float32)
    near = ((targets >= 0) & (targets < atoms)).astype(jnp.int32)
    lane = jnp.where(targets < 0, targets + atoms, targets)
    lane = jnp.where(lane >= atoms, lane - atoms, lane)
    for n in range(NB):
        some = slice(n % group * rows, (n % group + 1) * rows)
        lanes[n // group, some, :] = jnp.broadcast_to(lane[n : n + 1, :], (rows, atoms))
        is_near[n // group, some, :] = jnp.broadcast_to(near[n : n + 1, :], (rows, atoms))


def couple(rows, own, other, coupling, work, arrived, keep, aside):
    lanes, is_near, inside, links, gathered_a, gathered_b, total = work
    pairs = coupling.shape[1]
    group = ROWS // rows
    groups = NB // group
    steps = NORB // BLOCKED
    chunk = pairs // steps
    buffers = (gathered_a, gathered_b)

    def link(g, pair):
        at = (g * pairs + pair) * ROWS
        if not isinstance(at, int):
            at = pl.multiple_of(at, ROWS)
        return links[pl.ds(at, ROWS), :]

    def build(g, first, count):
        for n in range(g * group, (g + 1) * group):
            valid = inside[n : n + 1, :]
            for row in range(rows):
                spread_rows(
                    links,
                    g * pairs + first,
                    n % group * rows + row,
                    lambda at, size: coupling[n, pl.ds(at, size), :] * valid,
                    first,
                    count,
                )

    def gather(g, first, count):
        target = buffers[g % 2]
        lane, mine = lanes[g], is_near[g] != 0
        for at in range(count):
            pair = first + at
            rows_at = pl.ds(pl.multiple_of(pair * ROWS, ROWS), ROWS)
            inner = jnp.take_along_axis(own[rows_at, :], lane, axis=1, mode="promise_in_bounds")
            outer = jnp.take_along_axis(other[rows_at, :], lane, axis=1, mode="promise_in_bounds")
            target[pair] = jnp.where(mine, inner, outer)

    def ahead(g, step):
        first = pl.multiple_of(step * chunk, ROWS)
        gather(g, first, chunk)
        build(g, first, chunk)

    arrived(0)
    lax.fori_loop(0, steps, lambda step, _: ahead(0, step), None)
    for g in range(groups):
        source = buffers[g % 2]
        if g < groups - 1:
            arrived(g + 1)

        def block_row(step, _):
            first = step * BLOCKED
            inner = [[None] * NORB for _ in range(BLOCKED)]
            for j in range(NORB):
                left = [link(g, (first + b) * NORB + j) for b in range(BLOCKED)]
                for l in range(NORB):
                    value = source[j * NORB + l]
                    for b in range(BLOCKED):
                        term = left[b] * value
                        inner[b][l] = term if j == 0 else inner[b][l] + term
            for k in range(NORB):
                sums = [None] * BLOCKED
                for l in range(NORB):
                    right = link(g, k * NORB + l)
                    for b in range(BLOCKED):
                        term = inner[b][l] * right
                        sums[b] = term if l == 0 else sums[b] + term
                for b in range(BLOCKED):
                    at = (first + b) * NORB + k
                    value = sums[b] if g == 0 else total[at] + sums[b]
                    if g < groups - 1:
                        total[at] = value
                    else:
                        width = ROWS // 2
                        while width >= rows:
                            value = value + pltpu.roll(value, width, 0)
                            width //= 2
                        keep(at, value[:rows])
            if g < groups - 1:
                ahead(g + 1, step)
            else:
                aside(step, steps)

        lax.fori_loop(0, steps, block_row, None)


def first_kernel(*refs):
    far_hbm, free_hbm = refs[0:2], refs[2:4]
    retarded_hbm, coupling_hbm, offsets, shifts, coupled, occupied = refs[4:10]
    out_hbm, start_hbm, left_hbm, right_hbm, mixing_hbm = refs[10:15]
    out, start, left, right, mixing = refs[15:20]
    far, free, retarded, coupling, other = refs[20:25]
    work, (fetched, arriving, leaving, passing) = refs[25:32], refs[32:36]
    energies, pairs, atoms = retarded.shape
    rows = 2 * energies
    group = ROWS // rows
    copies = [pltpu.make_async_copy(free_hbm[f], free.at[f], fetched.at[f]) for f in range(2)]
    copies += [pltpu.make_async_copy(far_hbm[f], far.at[f], fetched.at[2 + f]) for f in range(2)]
    copies.append(pltpu.make_async_copy(retarded_hbm, retarded, fetched.at[4]))
    blocks = [
        pltpu.make_async_copy(coupling_hbm.at[n], coupling.at[n], arriving.at[n])
        for n in range(NB)
    ]
    for copy in copies[:4] + blocks + copies[4:]:
        copy.start()

    index_neighbours(rows, offsets, *work[:3])
    total = mixing.shape[1]
    gap = lax.broadcasted_iota(jnp.int32, (total, total), 1) - lax.broadcasted_iota(
        jnp.int32, (total, total), 0
    )
    lesser = jnp.zeros((total, total), jnp.float32)
    greater = jnp.zeros((total, total), jnp.float32)
    for mode in range(shifts.shape[0]):
        shift = shifts[mode]
        absorb = coupled[mode] * occupied[mode]
        emit = coupled[mode] * (occupied[mode] + 1.0)
        ahead = gap == shift
        behind = gap == -shift
        lesser = lesser + jnp.where(ahead, emit, jnp.where(behind, absorb, 0.0))
        greater = greater + jnp.where(ahead, absorb, jnp.where(behind, emit, 0.0))
    mixing[0] = lesser
    mixing[1] = greater

    for f in range(2):
        copies[f].wait()
        copies[2 + f].wait()
    for row in range(ROWS):
        function, energy = row % rows // energies, row % energies
        for target, sources in ((start, free), (other, far)):
            read = lambda at, size: sources[function, energy, at : at + size, :]
            spread_rows(target, 0, row, read, 0, pairs)
    copies[4].wait()
    share = left.shape[0] // ROWS

    def arrived(g):
        for n in range(g * group, (g + 1) * group):
            blocks[n].wait()

    def keep(at, value):
        out[at] = value

    def aside(step, steps):
        some = pl.ds(step * (pairs // steps), pairs // steps)
        pltpu.make_async_copy(out.at[some], out_hbm.at[some], leaving.at[step]).start()
        for row in range(ROWS):
            for target, count, skipped in (
                (left, share // steps, row // rows * share),
                (right, pairs // steps, 0),
            ):
                first = step * count
                read = lambda at, size: retarded[row % energies, pl.ds(skipped + at, size), :]
                spread_rows(target, first, row, read, first, count)

    couple(rows, start, other, coupling, work, arrived, keep, aside)
    sides = [
        pltpu.make_async_copy(held, target, passing.at[at])
        for at, (held, target) in enumerate(
            ((start, start_hbm), (left, left_hbm), (right, right_hbm), (mixing, mixing_hbm))
        )
    ]
    for side in sides:
        side.start()
    steps = NORB // BLOCKED
    for step in range(steps):
        some = pl.ds(step * (pairs // steps), pairs // steps)
        pltpu.make_async_copy(out.at[some], out_hbm.at[some], leaving.at[step]).wait()
    if out.shape[0] > pairs:
        for at in range(pairs, out.shape[0]):
            out[at] = jnp.zeros(out.shape[1:], jnp.float32)
        some = pl.ds(pairs, out.shape[0] - pairs)
        pltpu.make_async_copy(out.at[some], out_hbm.at[some], leaving.at[0]).start()
        pltpu.make_async_copy(out.at[some], out_hbm.at[some], leaving.at[0]).wait()
    for side in sides:
        side.wait()


def couple_kernel(rows, own, far, coupling, offsets, out, other, *work):
    pairs = coupling.shape[1]
    index_neighbours(rows, offsets, *work[:3])
    for pair in range(pairs):
        value = far[pair]
        for at in range(0, ROWS, rows):
            other[pair * ROWS + at : pair * ROWS + at + rows, :] = value

    def keep(at, value):
        out[at] = value

    couple(rows, own, other, coupling, work, lambda g: None, keep, lambda step, steps: None)
    for at in range(pairs, out.shape[0]):
        out[at] = jnp.zeros(out.shape[1:], jnp.float32)


def mix_kernel(fused, mixing, blocks, out, before, after):
    parts, share, rows, atoms = blocks.shape
    energies = rows // fused
    for f in range(fused):
        some = slice(f * energies, (f + 1) * energies)
        for part in range(parts):
            for pair in range(share):
                before[part * energies : (part + 1) * energies, pair * atoms : (pair + 1) * atoms] = (
                    blocks[part, pair, some, :]
                )
        after[...] = jnp.dot(
            mixing[f], before[...], precision=TOP_RANK, preferred_element_type=jnp.float32
        )
        for part in range(parts):
            for pair in range(share):
                out[part, pair, some, :] = after[
                    part * energies : (part + 1) * energies, pair * atoms : (pair + 1) * atoms
                ]


def dress(rows, sigma, left, right, copied, keep):
    parts = ROWS // rows
    for pair in range(NORB * NORB):
        value = sigma[pair]
        for part in range(parts):
            copied[pair, part * rows : (part + 1) * rows, :] = value
    for i in range(NORB // parts):
        inner = [None] * NORB
        for j in range(NORB):
            factor = left[i * NORB + j]
            for l in range(NORB):
                term = factor * copied[j * NORB + l]
                inner[l] = term if j == 0 else inner[l] + term
        for k in range(NORB):
            value = inner[0] * right[k * NORB]
            for l in range(1, NORB):
                value = value + inner[l] * right[k * NORB + l]
            keep(i * NORB + k, value)


def dress_between_kernel(rows, sigma, left, right, free, own, compact, copied):
    atoms = sigma.shape[2]
    share = left.shape[0]
    row_at = lax.broadcasted_iota(jnp.int32, (ROWS, atoms), 0)

    def keep(at, value):
        for part in range(ROWS // rows):
            held = (row_at >= part * rows) & (row_at < (part + 1) * rows)
            piece = jnp.where(held, value, 0.0)
            width = ROWS // 2
            while width >= rows:
                piece = piece + pltpu.roll(piece, width, 0)
                width //= 2
            pair = part * share + at
            piece = piece + free[pair * ROWS : (pair + 1) * ROWS, :]
            own[pair * ROWS : (pair + 1) * ROWS, :] = piece
            compact[pair] = piece[:rows]

    dress(rows, sigma, left, right, copied, keep)


def dress_last_kernel(*refs):
    sigma, left, right = refs[:3]
    free, out_hbm = refs[3:5], refs[5:7]
    copied, dressed, out, leaving = refs[7:]
    energies, pairs, _ = free[0].shape
    rows = 2 * energies
    parts = ROWS // rows
    share = left.shape[0]
    stage = 2 * NORB
    copies = []

    def keep(at, value):
        dressed[at * ROWS : (at + 1) * ROWS, :] = value
        if (at + 1) % stage and at + 1 < share:
            return
        done = at // stage * stage
        for row in range(ROWS):
            function, energy, part = row % rows // energies, row % energies, row // rows
            for begin in range(done, at + 1, ROWS):
                size = min(ROWS, at + 1 - begin)
                first = part * share + begin
                piece = dressed[pl.ds(begin * ROWS + row, size, stride=ROWS), :]
                out[function, energy, first : first + size, :] = (
                    free[function][energy, first : first + size, :] + piece
                )
        for function in range(2):
            for part in range(parts):
                some = pl.ds(part * share + done, at + 1 - done)
                copies.append(
                    pltpu.make_async_copy(
                        out.at[function, :, some, :],
                        out_hbm[function].at[:, some, :],
                        leaving.at[len(copies)],
                    )
                )
                copies[-1].start()

    dress(rows, sigma, left, right, copied, keep)
    for copy in copies:
        copy.wait()


def call(kernel, outs, scratch, flops, *operands, spaces=None, targets=None, params=PARAMS):
    shapes = [jax.ShapeDtypeStruct(x, jnp.float32) for x in outs]
    vmem = pl.BlockSpec(memory_space=pltpu.VMEM)
    moved = sum(x.size for x in operands) + sum(x.size for x in shapes)
    return pl.pallas_call(
        kernel,
        out_shape=shapes,
        in_specs=spaces or [vmem] * len(operands),
        out_specs=targets or [vmem] * len(shapes),
        scratch_shapes=scratch,
        compiler_params=params,
        cost_estimate=pl.CostEstimate(
            flops=flops, bytes_accessed=4 * moved, transcendentals=0
        ),
    )(*operands)


def beside(block):
    count = lax.axis_size("slab")
    if count == 2:
        return lax.ppermute(block, "slab", [(0, 1), (1, 0)])
    forward = [(i, i + 1) for i in range(count - 1)]
    backward = [(target, source) for source, target in forward]
    axis = block.ndim - 1
    atoms = block.shape[axis]
    low = lax.ppermute(lax.slice_in_dim(block, atoms - HW, atoms, axis=axis), "slab", forward)
    high = lax.ppermute(lax.slice_in_dim(block, 0, HW, axis=axis), "slab", backward)
    gap = jnp.zeros(block.shape[:-1] + (atoms - 2 * HW,), block.dtype)
    return jnp.concatenate([high, gap, low], axis=axis)


def body(
    lesser_free,
    greater_free,
    retarded,
    coupling,
    neighbour_offsets,
    phonon_shift,
    phonon_coupling,
    phonon_occupation,
):
    energies, pairs, atoms = lesser_free.shape
    rows = 2 * energies
    groups = NB * rows // ROWS
    parts = lax.axis_size("energy")
    share = -(-pairs // parts)
    total = energies * parts
    vmem = pl.BlockSpec(memory_space=pltpu.VMEM)
    smem = pl.BlockSpec(memory_space=pltpu.SMEM)
    away = pl.BlockSpec(memory_space=pltpu.HBM)
    held = lambda *dims: pltpu.VMEM(dims, jnp.float32)
    wide = (pairs * ROWS, atoms)
    deep = (pairs, ROWS, atoms)
    thin = (pairs * rows, atoms)
    every = (parts * share, rows, atoms)
    flops = 4 * NORB * rows * pairs * atoms
    index = pltpu.VMEM((groups, ROWS, atoms), jnp.int32)
    work = [index, index, held(NB, atoms), held(groups * pairs * ROWS, atoms)] + [held(*deep)] * 3
    transfer = lambda count: pltpu.SemaphoreType.DMA((count,))

    free = (lesser_free, greater_free)
    coupled, start, left, right, mixing = call(
        first_kernel,
        [every, wide, thin, wide, (2, total, total)],
        [held(*every), held(*wide), held(*thin), held(*wide), held(2, total, total)]
        + [held(2, *retarded.shape), held(2, *retarded.shape), held(*retarded.shape)]
        + [held(*coupling.shape), held(*wide)]
        + work
        + [transfer(5), transfer(NB), transfer(NORB // BLOCKED), transfer(4)],
        NB * flops,
        *(beside(g) for g in free),
        *free,
        retarded,
        coupling,
        neighbour_offsets,
        phonon_shift,
        phonon_coupling,
        phonon_occupation,
        spaces=[away] * 6 + [vmem] + [smem] * 3,
        targets=[away] * 5,
        params=ALONE,
    )
    left = left.reshape(pairs * rows // ROWS, ROWS, atoms)
    right = right.reshape(deep)

    for step in range(ITERS):
        if step > 0:
            own, compact = call(
                functools.partial(dress_between_kernel, rows),
                [wide, (pairs, rows, atoms)],
                [held(*deep)],
                flops,
                sigma,
                left,
                right,
                start,
            )
            (coupled,) = call(
                functools.partial(couple_kernel, rows),
                [every],
                [held(*wide)] + work,
                NB * flops,
                own,
                beside(compact),
                coupling,
                neighbour_offsets,
            )
        gathered = lax.all_to_all(coupled.reshape(parts, share, rows, atoms), "energy", 0, 0)
        (mixed,) = call(
            functools.partial(mix_kernel, 2),
            [gathered.shape],
            [held(total, share * atoms)] * 2,
            2 * total * gathered.size,
            mixing,
            gathered,
        )
        sigma = lax.all_to_all(mixed, "energy", 0, 0).reshape(every)
    stages = -(-thin[0] // (ROWS * 2 * NORB))
    return call(
        dress_last_kernel,
        [lesser_free.shape] * 2,
        [held(*deep), held(*thin), held(2, *lesser_free.shape)]
        + [transfer(stages * 2 * ROWS // rows)],
        flops,
        sigma,
        left,
        right,
        *free,
        targets=[away] * 2,
    )


def solution(mesh):
    placed = (
        P("energy", None, "slab"),
        P("energy", None, "slab"),
        P("energy", None, "slab"),
        P(None, None, "slab"),
        P(None, "slab"),
        P(),
        P(),
        P(),
    )
    return jax.shard_map(
        body,
        mesh=mesh,
        in_specs=placed,
        out_specs=(P("energy", None, "slab"), P("energy", None, "slab")),
        check_vma=False,
    )
```

time: 93.8 us -> 91 us (0.970)
  blocking collectives: 41.3 us -> 60.8 us
  local copies, waits for them, and re-layouts: 11.3 us -> 1.76 us
  starting transfers between devices: 9.5 us -> 0.67 us
  waiting for transfers between devices: 7.51 us -> 3.07 us
  Pallas kernels: 21.8 us -> 23.4 us
    all_to_all x3 -> x4, blocking collectives: 41.3 us -> 60.8 us  [the longest x2 33.6 us: body(): lax.all_to_all(coupled.reshape(parts, share, rows, atoms), 'energy', 0, 0)]
    unnamed x48 -> x22, local copies, waits for them, and re-layouts: 11.3 us -> 1.76 us
    all_to_all x1 -> x0, starting transfers between devices: 8.33 us -> none  [body(): lax.all_to_all(x.reshape(parts, share, rows, atoms), 'energy', 0, 0)]
    all_to_all x1 -> x0, waiting for transfers between devices: 6.44 us -> none  [body(): lax.all_to_all(x.reshape(parts, share, rows, atoms), 'energy', 0, 0)]
    ppermute x4 -> x3, waiting for transfers between devices: 1.08 us -> 3.07 us  [beside(): return lax.ppermute(block, 'slab', [(0, 1), (1, 0)])]
    pallas_call x8 -> x6, Pallas kernels: 21.8 us -> 23.4 us  [call(): pl.pallas_call(kernel, out_shape=shapes, in_specs=spaces or [vmem] * len(...]
  transfers between devices with their start and end apart: 5 -> 3, of which waited for: 3 -> 3; matrix products, arithmetic and copies ran while one was open for 1% -> 0% of each run, Pallas kernels for 2% -> 0%
where the time goes in v4:
time: 91 us; the launch traced here: 90.4 us
  blocking collectives  60.8 us (67%)
  Pallas kernels  23.4 us (26%)
  waiting for transfers between devices  3.07 us (3%)
  local copies, waits for them, and re-layouts  1.76 us (2%)
    all_to_all x2, blocking collectives, body(): lax.all_to_all(coupled.reshape(parts, share, rows, atoms), 'energy', 0, 0)  33.6 us
    all_to_all x2, blocking collectives, body(): sigma = lax.all_to_all(mixed, 'energy', 0, 0).reshape(every)  27.2 us
    pallas_call x6, Pallas kernels, call(): pl.pallas_call(kernel, out_shape=shapes, in_specs=spaces or [vmem] * len(...  23.4 us
    ppermute x3, waiting for transfers between devices, beside(): return lax.ppermute(block, 'slab', [(0, 1), (1, 0)])  3.07 us
  transfers between devices with their start and end apart: 3, of which 3 were waited for; matrix products, arithmetic and copies ran while one was open for 0% of the time, Pallas kernels for 0%

profile of v4, /device:TPU:0, one launch (start us, length us, event | category | flops | bytes accessed | tf_op | source)
XLA Modules:
  0.0 90.4 jit_solution(257418128499927467)
XLA Ops:
  0.6 0.5 collective-permute-start
  1.1 0.1 collective-permute-start.1
  1.2 1.1 %collective-permute-done.refs_0_ = f32[2,144,128]{2,1,0:T(8,128)S(1)} collective-permute-done((f32[2,144,128]{2,1,0:T(8,128)}, f32[2,144,128]{2,1,0:T(8,128)S(1)}, u32[]{:S(2)}, u32[]{:S(2)}) %collective-permute-start) | collective-permute-done | bytes 147488 | tf_op jit(solution)/shard_map/ppermute | solution.py:361
  2.4 0.4 collective-permute-done.1.refs_1_
  2.7 0.3 copy-done.9
  3.0 0.7 copy-done.10
  3.7 12.0 %shard_map.95 = (f32[144,4,128]{2,1,0:T(4,128)}, f32[1152,128]{1,0:T(8,128)}, f32[576,128]{1,0:T(8,128)}, f32[1152,128]{1,0:T(8,128)}, f32[2,32,32]{2,1,0:T(8,128)}) custom-call(f32[2,144,128]{2,1,0:T(8,128)} %copy-done.9, f32[2,144,128]{2,1,0:T(8,128)} %copy-done.10, f32[2,144,128]{2,1,0:T(8,128)} %refs_3_.3, f32[2,144,128]{2,1,0:T(8,128)} %refs_4_.3, ...), custom_call_target="tpu_custom_call" | custom-call | flops 42467328 | bytes 3406592 | tf_op jit(solution)/shard_map/pallas_call | solution.py:345
  15.7 0.0 copy-start.3
  15.8 19.4 %all_to_all.20.blocks = f32[16,9,4,128]{3,2,1,0:T(4,128)S(1)} all-to-all(f32[16,9,4,128]{3,2,1,0:T(4,128)} %bitcast.13), channel_id=1, replica_groups=mesh['energy'=16,'slab'=2] {'energy'}, dimensions={0} | all-to-all | bytes 589824 | tf_op jit(solution)/shard_map/all_to_all | solution.py:448
  35.1 0.8 copy-done.6
  35.9 0.5 shard_map.96
  36.4 13.6 %all_to_all.21 = f32[16,9,4,128]{3,2,1,0:T(4,128)S(1)} all-to-all(f32[16,9,4,128]{3,2,1,0:T(4,128)S(1)} %shard_map.96), channel_id=1, replica_groups=mesh['energy'=16,'slab'=2] {'energy'}, dimensions={0} | all-to-all | bytes 589824 | tf_op jit(solution)/shard_map/all_to_all | solution.py:457
  50.0 0.0 copy-start
  50.0 0.0 copy-start.8
  50.0 0.6 shard_map.97
  50.7 0.1 collective-permute-start.2
  50.7 1.6 %collective-permute-done.2.far = f32[144,4,128]{2,1,0:T(4,128)S(1)} collective-permute-done((f32[144,4,128]{2,1,0:T(4,128)S(1)}, f32[144,4,128]{2,1,0:T(4,128)S(1)}, u32[]{:S(2)}, u32[]{:S(2)}) %collective-permute-start.2) | collective-permute-done | bytes 294944 | tf_op jit(solution)/shard_map/ppermute | solution.py:361
  52.3 8.4 %shard_map.98 = f32[144,4,128]{2,1,0:T(4,128)S(1)} custom-call(f32[1152,128]{1,0:T(8,128)S(1)} %get-tuple-element.14.own, f32[144,4,128]{2,1,0:T(4,128)S(1)} %collective-permute-done.2.far, f32[12,144,128]{2,1,0:T(8,128)S(1)} %copy-done, s32[12,128]{1,0:T(8,128)S(1)} %copy-done.8), custom_call_target="tpu_custom_call" | custom-call | flops 42467328 | bytes 2070528 | tf_op jit(solution)/shard_map/pallas_call | solution.py:345
  60.8 14.2 %all_to_all.22.blocks = f32[16,9,4,128]{3,2,1,0:T(4,128)S(1)} all-to-all(f32[16,9,4,128]{3,2,1,0:T(4,128)S(1)} %bitcast.12), channel_id=1, replica_groups=mesh['energy'=16,'slab'=2] {'energy'}, dimensions={0} | all-to-all | bytes 589824 | tf_op jit(solution)/shard_map/all_to_all | solution.py:448
  75.0 0.5 shard_map.99
  75.5 0.0 copy-start.4
  75.5 0.0 copy-start.5
  75.5 13.6 %all_to_all.23 = f32[16,9,4,128]{3,2,1,0:T(4,128)S(1)} all-to-all(f32[16,9,4,128]{3,2,1,0:T(4,128)S(1)} %shard_map.99), channel_id=1, replica_groups=mesh['energy'=16,'slab'=2] {'energy'}, dimensions={0} | all-to-all | bytes 589824 | tf_op jit(solution)/shard_map/all_to_all | solution.py:457
  89.1 1.3 %shard_map.100 = (f32[2,144,128]{2,1,0:T(8,128)}, f32[2,144,128]{2,1,0:T(8,128)}) custom-call(f32[144,4,128]{2,1,0:T(4,128)S(1)} %bitcast.11, f32[72,8,128]{2,1,0:T(8,128)S(1)} %bitcast.10, f32[144,8,128]{2,1,0:T(8,128)S(1)} %bitcast.7, f32[2,144,128]{2,1,0:T(8,128)S(1)} %copy-done.4, f32[2,144,128]{2,1,0:T(8,128)S(1)} %copy-done.5), custom_call_target="tpu_custom_call" | custom-call | flops 3538944 | bytes 1769472 | tf_op jit(solution)/shard_map/pallas_call | solution.py:345
  (14 shorter events, 0.0 us)
Async XLA Ops:
  0.6 1.7 %collective-permute-start = (f32[2,144,128]{2,1,0:T(8,128)}, f32[2,144,128]{2,1,0:T(8,128)S(1)}, u32[]{:S(2)}, u32[]{:S(2)}) collective-permute-start(f32[2,144,128]{2,1,0:T(8,128)} %refs_3_.3), channel_id=1, source_target_pairs={{0,1},{1,0},{2,3},{3,2},{4,5},{5,4},{6,7},{7,6},{8,9},{9,8},{10,11... | collective-permute-start | bytes 442376 | tf_op jit(solution)/shard_map/ppermute | solution.py:361
  1.1 1.6 %collective-permute-start.1 = (f32[2,144,128]{2,1,0:T(8,128)}, f32[2,144,128]{2,1,0:T(8,128)S(1)}, u32[]{:S(2)}, u32[]{:S(2)}) collective-permute-start(f32[2,144,128]{2,1,0:T(8,128)} %refs_4_.3), channel_id=1, source_target_pairs={{0,1},{1,0},{2,3},{3,2},{4,5},{5,4},{6,7},{7,6},{8,9},{9,8},{10,11... | collective-permute-start | bytes 442376 | tf_op jit(solution)/shard_map/ppermute | solution.py:361
  2.4 0.7 copy-start.9
  3.0 0.7 copy-start.10
  15.7 34.3 %copy-start.3 = (f32[1152,128]{1,0:T(8,128)S(1)}, f32[1152,128]{1,0:T(8,128)}, u32[]{:S(2)}) copy-start(f32[1152,128]{1,0:T(8,128)} %get-tuple-element.13.free) | copy-start | bytes 1769476
  35.1 0.8 copy-start.6
  35.9 14.1 %copy-start.1 = (f32[1152,128]{1,0:T(8,128)S(1)}, f32[1152,128]{1,0:T(8,128)}, u32[]{:S(2)}) copy-start(f32[1152,128]{1,0:T(8,128)} %get-tuple-element.12) | copy-start | bytes 1769476
  36.4 13.6 %copy-start.2 = (f32[576,128]{1,0:T(8,128)S(1)}, f32[576,128]{1,0:T(8,128)}, u32[]{:S(2)}) copy-start(f32[576,128]{1,0:T(8,128)} %get-tuple-element.11) | copy-start | bytes 884740
  50.0 2.3 %copy-start = (f32[12,144,128]{2,1,0:T(8,128)S(1)}, f32[12,144,128]{2,1,0:T(8,128)}, u32[]{:S(2)}) copy-start(f32[12,144,128]{2,1,0:T(8,128)} %coupling.1) | copy-start | bytes 2654212
  50.0 2.3 %copy-start.8 = (s32[12,128]{1,0:T(8,128)S(1)}, s32[12,128]{1,0:T(8,128)}, u32[]{:S(2)}) copy-start(s32[12,128]{1,0:T(8,128)} %offsets.1) | copy-start | bytes 18436
  50.7 1.6 %collective-permute-start.2 = (f32[144,4,128]{2,1,0:T(4,128)S(1)}, f32[144,4,128]{2,1,0:T(4,128)S(1)}, u32[]{:S(2)}, u32[]{:S(2)}) collective-permute-start(f32[144,4,128]{2,1,0:T(4,128)S(1)} %get-tuple-element.15), channel_id=1, source_target_pairs={{0,1},{1,0},{2,3},{3,2},{4,5},{5,4},{6,7},{7,6},{8,9},{9,8},{10,11... | collective-permute-start | bytes 884744 | tf_op jit(solution)/shard_map/ppermute | solution.py:361
  60.7 14.2 %copy-start.7 = (f32[2,32,32]{2,1,0:T(8,128)S(1)}, f32[2,32,32]{2,1,0:T(8,128)}, u32[]{:S(2)}) copy-start(f32[2,32,32]{2,1,0:T(8,128)} %get-tuple-element.9.mixing) | copy-start | bytes 24580
  75.5 13.6 %copy-start.4 = (f32[2,144,128]{2,1,0:T(8,128)S(1)}, f32[2,144,128]{2,1,0:T(8,128)}, u32[]{:S(2)}) copy-start(f32[2,144,128]{2,1,0:T(8,128)} %refs_3_.3) | copy-start | bytes 442372
  75.5 13.6 %copy-start.5 = (f32[2,144,128]{2,1,0:T(8,128)S(1)}, f32[2,144,128]{2,1,0:T(8,128)}, u32[]{:S(2)}) copy-start(f32[2,144,128]{2,1,0:T(8,128)} %refs_4_.3) | copy-start | bytes 442372

commit v5 on v4

--- a/solution.py
+++ b/solution.py
@@ -43,27 +43,27 @@
 
 
 def couple(rows, own, other, coupling, work, arrived, keep, aside):
-    lanes, is_near, inside, links, gathered_a, gathered_b, total = work
+    lanes, is_near, inside, links_a, links_b, gathered_a, gathered_b, total = work
     pairs = coupling.shape[1]
     group = ROWS // rows
     groups = NB // group
     steps = NORB // BLOCKED
     chunk = pairs // steps
-    buffers = (gathered_a, gathered_b)
+    buffers, links = (gathered_a, gathered_b), (links_a, links_b)
 
     def link(g, pair):
-        at = (g * pairs + pair) * ROWS
+        at = pair * ROWS
         if not isinstance(at, int):
             at = pl.multiple_of(at, ROWS)
-        return links[pl.ds(at, ROWS), :]
+        return links[g % 2][pl.ds(at, ROWS), :]
 
     def build(g, first, count):
         for n in range(g * group, (g + 1) * group):
             valid = inside[n : n + 1, :]
             for row in range(rows):
                 spread_rows(
-                    links,
-                    g * pairs + first,
+                    links[g % 2],
+                    first,
                     n % group * rows + row,
                     lambda at, size: coupling[n, pl.ds(at, size), :] * valid,
                     first,
@@ -128,27 +128,23 @@
         lax.fori_loop(0, steps, block_row, None)
 
 
-def first_kernel(*refs):
-    far_hbm, free_hbm = refs[0:2], refs[2:4]
-    retarded_hbm, coupling_hbm, offsets, shifts, coupled, occupied = refs[4:10]
-    out_hbm, start_hbm, left_hbm, right_hbm, mixing_hbm = refs[10:15]
-    out, start, left, right, mixing = refs[15:20]
-    far, free, retarded, coupling, other = refs[20:25]
-    work, (fetched, arriving, leaving, passing) = refs[25:32], refs[32:36]
-    energies, pairs, atoms = retarded.shape
+def prep_kernel(*refs):
+    free_hbm, retarded_hbm, shifts, coupled, occupied = refs[0:2], *refs[2:6]
+    targets = refs[6:10]
+    start, left, right, mixing = refs[10:14]
+    free, retarded, fetched, passing = refs[14:18]
+    energies, pairs, _ = retarded.shape
     rows = 2 * energies
-    group = ROWS // rows
+    share = left.shape[0] // ROWS
     copies = [pltpu.make_async_copy(free_hbm[f], free.at[f], fetched.at[f]) for f in range(2)]
-    copies += [pltpu.make_async_copy(far_hbm[f], far.at[f], fetched.at[2 + f]) for f in range(2)]
-    copies.append(pltpu.make_async_copy(retarded_hbm, retarded, fetched.at[4]))
-    blocks = [
-        pltpu.make_async_copy(coupling_hbm.at[n], coupling.at[n], arriving.at[n])
-        for n in range(NB)
+    copies.append(pltpu.make_async_copy(retarded_hbm, retarded, fetched.at[2]))
+    for copy in copies:
+        copy.start()
+    sides = [
+        pltpu.make_async_copy(held, target, passing.at[at])
+        for at, (held, target) in enumerate(zip((start, left, right, mixing), targets))
     ]
-    for copy in copies[:4] + blocks + copies[4:]:
-        copy.start()
-
-    index_neighbours(rows, offsets, *work[:3])
+
     total = mixing.shape[1]
     gap = lax.broadcasted_iota(jnp.int32, (total, total), 1) - lax.broadcasted_iota(
         jnp.int32, (total, total), 0
@@ -165,17 +161,50 @@
         greater = greater + jnp.where(ahead, absorb, jnp.where(behind, emit, 0.0))
     mixing[0] = lesser
     mixing[1] = greater
-
-    for f in range(2):
-        copies[f].wait()
-        copies[2 + f].wait()
+    sides[3].start()
+
+    copies[0].wait()
+    copies[1].wait()
     for row in range(ROWS):
         function, energy = row % rows // energies, row % energies
-        for target, sources in ((start, free), (other, far)):
-            read = lambda at, size: sources[function, energy, at : at + size, :]
-            spread_rows(target, 0, row, read, 0, pairs)
-    copies[4].wait()
-    share = left.shape[0] // ROWS
+        read = lambda at, size: free[function, energy, at : at + size, :]
+        spread_rows(start, 0, row, read, 0, pairs)
+    sides[0].start()
+    copies[2].wait()
+    for row in range(ROWS):
+        skipped = row // rows * share
+        read = lambda at, size: retarded[row % energies, at : at + size, :]
+        spread_rows(left, 0, row, read, skipped, share)
+        spread_rows(right, 0, row, read, 0, pairs)
+    sides[1].start()
+    sides[2].start()
+    for side in sides:
+        side.wait()
+
+
+def first_kernel(*refs):
+    far_hbm, own_hbm, coupling_hbm, offsets, out_hbm = refs[0:2], *refs[2:6]
+    out, own, far, coupling, other = refs[6:11]
+    work, (fetched, arriving, leaving) = refs[11:19], refs[19:22]
+    energies, pairs = far.shape[1:3]
+    rows = 2 * energies
+    group = ROWS // rows
+    copies = [pltpu.make_async_copy(far_hbm[f], far.at[f], fetched.at[f]) for f in range(2)]
+    copies.append(pltpu.make_async_copy(own_hbm, own, fetched.at[2]))
+    blocks = [
+        pltpu.make_async_copy(coupling_hbm.at[n], coupling.at[n], arriving.at[n])
+        for n in range(NB)
+    ]
+    for copy in copies + blocks:
+        copy.start()
+    index_neighbours(rows, offsets, *work[:3])
+    for copy in copies[:2]:
+        copy.wait()
+    for row in range(ROWS):
+        function, energy = row % rows // energies, row % energies
+        read = lambda at, size: far[function, energy, at : at + size, :]
+        spread_rows(other, 0, row, read, 0, pairs)
+    copies[2].wait()
 
     def arrived(g):
         for n in range(g * group, (g + 1) * group):
@@ -184,39 +213,23 @@
     def keep(at, value):
         out[at] = value
 
-    def aside(step, steps):
+    def leave(step, steps):
         some = pl.ds(step * (pairs // steps), pairs // steps)
-        pltpu.make_async_copy(out.at[some], out_hbm.at[some], leaving.at[step]).start()
-        for row in range(ROWS):
-            for target, count, skipped in (
-                (left, share // steps, row // rows * share),
-                (right, pairs // steps, 0),
-            ):
-                first = step * count
-                read = lambda at, size: retarded[row % energies, pl.ds(skipped + at, size), :]
-                spread_rows(target, first, row, read, first, count)
-
-    couple(rows, start, other, coupling, work, arrived, keep, aside)
-    sides = [
-        pltpu.make_async_copy(held, target, passing.at[at])
-        for at, (held, target) in enumerate(
-            ((start, start_hbm), (left, left_hbm), (right, right_hbm), (mixing, mixing_hbm))
-        )
-    ]
-    for side in sides:
-        side.start()
+        return pltpu.make_async_copy(out.at[some], out_hbm.at[some], leaving.at[step])
+
+    couple(
+        rows, own, other, coupling, work, arrived, keep, lambda step, steps: leave(step, steps).start()
+    )
     steps = NORB // BLOCKED
-    for step in range(steps):
-        some = pl.ds(step * (pairs // steps), pairs // steps)
-        pltpu.make_async_copy(out.at[some], out_hbm.at[some], leaving.at[step]).wait()
     if out.shape[0] > pairs:
         for at in range(pairs, out.shape[0]):
             out[at] = jnp.zeros(out.shape[1:], jnp.float32)
         some = pl.ds(pairs, out.shape[0] - pairs)
-        pltpu.make_async_copy(out.at[some], out_hbm.at[some], leaving.at[0]).start()
-        pltpu.make_async_copy(out.at[some], out_hbm.at[some], leaving.at[0]).wait()
-    for side in sides:
-        side.wait()
+        rest = pltpu.make_async_copy(out.at[some], out_hbm.at[some], leaving.at[steps])
+        rest.start()
+        rest.wait()
+    for step in range(steps):
+        leave(step, steps).wait()
 
 
 def couple_kernel(rows, own, far, coupling, offsets, out, other, *work):
@@ -395,29 +408,39 @@
     every = (parts * share, rows, atoms)
     flops = 4 * NORB * rows * pairs * atoms
     index = pltpu.VMEM((groups, ROWS, atoms), jnp.int32)
-    work = [index, index, held(NB, atoms), held(groups * pairs * ROWS, atoms)] + [held(*deep)] * 3
+    work = [index, index, held(NB, atoms)] + [held(*wide)] * 2 + [held(*deep)] * 3
     transfer = lambda count: pltpu.SemaphoreType.DMA((count,))
 
     free = (lesser_free, greater_free)
-    coupled, start, left, right, mixing = call(
-        first_kernel,
-        [every, wide, thin, wide, (2, total, total)],
-        [held(*every), held(*wide), held(*thin), held(*wide), held(2, total, total)]
-        + [held(2, *retarded.shape), held(2, *retarded.shape), held(*retarded.shape)]
-        + [held(*coupling.shape), held(*wide)]
-        + work
-        + [transfer(5), transfer(NB), transfer(NORB // BLOCKED), transfer(4)],
-        NB * flops,
-        *(beside(g) for g in free),
+    halos = [beside(g) for g in free]
+    start, left, right, mixing = call(
+        prep_kernel,
+        [wide, thin, wide, (2, total, total)],
+        [held(*wide), held(*thin), held(*wide), held(2, total, total)]
+        + [held(2, *retarded.shape), held(*retarded.shape), transfer(3), transfer(4)],
+        4 * ROWS * retarded.size,
         *free,
         retarded,
-        coupling,
-        neighbour_offsets,
         phonon_shift,
         phonon_coupling,
         phonon_occupation,
-        spaces=[away] * 6 + [vmem] + [smem] * 3,
-        targets=[away] * 5,
+        spaces=[away] * 3 + [smem] * 3,
+        targets=[away] * 4,
+        params=ALONE,
+    )
+    (coupled,) = call(
+        first_kernel,
+        [every],
+        [held(*every), held(*wide), held(2, *retarded.shape), held(*coupling.shape), held(*wide)]
+        + work
+        + [transfer(3), transfer(NB), transfer(NORB // BLOCKED + 1)],
+        NB * flops,
+        *halos,
+        start,
+        coupling,
+        neighbour_offsets,
+        spaces=[pl.BlockSpec(memory_space=pl.ANY)] * 2 + [away] * 2 + [vmem],
+        targets=[away],
         params=ALONE,
     )
     left = left.reshape(pairs * rows // ROWS, ROWS, atoms)

time: 91 us -> 88.1 us (0.968)
  waiting for transfers between devices: 3.07 us -> 1.57 us
  local copies, waits for them, and re-layouts: 1.76 us -> 0.73 us
    ppermute x3, waiting for transfers between devices: 3.07 us -> 1.57 us  [beside(): return lax.ppermute(block, 'slab', [(0, 1), (1, 0)])]
    unnamed x22 -> x20, local copies, waits for them, and re-layouts: 1.76 us -> 0.73 us
    pallas_call x6 -> x7, Pallas kernels: 23.4 us -> 23.2 us  [call(): pl.pallas_call(kernel, out_shape=shapes, in_specs=spaces or [vmem] * len(...]
  transfers between devices with their start and end apart: 3 -> 3, of which waited for: 3 -> 1; matrix products, arithmetic and copies ran while one was open for 0% -> 0% of each run, Pallas kernels for 0% -> 3%
where the time goes in v5:
time: 88.1 us; the launch traced here: 87.6 us
  blocking collectives  60.6 us (69%)
  Pallas kernels  23.2 us (26%)
  waiting for transfers between devices  1.57 us (2%)
    all_to_all x2, blocking collectives, body(): lax.all_to_all(coupled.reshape(parts, share, rows, atoms), 'energy', 0, 0)  33.6 us
    all_to_all x2, blocking collectives, body(): sigma = lax.all_to_all(mixed, 'energy', 0, 0).reshape(every)  27.1 us
    pallas_call x7, Pallas kernels, call(): pl.pallas_call(kernel, out_shape=shapes, in_specs=spaces or [vmem] * len(...  23.2 us
  transfers between devices with their start and end apart: 3, of which 1 were waited for; matrix products, arithmetic and copies ran while one was open for 0% of the time, Pallas kernels for 3%

profile of v5, /device:TPU:0, one launch (start us, length us, event | category | flops | bytes accessed | tf_op | source)
XLA Modules:
  0.0 87.6 jit_solution(16863703614158189664)
XLA Ops:
  0.6 0.5 collective-permute-start
  1.1 0.1 collective-permute-start.1
  1.2 2.9 %shard_map.95 = (f32[1152,128]{1,0:T(8,128)}, f32[576,128]{1,0:T(8,128)}, f32[1152,128]{1,0:T(8,128)}, f32[2,32,32]{2,1,0:T(8,128)}) custom-call(f32[2,144,128]{2,1,0:T(8,128)} %refs_3_.5, f32[2,144,128]{2,1,0:T(8,128)} %refs_4_.5, f32[2,144,128]{2,1,0:T(8,128)} %refs_2_.1, s32[64]{0:T(128)} %refs_3_.3, f32[64]{0:T(128)} %refs_4_.3, f32[64]{0:T(128)} %refs_5_.1), custom_call_target="tpu_custom_call" | custom-call | flops 1179648 | bytes 1925888 | tf_op jit(solution)/shard_map/pallas_call | solution.py:358
  4.2 0.0 copy-start.8
  4.2 0.0 collective-permute-done.1.refs_1_
  4.2 0.0 copy-start.9
  4.2 0.6 copy-done.8
  4.9 0.0 copy-done.9
  4.9 10.1 %shard_map.96 = f32[144,4,128]{2,1,0:T(4,128)} custom-call(f32[2,144,128]{2,1,0:T(8,128)} %copy-done.8, f32[2,144,128]{2,1,0:T(8,128)} %copy-done.9, f32[1152,128]{1,0:T(8,128)} %get-tuple-element.9.refs_2_.free, f32[12,144,128]{2,1,0:T(8,128)} %coupling.1, s32[12,128]{1,0:T(8,128)} %offsets.1), custom_call_target="tpu_custom_call" | custom-call | flops 42467328 | bytes 2070528 | tf_op jit(solution)/shard_map/pallas_call | solution.py:358
  15.0 19.4 %all_to_all.20.blocks = f32[16,9,4,128]{3,2,1,0:T(4,128)S(1)} all-to-all(f32[16,9,4,128]{3,2,1,0:T(4,128)} %bitcast.13), channel_id=1, replica_groups=mesh['energy'=16,'slab'=2] {'energy'}, dimensions={0} | all-to-all | bytes 589824 | tf_op jit(solution)/shard_map/all_to_all | solution.py:471
  34.4 0.5 shard_map.97
  34.9 13.5 %all_to_all.21 = f32[16,9,4,128]{3,2,1,0:T(4,128)S(1)} all-to-all(f32[16,9,4,128]{3,2,1,0:T(4,128)S(1)} %shard_map.97), channel_id=1, replica_groups=mesh['energy'=16,'slab'=2] {'energy'}, dimensions={0} | all-to-all | bytes 589824 | tf_op jit(solution)/shard_map/all_to_all | solution.py:480
  48.4 0.0 copy-start
  48.4 0.0 copy-start.7
  48.4 0.6 shard_map.98
  49.0 0.1 collective-permute-start.2
  49.1 1.6 %collective-permute-done.2.far = f32[144,4,128]{2,1,0:T(4,128)S(1)} collective-permute-done((f32[144,4,128]{2,1,0:T(4,128)S(1)}, f32[144,4,128]{2,1,0:T(4,128)S(1)}, u32[]{:S(2)}, u32[]{:S(2)}) %collective-permute-start.2) | collective-permute-done | bytes 294944 | tf_op jit(solution)/shard_map/ppermute | solution.py:374
  50.7 7.3 %shard_map.99 = f32[144,4,128]{2,1,0:T(4,128)S(1)} custom-call(f32[1152,128]{1,0:T(8,128)S(1)} %get-tuple-element.12.own, f32[144,4,128]{2,1,0:T(4,128)S(1)} %collective-permute-done.2.far, f32[12,144,128]{2,1,0:T(8,128)S(1)} %copy-done, s32[12,128]{1,0:T(8,128)S(1)} %copy-done.7), custom_call_target="tpu_custom_call" | custom-call | flops 42467328 | bytes 2070528 | tf_op jit(solution)/shard_map/pallas_call | solution.py:358
  58.0 14.2 %all_to_all.22.blocks = f32[16,9,4,128]{3,2,1,0:T(4,128)S(1)} all-to-all(f32[16,9,4,128]{3,2,1,0:T(4,128)S(1)} %bitcast.12), channel_id=1, replica_groups=mesh['energy'=16,'slab'=2] {'energy'}, dimensions={0} | all-to-all | bytes 589824 | tf_op jit(solution)/shard_map/all_to_all | solution.py:471
  72.2 0.5 shard_map.100
  72.7 0.0 copy-start.4
  72.7 0.0 copy-start.5
  72.7 13.6 %all_to_all.23 = f32[16,9,4,128]{3,2,1,0:T(4,128)S(1)} all-to-all(f32[16,9,4,128]{3,2,1,0:T(4,128)S(1)} %shard_map.100), channel_id=1, replica_groups=mesh['energy'=16,'slab'=2] {'energy'}, dimensions={0} | all-to-all | bytes 589824 | tf_op jit(solution)/shard_map/all_to_all | solution.py:480
  86.3 1.3 %shard_map.101 = (f32[2,144,128]{2,1,0:T(8,128)}, f32[2,144,128]{2,1,0:T(8,128)}) custom-call(f32[144,4,128]{2,1,0:T(4,128)S(1)} %bitcast.11, f32[72,8,128]{2,1,0:T(8,128)S(1)} %bitcast.10, f32[144,8,128]{2,1,0:T(8,128)S(1)} %bitcast.7, f32[2,144,128]{2,1,0:T(8,128)S(1)} %copy-done.4, f32[2,144,128]{2,1,0:T(8,128)S(1)} %copy-done.5), custom_call_target="tpu_custom_call" | custom-call | flops 3538944 | bytes 1769472 | tf_op jit(solution)/shard_map/pallas_call | solution.py:358
  (13 shorter events, 0.0 us)
Async XLA Ops:
  0.6 3.6 %collective-permute-start = (f32[2,144,128]{2,1,0:T(8,128)}, f32[2,144,128]{2,1,0:T(8,128)S(1)}, u32[]{:S(2)}, u32[]{:S(2)}) collective-permute-start(f32[2,144,128]{2,1,0:T(8,128)} %refs_3_.5), channel_id=1, source_target_pairs={{0,1},{1,0},{2,3},{3,2},{4,5},{5,4},{6,7},{7,6},{8,9},{9,8},{10,11... | collective-permute-start | bytes 442376 | tf_op jit(solution)/shard_map/ppermute | solution.py:374
  1.1 3.1 %collective-permute-start.1 = (f32[2,144,128]{2,1,0:T(8,128)}, f32[2,144,128]{2,1,0:T(8,128)S(1)}, u32[]{:S(2)}, u32[]{:S(2)}) collective-permute-start(f32[2,144,128]{2,1,0:T(8,128)} %refs_4_.5), channel_id=1, source_target_pairs={{0,1},{1,0},{2,3},{3,2},{4,5},{5,4},{6,7},{7,6},{8,9},{9,8},{10,11... | collective-permute-start | bytes 442376 | tf_op jit(solution)/shard_map/ppermute | solution.py:374
  4.2 0.7 copy-start.8
  4.2 0.7 copy-start.9
  15.0 19.4 %copy-start.6 = (f32[2,32,32]{2,1,0:T(8,128)S(1)}, f32[2,32,32]{2,1,0:T(8,128)}, u32[]{:S(2)}) copy-start(f32[2,32,32]{2,1,0:T(8,128)} %get-tuple-element.8.mixing) | copy-start | bytes 24580
  15.0 33.4 %copy-start.3 = (f32[576,128]{1,0:T(8,128)S(1)}, f32[576,128]{1,0:T(8,128)}, u32[]{:S(2)}) copy-start(f32[576,128]{1,0:T(8,128)} %get-tuple-element.10) | copy-start | bytes 884740
  34.4 14.0 %copy-start.1 = (f32[1152,128]{1,0:T(8,128)S(1)}, f32[1152,128]{1,0:T(8,128)}, u32[]{:S(2)}) copy-start(f32[1152,128]{1,0:T(8,128)} %get-tuple-element.11) | copy-start | bytes 1769476
  34.4 14.0 %copy-start.2 = (f32[1152,128]{1,0:T(8,128)S(1)}, f32[1152,128]{1,0:T(8,128)}, u32[]{:S(2)}) copy-start(f32[1152,128]{1,0:T(8,128)} %get-tuple-element.9.refs_2_.free) | copy-start | bytes 1769476
  48.4 2.3 %copy-start = (f32[12,144,128]{2,1,0:T(8,128)S(1)}, f32[12,144,128]{2,1,0:T(8,128)}, u32[]{:S(2)}) copy-start(f32[12,144,128]{2,1,0:T(8,128)} %coupling.1) | copy-start | bytes 2654212
  48.4 2.3 %copy-start.7 = (s32[12,128]{1,0:T(8,128)S(1)}, s32[12,128]{1,0:T(8,128)}, u32[]{:S(2)}) copy-start(s32[12,128]{1,0:T(8,128)} %offsets.1) | copy-start | bytes 18436
  49.0 1.6 %collective-permute-start.2 = (f32[144,4,128]{2,1,0:T(4,128)S(1)}, f32[144,4,128]{2,1,0:T(4,128)S(1)}, u32[]{:S(2)}, u32[]{:S(2)}) collective-permute-start(f32[144,4,128]{2,1,0:T(4,128)S(1)} %get-tuple-element.13), channel_id=1, source_target_pairs={{0,1},{1,0},{2,3},{3,2},{4,5},{5,4},{6,7},{7,6},{8,9},{9,8},{10,11... | collective-permute-start | bytes 884744 | tf_op jit(solution)/shard_map/ppermute | solution.py:374
  72.7 13.6 %copy-start.4 = (f32[2,144,128]{2,1,0:T(8,128)S(1)}, f32[2,144,128]{2,1,0:T(8,128)}, u32[]{:S(2)}) copy-start(f32[2,144,128]{2,1,0:T(8,128)} %refs_3_.5) | copy-start | bytes 442372
  72.7 13.6 %copy-start.5 = (f32[2,144,128]{2,1,0:T(8,128)S(1)}, f32[2,144,128]{2,1,0:T(8,128)}, u32[]{:S(2)}) copy-start(f32[2,144,128]{2,1,0:T(8,128)} %refs_4_.5) | copy-start | bytes 442372

commit v6 on v5

--- a/solution.py
+++ b/solution.py
@@ -16,7 +16,6 @@
 
 TOP_RANK = lax.Precision.HIGHEST
 PARAMS = pltpu.CompilerParams(vmem_limit_bytes=24 * 1024 * 1024)
-ALONE = pltpu.CompilerParams(vmem_limit_bytes=60 * 1024 * 1024)
 
 
 def spread_rows(target, base, row, source, first, count):
@@ -42,7 +41,7 @@
         is_near[n // group, some, :] = jnp.broadcast_to(near[n : n + 1, :], (rows, atoms))
 
 
-def couple(rows, own, other, coupling, work, arrived, keep, aside):
+def couple(rows, own, other, coupling, work, keep):
     lanes, is_near, inside, links_a, links_b, gathered_a, gathered_b, total = work
     pairs = coupling.shape[1]
     group = ROWS // rows
@@ -85,12 +84,9 @@
         gather(g, first, chunk)
         build(g, first, chunk)
 
-    arrived(0)
     lax.fori_loop(0, steps, lambda step, _: ahead(0, step), None)
     for g in range(groups):
         source = buffers[g % 2]
-        if g < groups - 1:
-            arrived(g + 1)
 
         def block_row(step, _):
             first = step * BLOCKED
@@ -122,29 +118,40 @@
                         keep(at, value[:rows])
             if g < groups - 1:
                 ahead(g + 1, step)
-            else:
-                aside(step, steps)
 
         lax.fori_loop(0, steps, block_row, None)
 
 
 def prep_kernel(*refs):
-    free_hbm, retarded_hbm, shifts, coupled, occupied = refs[0:2], *refs[2:6]
-    targets = refs[6:10]
-    start, left, right, mixing = refs[10:14]
-    free, retarded, fetched, passing = refs[14:18]
+    free_hbm, retarded_hbm, modes_hbm, coupling_hbm = refs[0:2], refs[2], refs[3:6], refs[6]
+    start, left, right, mixing, coupling = refs[7:12]
+    free, retarded, shifts, coupled, occupied, sems = refs[12:]
     energies, pairs, _ = retarded.shape
     rows = 2 * energies
     share = left.shape[0] // ROWS
-    copies = [pltpu.make_async_copy(free_hbm[f], free.at[f], fetched.at[f]) for f in range(2)]
-    copies.append(pltpu.make_async_copy(retarded_hbm, retarded, fetched.at[2]))
+    moves = [(free_hbm[f], free.at[f]) for f in range(2)] + [(retarded_hbm, retarded)]
+    moves += list(zip(modes_hbm, (shifts, coupled, occupied))) + [(coupling_hbm, coupling)]
+    copies = [
+        pltpu.make_async_copy(source, target, sems.at[at])
+        for at, (source, target) in enumerate(moves)
+    ]
     for copy in copies:
         copy.start()
-    sides = [
-        pltpu.make_async_copy(held, target, passing.at[at])
-        for at, (held, target) in enumerate(zip((start, left, right, mixing), targets))
-    ]
-
+
+    copies[0].wait()
+    copies[1].wait()
+    for row in range(ROWS):
+        function, energy = row % rows // energies, row % energies
+        read = lambda at, size: free[function, energy, at : at + size, :]
+        spread_rows(start, 0, row, read, 0, pairs)
+    copies[2].wait()
+    for row in range(ROWS):
+        skipped = row // rows * share
+        read = lambda at, size: retarded[row % energies, at : at + size, :]
+        spread_rows(left, 0, row, read, skipped, share)
+        spread_rows(right, 0, row, read, 0, pairs)
+    for copy in copies[3:6]:
+        copy.wait()
     total = mixing.shape[1]
     gap = lax.broadcasted_iota(jnp.int32, (total, total), 1) - lax.broadcasted_iota(
         jnp.int32, (total, total), 0
@@ -161,89 +168,29 @@
         greater = greater + jnp.where(ahead, absorb, jnp.where(behind, emit, 0.0))
     mixing[0] = lesser
     mixing[1] = greater
-    sides[3].start()
-
-    copies[0].wait()
-    copies[1].wait()
-    for row in range(ROWS):
-        function, energy = row % rows // energies, row % energies
-        read = lambda at, size: free[function, energy, at : at + size, :]
-        spread_rows(start, 0, row, read, 0, pairs)
-    sides[0].start()
-    copies[2].wait()
-    for row in range(ROWS):
-        skipped = row // rows * share
-        read = lambda at, size: retarded[row % energies, at : at + size, :]
-        spread_rows(left, 0, row, read, skipped, share)
-        spread_rows(right, 0, row, read, 0, pairs)
-    sides[1].start()
-    sides[2].start()
-    for side in sides:
-        side.wait()
-
-
-def first_kernel(*refs):
-    far_hbm, own_hbm, coupling_hbm, offsets, out_hbm = refs[0:2], *refs[2:6]
-    out, own, far, coupling, other = refs[6:11]
-    work, (fetched, arriving, leaving) = refs[11:19], refs[19:22]
-    energies, pairs = far.shape[1:3]
-    rows = 2 * energies
-    group = ROWS // rows
-    copies = [pltpu.make_async_copy(far_hbm[f], far.at[f], fetched.at[f]) for f in range(2)]
-    copies.append(pltpu.make_async_copy(own_hbm, own, fetched.at[2]))
-    blocks = [
-        pltpu.make_async_copy(coupling_hbm.at[n], coupling.at[n], arriving.at[n])
-        for n in range(NB)
-    ]
-    for copy in copies + blocks:
-        copy.start()
+    copies[6].wait()
+
+
+def couple_kernel(rows, own, *refs):
+    far, (coupling, offsets, out, other, *work) = refs[:-12], refs[-12:]
+    pairs = coupling.shape[1]
     index_neighbours(rows, offsets, *work[:3])
-    for copy in copies[:2]:
-        copy.wait()
-    for row in range(ROWS):
-        function, energy = row % rows // energies, row % energies
-        read = lambda at, size: far[function, energy, at : at + size, :]
-        spread_rows(other, 0, row, read, 0, pairs)
-    copies[2].wait()
-
-    def arrived(g):
-        for n in range(g * group, (g + 1) * group):
-            blocks[n].wait()
+    if len(far) == 1:
+        for pair in range(pairs):
+            value = far[0][pair]
+            for at in range(0, ROWS, rows):
+                other[pair * ROWS + at : pair * ROWS + at + rows, :] = value
+    else:
+        energies = rows // len(far)
+        for row in range(ROWS):
+            source = far[row % rows // energies]
+            read = lambda at, size: source[row % energies, at : at + size, :]
+            spread_rows(other, 0, row, read, 0, pairs)
 
     def keep(at, value):
         out[at] = value
 
-    def leave(step, steps):
-        some = pl.ds(step * (pairs // steps), pairs // steps)
-        return pltpu.make_async_copy(out.at[some], out_hbm.at[some], leaving.at[step])
-
-    couple(
-        rows, own, other, coupling, work, arrived, keep, lambda step, steps: leave(step, steps).start()
-    )
-    steps = NORB // BLOCKED
-    if out.shape[0] > pairs:
-        for at in range(pairs, out.shape[0]):
-            out[at] = jnp.zeros(out.shape[1:], jnp.float32)
-        some = pl.ds(pairs, out.shape[0] - pairs)
-        rest = pltpu.make_async_copy(out.at[some], out_hbm.at[some], leaving.at[steps])
-        rest.start()
-        rest.wait()
-    for step in range(steps):
-        leave(step, steps).wait()
-
-
-def couple_kernel(rows, own, far, coupling, offsets, out, other, *work):
-    pairs = coupling.shape[1]
-    index_neighbours(rows, offsets, *work[:3])
-    for pair in range(pairs):
-        value = far[pair]
-        for at in range(0, ROWS, rows):
-            other[pair * ROWS + at : pair * ROWS + at + rows, :] = value
-
-    def keep(at, value):
-        out[at] = value
-
-    couple(rows, own, other, coupling, work, lambda g: None, keep, lambda step, steps: None)
+    couple(rows, own, other, coupling, work, keep)
     for at in range(pairs, out.shape[0]):
         out[at] = jnp.zeros(out.shape[1:], jnp.float32)
 
@@ -351,7 +298,7 @@
         copy.wait()
 
 
-def call(kernel, outs, scratch, flops, *operands, spaces=None, targets=None, params=PARAMS):
+def call(kernel, outs, scratch, flops, *operands, spaces=None, targets=None):
     shapes = [jax.ShapeDtypeStruct(x, jnp.float32) for x in outs]
     vmem = pl.BlockSpec(memory_space=pltpu.VMEM)
     moved = sum(x.size for x in operands) + sum(x.size for x in shapes)
@@ -361,7 +308,7 @@
         in_specs=spaces or [vmem] * len(operands),
         out_specs=targets or [vmem] * len(shapes),
         scratch_shapes=scratch,
-        compiler_params=params,
+        compiler_params=PARAMS,
         cost_estimate=pl.CostEstimate(
             flops=flops, bytes_accessed=4 * moved, transcendentals=0
         ),
@@ -398,8 +345,6 @@
     parts = lax.axis_size("energy")
     share = -(-pairs // parts)
     total = energies * parts
-    vmem = pl.BlockSpec(memory_space=pltpu.VMEM)
-    smem = pl.BlockSpec(memory_space=pltpu.SMEM)
     away = pl.BlockSpec(memory_space=pltpu.HBM)
     held = lambda *dims: pltpu.VMEM(dims, jnp.float32)
     wide = (pairs * ROWS, atoms)
@@ -413,36 +358,21 @@
 
     free = (lesser_free, greater_free)
     halos = [beside(g) for g in free]
-    start, left, right, mixing = call(
+    phonons = (phonon_shift, phonon_coupling, phonon_occupation)
+    own, left, right, mixing, links = call(
         prep_kernel,
-        [wide, thin, wide, (2, total, total)],
-        [held(*wide), held(*thin), held(*wide), held(2, total, total)]
-        + [held(2, *retarded.shape), held(*retarded.shape), transfer(3), transfer(4)],
+        [wide, thin, wide, (2, total, total), coupling.shape],
+        [held(2, *retarded.shape), held(*retarded.shape)]
+        + [pltpu.SMEM(x.shape, x.dtype) for x in phonons]
+        + [transfer(7)],
         4 * ROWS * retarded.size,
-        *free,
-        retarded,
-        phonon_shift,
-        phonon_coupling,
-        phonon_occupation,
-        spaces=[away] * 3 + [smem] * 3,
-        targets=[away] * 4,
-        params=ALONE,
+        *(
+            pltpu.with_memory_space_constraint(x, pltpu.HBM)
+            for x in (*free, retarded, *phonons, coupling)
+        ),
+        spaces=[away] * 7,
     )
-    (coupled,) = call(
-        first_kernel,
-        [every],
-        [held(*every), held(*wide), held(2, *retarded.shape), held(*coupling.shape), held(*wide)]
-        + work
-        + [transfer(3), transfer(NB), transfer(NORB // BLOCKED + 1)],
-        NB * flops,
-        *halos,
-        start,
-        coupling,
-        neighbour_offsets,
-        spaces=[pl.BlockSpec(memory_space=pl.ANY)] * 2 + [away] * 2 + [vmem],
-        targets=[away],
-        params=ALONE,
-    )
+    start = own
     left = left.reshape(pairs * rows // ROWS, ROWS, atoms)
     right = right.reshape(deep)
 
@@ -458,16 +388,17 @@
                 right,
                 start,
             )
-            (coupled,) = call(
-                functools.partial(couple_kernel, rows),
-                [every],
-                [held(*wide)] + work,
-                NB * flops,
-                own,
-                beside(compact),
-                coupling,
-                neighbour_offsets,
-            )
+            halos = [beside(compact)]
+        (coupled,) = call(
+            functools.partial(couple_kernel, rows),
+            [every],
+            [held(*wide)] + work,
+            NB * flops,
+            own,
+            *halos,
+            links,
+            neighbour_offsets,
+        )
         gathered = lax.all_to_all(coupled.reshape(parts, share, rows, atoms), "energy", 0, 0)
         (mixed,) = call(
             functools.partial(mix_kernel, 2),

time: 88.1 us -> 82.8 us (0.940)
  Pallas kernels: 23.2 us -> 19.2 us
    pallas_call x7, Pallas kernels: 23.2 us -> 19.2 us  [call(): pl.pallas_call(kernel, out_shape=shapes, in_specs=spaces or [vmem] * len(...]
  transfers between devices with their start and end apart: 3 -> 3, of which waited for: 1 -> 1; matrix products, arithmetic and copies ran while one was open for 0% -> 0% of each run, Pallas kernels for 3% -> 2%
where the time goes in v6:
time: 82.8 us; the launch traced here: 82.5 us
  blocking collectives  60.3 us (73%)
  Pallas kernels  19.2 us (23%)
  waiting for transfers between devices  1.57 us (2%)
    all_to_all x2, blocking collectives, body(): lax.all_to_all(coupled.reshape(parts, share, rows, atoms), 'energy', 0, 0)  33.2 us
    all_to_all x2, blocking collectives, body(): sigma = lax.all_to_all(mixed, 'energy', 0, 0).reshape(every)  27.1 us
    pallas_call x7, Pallas kernels, call(): pl.pallas_call(kernel, out_shape=shapes, in_specs=spaces or [vmem] * len(...  19.2 us
  transfers between devices with their start and end apart: 3, of which 1 were waited for; matrix products, arithmetic and copies ran while one was open for 0% of the time, Pallas kernels for 2%

profile of v6, /device:TPU:0, one launch (start us, length us, event | category | flops | bytes accessed | tf_op | source)
XLA Modules:
  0.0 82.5 jit_solution(7555878081477404325)
XLA Ops:
  0.6 0.5 collective-permute-start
  1.1 0.1 collective-permute-start.1
  1.2 0.0 copy-start.2
  1.2 1.7 %shard_map.95 = (f32[1152,128]{1,0:T(8,128)S(1)}, f32[576,128]{1,0:T(8,128)S(1)}, f32[1152,128]{1,0:T(8,128)S(1)}, f32[2,32,32]{2,1,0:T(8,128)S(1)}, f32[12,144,128]{2,1,0:T(8,128)S(1)}) custom-call(f32[2,144,128]{2,1,0:T(8,128)} %refs_3_.5, f32[2,144,128]{2,1,0:T(8,128)} %refs_4_.3, f32[2,144,128]{2,1,0:T(8,128)} %refs_2_.2, s32[64]{0:T(128)} %refs_3_.3, ...), custom_call_target="tpu_custom_call" | custom-call | flops 1179648 | bytes 3695360 | tf_op jit(solution)/shard_map/pallas_call | solution.py:305
  3.0 0.0 collective-permute-done.refs_0_
  3.0 0.0 collective-permute-done.1.refs_1_
  3.0 0.0 copy-done.2
  3.0 7.3 %shard_map.96 = f32[144,4,128]{2,1,0:T(4,128)S(1)} custom-call(f32[1152,128]{1,0:T(8,128)S(1)} %get-tuple-element.10.own.free, f32[2,144,128]{2,1,0:T(8,128)S(1)} %collective-permute-done.refs_0_, f32[2,144,128]{2,1,0:T(8,128)S(1)} %collective-permute-done.1.refs_1_, f32[12,144,128]{2,1,0:T(8,128)S(1)} %get-tuple-element.11.refs_2_.refs_1_, ...), custom_call_target="tpu_custom_call" | custom-call | flops 42467328 | bytes 2070528 | tf_op jit(solution)/shard_map/pallas_call | solution.py:305
  10.3 19.0 %all_to_all.20.blocks = f32[16,9,4,128]{3,2,1,0:T(4,128)S(1)} all-to-all(f32[16,9,4,128]{3,2,1,0:T(4,128)S(1)} %bitcast.13), channel_id=1, replica_groups=mesh['energy'=16,'slab'=2] {'energy'}, dimensions={0} | all-to-all | bytes 589824 | tf_op jit(solution)/shard_map/all_to_all | solution.py:402
  29.3 0.5 shard_map.97
  29.8 13.5 %all_to_all.21 = f32[16,9,4,128]{3,2,1,0:T(4,128)S(1)} all-to-all(f32[16,9,4,128]{3,2,1,0:T(4,128)S(1)} %shard_map.97), channel_id=1, replica_groups=mesh['energy'=16,'slab'=2] {'energy'}, dimensions={0} | all-to-all | bytes 589824 | tf_op jit(solution)/shard_map/all_to_all | solution.py:411
  43.3 0.6 shard_map.98
  43.9 0.1 collective-permute-start.2
  44.0 1.6 %collective-permute-done.2.refs_0_ = f32[144,4,128]{2,1,0:T(4,128)S(1)} collective-permute-done((f32[144,4,128]{2,1,0:T(4,128)S(1)}, f32[144,4,128]{2,1,0:T(4,128)S(1)}, u32[]{:S(2)}, u32[]{:S(2)}) %collective-permute-start.2) | collective-permute-done | bytes 294944 | tf_op jit(solution)/shard_map/ppermute | solution.py:321
  45.6 7.2 %shard_map.99 = f32[144,4,128]{2,1,0:T(4,128)S(1)} custom-call(f32[1152,128]{1,0:T(8,128)S(1)} %get-tuple-element.14.own, f32[144,4,128]{2,1,0:T(4,128)S(1)} %collective-permute-done.2.refs_0_, f32[12,144,128]{2,1,0:T(8,128)S(1)} %get-tuple-element.11.refs_2_.refs_1_, s32[12,128]{1,0:T(8,128)S(1)} %copy-done.2), custom_call_target="tpu_custom_call" | custom-call | flops 42467328 | bytes 2070528 | tf_op jit(solution)/shard_map/pallas_call | solution.py:305
  52.8 14.2 %all_to_all.22.blocks = f32[16,9,4,128]{3,2,1,0:T(4,128)S(1)} all-to-all(f32[16,9,4,128]{3,2,1,0:T(4,128)S(1)} %bitcast.12), channel_id=1, replica_groups=mesh['energy'=16,'slab'=2] {'energy'}, dimensions={0} | all-to-all | bytes 589824 | tf_op jit(solution)/shard_map/all_to_all | solution.py:402
  67.0 0.5 shard_map.100
  67.6 0.0 copy-start
  67.6 0.0 copy-start.1
  67.6 13.6 %all_to_all.23 = f32[16,9,4,128]{3,2,1,0:T(4,128)S(1)} all-to-all(f32[16,9,4,128]{3,2,1,0:T(4,128)S(1)} %shard_map.100), channel_id=1, replica_groups=mesh['energy'=16,'slab'=2] {'energy'}, dimensions={0} | all-to-all | bytes 589824 | tf_op jit(solution)/shard_map/all_to_all | solution.py:411
  81.2 0.0 copy-done
  81.2 0.0 copy-done.1
  81.2 1.3 %shard_map.101 = (f32[2,144,128]{2,1,0:T(8,128)}, f32[2,144,128]{2,1,0:T(8,128)}) custom-call(f32[144,4,128]{2,1,0:T(4,128)S(1)} %bitcast.11, f32[72,8,128]{2,1,0:T(8,128)S(1)} %bitcast.10, f32[144,8,128]{2,1,0:T(8,128)S(1)} %bitcast.7, f32[2,144,128]{2,1,0:T(8,128)S(1)} %copy-done, f32[2,144,128]{2,1,0:T(8,128)S(1)} %copy-done.1), custom_call_target="tpu_custom_call" | custom-call | flops 3538944 | bytes 1769472 | tf_op jit(solution)/shard_map/pallas_call | solution.py:305
Async XLA Ops:
  0.6 2.4 %collective-permute-start = (f32[2,144,128]{2,1,0:T(8,128)}, f32[2,144,128]{2,1,0:T(8,128)S(1)}, u32[]{:S(2)}, u32[]{:S(2)}) collective-permute-start(f32[2,144,128]{2,1,0:T(8,128)} %refs_3_.5), channel_id=1, source_target_pairs={{0,1},{1,0},{2,3},{3,2},{4,5},{5,4},{6,7},{7,6},{8,9},{9,8},{10,11... | collective-permute-start | bytes 442376 | tf_op jit(solution)/shard_map/ppermute | solution.py:321
  1.1 1.8 %collective-permute-start.1 = (f32[2,144,128]{2,1,0:T(8,128)}, f32[2,144,128]{2,1,0:T(8,128)S(1)}, u32[]{:S(2)}, u32[]{:S(2)}) collective-permute-start(f32[2,144,128]{2,1,0:T(8,128)} %refs_4_.3), channel_id=1, source_target_pairs={{0,1},{1,0},{2,3},{3,2},{4,5},{5,4},{6,7},{7,6},{8,9},{9,8},{10,11... | collective-permute-start | bytes 442376 | tf_op jit(solution)/shard_map/ppermute | solution.py:321
  1.2 1.8 %copy-start.2 = (s32[12,128]{1,0:T(8,128)S(1)}, s32[12,128]{1,0:T(8,128)}, u32[]{:S(2)}) copy-start(s32[12,128]{1,0:T(8,128)} %refs_2_.3) | copy-start | bytes 18436
  43.9 1.6 %collective-permute-start.2 = (f32[144,4,128]{2,1,0:T(4,128)S(1)}, f32[144,4,128]{2,1,0:T(4,128)S(1)}, u32[]{:S(2)}, u32[]{:S(2)}) collective-permute-start(f32[144,4,128]{2,1,0:T(4,128)S(1)} %get-tuple-element.15), channel_id=1, source_target_pairs={{0,1},{1,0},{2,3},{3,2},{4,5},{5,4},{6,7},{7,6},{8,9},{9,8},{10,11... | collective-permute-start | bytes 884744 | tf_op jit(solution)/shard_map/ppermute | solution.py:321
  67.6 13.6 %copy-start = (f32[2,144,128]{2,1,0:T(8,128)S(1)}, f32[2,144,128]{2,1,0:T(8,128)}, u32[]{:S(2)}) copy-start(f32[2,144,128]{2,1,0:T(8,128)} %refs_3_.5) | copy-start | bytes 442372
  67.6 13.6 %copy-start.1 = (f32[2,144,128]{2,1,0:T(8,128)S(1)}, f32[2,144,128]{2,1,0:T(8,128)}, u32[]{:S(2)}) copy-start(f32[2,144,128]{2,1,0:T(8,128)} %refs_4_.3) | copy-start | bytes 442372

commit v7 on v6

--- a/solution.py
+++ b/solution.py
@@ -12,7 +12,7 @@
 HW = 32
 ITERS = 2
 ROWS = 8
-BLOCKED = 2
+LANES = 128
 
 TOP_RANK = lax.Precision.HIGHEST
 PARAMS = pltpu.CompilerParams(vmem_limit_bytes=24 * 1024 * 1024)
@@ -41,33 +41,13 @@
         is_near[n // group, some, :] = jnp.broadcast_to(near[n : n + 1, :], (rows, atoms))
 
 
-def couple(rows, own, other, coupling, work, keep):
-    lanes, is_near, inside, links_a, links_b, gathered_a, gathered_b, total = work
-    pairs = coupling.shape[1]
-    group = ROWS // rows
-    groups = NB // group
-    steps = NORB // BLOCKED
+def couple(rows, blocked, unroll, own, other, lanes, is_near, links, work, keep):
+    gathered_a, gathered_b, total = work
+    groups = NB * rows // ROWS
+    pairs = total.shape[0]
+    steps = NORB // blocked
     chunk = pairs // steps
-    buffers, links = (gathered_a, gathered_b), (links_a, links_b)
-
-    def link(g, pair):
-        at = pair * ROWS
-        if not isinstance(at, int):
-            at = pl.multiple_of(at, ROWS)
-        return links[g % 2][pl.ds(at, ROWS), :]
-
-    def build(g, first, count):
-        for n in range(g * group, (g + 1) * group):
-            valid = inside[n : n + 1, :]
-            for row in range(rows):
-                spread_rows(
-                    links[g % 2],
-                    first,
-                    n % group * rows + row,
-                    lambda at, size: coupling[n, pl.ds(at, size), :] * valid,
-                    first,
-                    count,
-                )
+    buffers = (gathered_a, gathered_b)
 
     def gather(g, first, count):
         target = buffers[g % 2]
@@ -79,33 +59,28 @@
             outer = jnp.take_along_axis(other[rows_at, :], lane, axis=1, mode="promise_in_bounds")
             target[pair] = jnp.where(mine, inner, outer)
 
-    def ahead(g, step):
-        first = pl.multiple_of(step * chunk, ROWS)
-        gather(g, first, chunk)
-        build(g, first, chunk)
-
-    lax.fori_loop(0, steps, lambda step, _: ahead(0, step), None)
+    lax.fori_loop(0, steps, lambda step, _: gather(0, step * chunk, chunk), None)
     for g in range(groups):
         source = buffers[g % 2]
 
         def block_row(step, _):
-            first = step * BLOCKED
-            inner = [[None] * NORB for _ in range(BLOCKED)]
+            first = step * blocked
+            inner = [[None] * NORB for _ in range(blocked)]
             for j in range(NORB):
-                left = [link(g, (first + b) * NORB + j) for b in range(BLOCKED)]
+                left = [links[g, (first + b) * NORB + j] for b in range(blocked)]
                 for l in range(NORB):
                     value = source[j * NORB + l]
-                    for b in range(BLOCKED):
+                    for b in range(blocked):
                         term = left[b] * value
                         inner[b][l] = term if j == 0 else inner[b][l] + term
             for k in range(NORB):
-                sums = [None] * BLOCKED
+                sums = [None] * blocked
                 for l in range(NORB):
-                    right = link(g, k * NORB + l)
-                    for b in range(BLOCKED):
+                    right = links[g, k * NORB + l]
+                    for b in range(blocked):
                         term = inner[b][l] * right
                         sums[b] = term if l == 0 else sums[b] + term
-                for b in range(BLOCKED):
+                for b in range(blocked):
                     at = (first + b) * NORB + k
                     value = sums[b] if g == 0 else total[at] + sums[b]
                     if g < groups - 1:
@@ -117,20 +92,47 @@
                             width //= 2
                         keep(at, value[:rows])
             if g < groups - 1:
-                ahead(g + 1, step)
-
-        lax.fori_loop(0, steps, block_row, None)
+                gather(g + 1, step * chunk, chunk)
+
+        lax.fori_loop(0, steps, block_row, None, unroll=unroll)
+
+
+def mix_weights(mixing, shifts, coupled, occupied):
+    total = mixing.shape[1]
+    lane = lax.broadcasted_iota(jnp.int32, (ROWS, LANES), 1)
+    row = lax.broadcasted_iota(jnp.int32, (ROWS, LANES), 0)
+    emitted = jnp.zeros((ROWS, LANES), jnp.float32)
+    absorbed = jnp.zeros((ROWS, LANES), jnp.float32)
+    for mode in range(shifts.shape[0]):
+        hit = lane == shifts[mode]
+        absorb = coupled[mode] * occupied[mode]
+        emit = coupled[mode] * (occupied[mode] + 1.0)
+        emitted = emitted + jnp.where(hit, emit, 0.0)
+        absorbed = absorbed + jnp.where(hit, absorb, 0.0)
+    for at in range(0, total, ROWS):
+        for first in range(0, total, LANES):
+            width = min(LANES, total - first)
+            gap = lane + first - (row + at)
+            far = jnp.minimum(jnp.abs(gap), LANES - 1)
+            emit = jnp.take_along_axis(emitted, far, axis=1, mode="promise_in_bounds")
+            absorb = jnp.take_along_axis(absorbed, far, axis=1, mode="promise_in_bounds")
+            some = slice(first, first + width)
+            mixing[0, at : at + ROWS, some] = jnp.where(gap > 0, emit, absorb)[:, :width]
+            mixing[1, at : at + ROWS, some] = jnp.where(gap > 0, absorb, emit)[:, :width]
 
 
 def prep_kernel(*refs):
-    free_hbm, retarded_hbm, modes_hbm, coupling_hbm = refs[0:2], refs[2], refs[3:6], refs[6]
-    start, left, right, mixing, coupling = refs[7:12]
-    free, retarded, shifts, coupled, occupied, sems = refs[12:]
+    free_hbm, retarded_hbm, modes_hbm = refs[0:2], refs[2], refs[3:6]
+    offsets_hbm, coupling_hbm = refs[6:8]
+    start, left, right, mixing, links, lanes, is_near = refs[8:15]
+    free, retarded, shifts, coupled, occupied, offsets, coupling, inside, sems = refs[15:]
     energies, pairs, _ = retarded.shape
     rows = 2 * energies
+    group = ROWS // rows
     share = left.shape[0] // ROWS
     moves = [(free_hbm[f], free.at[f]) for f in range(2)] + [(retarded_hbm, retarded)]
-    moves += list(zip(modes_hbm, (shifts, coupled, occupied))) + [(coupling_hbm, coupling)]
+    moves += list(zip(modes_hbm, (shifts, coupled, occupied))) + [(offsets_hbm, offsets)]
+    moves += [(coupling_hbm.at[n], coupling.at[n]) for n in range(NB)]
     copies = [
         pltpu.make_async_copy(source, target, sems.at[at])
         for at, (source, target) in enumerate(moves)
@@ -150,31 +152,21 @@
         read = lambda at, size: retarded[row % energies, at : at + size, :]
         spread_rows(left, 0, row, read, skipped, share)
         spread_rows(right, 0, row, read, 0, pairs)
-    for copy in copies[3:6]:
+    for copy in copies[3:7]:
         copy.wait()
-    total = mixing.shape[1]
-    gap = lax.broadcasted_iota(jnp.int32, (total, total), 1) - lax.broadcasted_iota(
-        jnp.int32, (total, total), 0
-    )
-    lesser = jnp.zeros((total, total), jnp.float32)
-    greater = jnp.zeros((total, total), jnp.float32)
-    for mode in range(shifts.shape[0]):
-        shift = shifts[mode]
-        absorb = coupled[mode] * occupied[mode]
-        emit = coupled[mode] * (occupied[mode] + 1.0)
-        ahead = gap == shift
-        behind = gap == -shift
-        lesser = lesser + jnp.where(ahead, emit, jnp.where(behind, absorb, 0.0))
-        greater = greater + jnp.where(ahead, absorb, jnp.where(behind, emit, 0.0))
-    mixing[0] = lesser
-    mixing[1] = greater
-    copies[6].wait()
-
-
-def couple_kernel(rows, own, *refs):
-    far, (coupling, offsets, out, other, *work) = refs[:-12], refs[-12:]
-    pairs = coupling.shape[1]
-    index_neighbours(rows, offsets, *work[:3])
+    mix_weights(mixing, shifts, coupled, occupied)
+    index_neighbours(rows, offsets, lanes, is_near, inside)
+    for n in range(NB):
+        copies[7 + n].wait()
+        valid = inside[n : n + 1, :]
+        for row in range(rows):
+            read = lambda at, size: coupling[n, at : at + size, :] * valid
+            spread_rows(links, n // group * pairs, n % group * rows + row, read, 0, pairs)
+
+
+def couple_kernel(rows, blocked, unroll, own, *refs):
+    far, (lanes, is_near, links, out, other, *work) = refs[:-8], refs[-8:]
+    pairs = links.shape[1]
     if len(far) == 1:
         for pair in range(pairs):
             value = far[0][pair]
@@ -190,7 +182,7 @@
     def keep(at, value):
         out[at] = value
 
-    couple(rows, own, other, coupling, work, keep)
+    couple(rows, blocked, unroll, own, other, lanes, is_near, links, work, keep)
     for at in range(pairs, out.shape[0]):
         out[at] = jnp.zeros(out.shape[1:], jnp.float32)
 
@@ -299,7 +291,10 @@
 
 
 def call(kernel, outs, scratch, flops, *operands, spaces=None, targets=None):
-    shapes = [jax.ShapeDtypeStruct(x, jnp.float32) for x in outs]
+    shapes = [
+        x if isinstance(x, jax.ShapeDtypeStruct) else jax.ShapeDtypeStruct(x, jnp.float32)
+        for x in outs
+    ]
     vmem = pl.BlockSpec(memory_space=pltpu.VMEM)
     moved = sum(x.size for x in operands) + sum(x.size for x in shapes)
     return pl.pallas_call(
@@ -352,26 +347,25 @@
     thin = (pairs * rows, atoms)
     every = (parts * share, rows, atoms)
     flops = 4 * NORB * rows * pairs * atoms
-    index = pltpu.VMEM((groups, ROWS, atoms), jnp.int32)
-    work = [index, index, held(NB, atoms)] + [held(*wide)] * 2 + [held(*deep)] * 3
+    index = jax.ShapeDtypeStruct((groups, ROWS, atoms), jnp.int32)
     transfer = lambda count: pltpu.SemaphoreType.DMA((count,))
 
     free = (lesser_free, greater_free)
     halos = [beside(g) for g in free]
     phonons = (phonon_shift, phonon_coupling, phonon_occupation)
-    own, left, right, mixing, links = call(
+    constants = (retarded, *phonons, neighbour_offsets, coupling)
+    own, left, right, mixing, links, lanes, is_near = call(
         prep_kernel,
-        [wide, thin, wide, (2, total, total), coupling.shape],
+        [wide, thin, wide, (2, total, total), (groups * wide[0], atoms), index, index],
         [held(2, *retarded.shape), held(*retarded.shape)]
         + [pltpu.SMEM(x.shape, x.dtype) for x in phonons]
-        + [transfer(7)],
-        4 * ROWS * retarded.size,
-        *(
-            pltpu.with_memory_space_constraint(x, pltpu.HBM)
-            for x in (*free, retarded, *phonons, coupling)
-        ),
-        spaces=[away] * 7,
+        + [pltpu.VMEM(neighbour_offsets.shape, jnp.int32)]
+        + [held(*coupling.shape), held(NB, atoms), transfer(7 + NB)],
+        rows * coupling.size,
+        *(pltpu.with_memory_space_constraint(x, pltpu.HBM) for x in (*free, *constants)),
+        spaces=[away] * 8,
     )
+    links = links.reshape(groups, pairs, ROWS, atoms)
     start = own
     left = left.reshape(pairs * rows // ROWS, ROWS, atoms)
     right = right.reshape(deep)
@@ -390,14 +384,15 @@
             )
             halos = [beside(compact)]
         (coupled,) = call(
-            functools.partial(couple_kernel, rows),
+            functools.partial(couple_kernel, rows, *((3, 1) if step == 0 else (2, 2))),
             [every],
-            [held(*wide)] + work,
+            [held(*wide)] + [held(*deep)] * 3,
             NB * flops,
             own,
             *halos,
+            lanes,
+            is_near,
             links,
-            neighbour_offsets,
         )
         gathered = lax.all_to_all(coupled.reshape(parts, share, rows, atoms), "energy", 0, 0)
         (mixed,) = call(

time: 82.8 us -> 83.5 us (level)
  Pallas kernels: 19.2 us -> 20.1 us
    pallas_call x7, Pallas kernels: 19.2 us -> 20.1 us  [call(): pl.pallas_call(kernel, out_shape=shapes, in_specs=spaces or [vmem] * len(...]
  transfers between devices with their start and end apart: 3 -> 3, of which waited for: 1 -> 1; matrix products, arithmetic and copies ran while one was open for 0% -> 0% of each run, Pallas kernels for 2% -> 3%
where the time goes in v7:
time: 83.5 us; the launch traced here: 83.3 us
  blocking collectives  60.2 us (72%)
  Pallas kernels  20.1 us (24%)
  waiting for transfers between devices  1.57 us (2%)
    all_to_all x2, blocking collectives, body(): lax.all_to_all(coupled.reshape(parts, share, rows, atoms), 'energy', 0, 0)  33.2 us
    all_to_all x2, blocking collectives, body(): sigma = lax.all_to_all(mixed, 'energy', 0, 0).reshape(every)  26.9 us
    pallas_call x7, Pallas kernels, call(): pl.pallas_call(kernel, out_shape=shapes, in_specs=spaces or [vmem] * len(...  20.1 us
  transfers between devices with their start and end apart: 3, of which 1 were waited for; matrix products, arithmetic and copies ran while one was open for 0% of the time, Pallas kernels for 3%

profile of v7, /device:TPU:0, one launch (start us, length us, event | category | flops | bytes accessed | tf_op | source)
XLA Modules:
  0.0 83.3 jit_solution(5402606623295336932)
XLA Ops:
  0.6 0.5 collective-permute-start
  1.1 0.1 collective-permute-start.1
  1.2 2.2 %shard_map.95 = (f32[1152,128]{1,0:T(8,128)S(1)}, f32[576,128]{1,0:T(8,128)S(1)}, f32[1152,128]{1,0:T(8,128)S(1)}, f32[2,32,32]{2,1,0:T(8,128)S(1)}, f32[6912,12...) custom-call(f32[2,144,128]{2,1,0:T(8,128)} %refs_3_.3, f32[2,144,128]{2,1,0:T(8,128)} %refs_4_.3, ...), custom_call_target="tpu_custom_call" | custom-call | flops 884736 | bytes 6404864 | tf_op jit(solution)/shard_map/pallas_call | solution.py:300
  3.4 0.0 collective-permute-done.refs_0_
  3.4 0.0 collective-permute-done.1.refs_1_
  3.4 7.4 %shard_map.96 = f32[144,4,128]{2,1,0:T(4,128)S(1)} custom-call(f32[1152,128]{1,0:T(8,128)S(1)} %get-tuple-element.12.own.free, f32[2,144,128]{2,1,0:T(8,128)S(1)} %collective-permute-done.refs_0_, f32[2,144,128]{2,1,0:T(8,128)S(1)} %collective-permute-done.1.refs_1_, s32[6,8,128]{2,1,0:T(8,128)S(1)} %get-tuple-element.13.refs_2_.refs_1_, ...), custom_call_target="tpu_custom_call" | custom-call | flops 42467328 | bytes 4767744 | tf_op jit(solution)/shard_map/pallas_call | solution.py:300
  10.8 19.0 %all_to_all.20.blocks = f32[16,9,4,128]{3,2,1,0:T(4,128)S(1)} all-to-all(f32[16,9,4,128]{3,2,1,0:T(4,128)S(1)} %bitcast.12), channel_id=1, replica_groups=mesh['energy'=16,'slab'=2] {'energy'}, dimensions={0} | all-to-all | bytes 589824 | tf_op jit(solution)/shard_map/all_to_all | solution.py:397
  29.8 0.5 shard_map.97
  30.4 13.5 %all_to_all.21 = f32[16,9,4,128]{3,2,1,0:T(4,128)S(1)} all-to-all(f32[16,9,4,128]{3,2,1,0:T(4,128)S(1)} %shard_map.97), channel_id=1, replica_groups=mesh['energy'=16,'slab'=2] {'energy'}, dimensions={0} | all-to-all | bytes 589824 | tf_op jit(solution)/shard_map/all_to_all | solution.py:406
  43.8 0.6 shard_map.98
  44.4 0.0 copy-start
  44.5 0.0 copy-start.1
  44.5 0.1 collective-permute-start.2
  44.6 1.6 %collective-permute-done.2.refs_0_ = f32[144,4,128]{2,1,0:T(4,128)S(1)} collective-permute-done((f32[144,4,128]{2,1,0:T(4,128)S(1)}, f32[144,4,128]{2,1,0:T(4,128)S(1)}, u32[]{:S(2)}, u32[]{:S(2)}) %collective-permute-start.2) | collective-permute-done | bytes 294944 | tf_op jit(solution)/shard_map/ppermute | solution.py:316
  46.1 7.6 %shard_map.99 = f32[144,4,128]{2,1,0:T(4,128)S(1)} custom-call(f32[1152,128]{1,0:T(8,128)S(1)} %get-tuple-element.18.own, f32[144,4,128]{2,1,0:T(4,128)S(1)} %collective-permute-done.2.refs_0_, s32[6,8,128]{2,1,0:T(8,128)S(1)} %get-tuple-element.13.refs_2_.refs_1_, s32[6,8,128]{2,1,0:T(8,128)S(1)} %get-tuple-element.14.refs_3_.refs_2_, ...), custom_call_target="tpu_custom_call" | custom-call | flops 42467328 | bytes 4767744 | tf_op jit(solution)/shard_map/pallas_call | solution.py:300
  53.8 14.2 %all_to_all.22.blocks = f32[16,9,4,128]{3,2,1,0:T(4,128)S(1)} all-to-all(f32[16,9,4,128]{3,2,1,0:T(4,128)S(1)} %bitcast.11), channel_id=1, replica_groups=mesh['energy'=16,'slab'=2] {'energy'}, dimensions={0} | all-to-all | bytes 589824 | tf_op jit(solution)/shard_map/all_to_all | solution.py:397
  68.0 0.5 shard_map.100
  68.5 13.5 %all_to_all.23 = f32[16,9,4,128]{3,2,1,0:T(4,128)S(1)} all-to-all(f32[16,9,4,128]{3,2,1,0:T(4,128)S(1)} %shard_map.100), channel_id=1, replica_groups=mesh['energy'=16,'slab'=2] {'energy'}, dimensions={0} | all-to-all | bytes 589824 | tf_op jit(solution)/shard_map/all_to_all | solution.py:406
  82.0 0.0 copy-done
  82.0 0.0 copy-done.1
  82.0 1.3 %shard_map.101 = (f32[2,144,128]{2,1,0:T(8,128)}, f32[2,144,128]{2,1,0:T(8,128)}) custom-call(f32[144,4,128]{2,1,0:T(4,128)S(1)} %bitcast.16, f32[72,8,128]{2,1,0:T(8,128)S(1)} %bitcast.15, f32[144,8,128]{2,1,0:T(8,128)S(1)} %bitcast.10, f32[2,144,128]{2,1,0:T(8,128)S(1)} %copy-done, f32[2,144,128]{2,1,0:T(8,128)S(1)} %copy-done.1), custom_call_target="tpu_custom_call" | custom-call | flops 3538944 | bytes 1769472 | tf_op jit(solution)/shard_map/pallas_call | solution.py:300
Async XLA Ops:
  0.6 2.8 %collective-permute-start = (f32[2,144,128]{2,1,0:T(8,128)}, f32[2,144,128]{2,1,0:T(8,128)S(1)}, u32[]{:S(2)}, u32[]{:S(2)}) collective-permute-start(f32[2,144,128]{2,1,0:T(8,128)} %refs_3_.3), channel_id=1, source_target_pairs={{0,1},{1,0},{2,3},{3,2},{4,5},{5,4},{6,7},{7,6},{8,9},{9,8},{10,11... | collective-permute-start | bytes 442376 | tf_op jit(solution)/shard_map/ppermute | solution.py:316
  1.1 2.3 %collective-permute-start.1 = (f32[2,144,128]{2,1,0:T(8,128)}, f32[2,144,128]{2,1,0:T(8,128)S(1)}, u32[]{:S(2)}, u32[]{:S(2)}) collective-permute-start(f32[2,144,128]{2,1,0:T(8,128)} %refs_4_.3), channel_id=1, source_target_pairs={{0,1},{1,0},{2,3},{3,2},{4,5},{5,4},{6,7},{7,6},{8,9},{9,8},{10,11... | collective-permute-start | bytes 442376 | tf_op jit(solution)/shard_map/ppermute | solution.py:316
  44.4 37.5 %copy-start = (f32[2,144,128]{2,1,0:T(8,128)S(1)}, f32[2,144,128]{2,1,0:T(8,128)}, u32[]{:S(2)}) copy-start(f32[2,144,128]{2,1,0:T(8,128)} %refs_3_.3) | copy-start | bytes 442372
  44.5 37.5 %copy-start.1 = (f32[2,144,128]{2,1,0:T(8,128)S(1)}, f32[2,144,128]{2,1,0:T(8,128)}, u32[]{:S(2)}) copy-start(f32[2,144,128]{2,1,0:T(8,128)} %refs_4_.3) | copy-start | bytes 442372
  44.5 1.6 %collective-permute-start.2 = (f32[144,4,128]{2,1,0:T(4,128)S(1)}, f32[144,4,128]{2,1,0:T(4,128)S(1)}, u32[]{:S(2)}, u32[]{:S(2)}) collective-permute-start(f32[144,4,128]{2,1,0:T(4,128)S(1)} %get-tuple-element.19), channel_id=1, source_target_pairs={{0,1},{1,0},{2,3},{3,2},{4,5},{5,4},{6,7},{7,6},{8,9},{9,8},{10,11... | collective-permute-start | bytes 884744 | tf_op jit(solution)/shard_map/ppermute | solution.py:316

commit v8 on v7

--- a/solution.py
+++ b/solution.py
@@ -13,16 +13,27 @@
 ITERS = 2
 ROWS = 8
 LANES = 128
+BLOCKED = 2
 
 TOP_RANK = lax.Precision.HIGHEST
 PARAMS = pltpu.CompilerParams(vmem_limit_bytes=24 * 1024 * 1024)
 
 
-def spread_rows(target, base, row, source, first, count):
-    for at in range(0, count, ROWS):
-        size = min(ROWS, count - at)
-        rows = pl.ds((base + at) * ROWS + row, size, stride=ROWS)
-        target[rows, :] = source(first + at, size)
+def each(count, step):
+    lax.fori_loop(0, count, lambda at, _: step(at), None)
+
+
+def eight(at):
+    return pl.ds(pl.multiple_of(at * ROWS, ROWS), ROWS)
+
+
+def spread_rows(target, base, sources, count):
+    def tile(at):
+        for row, source in sources:
+            rows = pl.ds((base + at * ROWS) * ROWS + row, ROWS, stride=ROWS)
+            target[rows, :] = source(pl.multiple_of(at * ROWS, ROWS))
+
+    each(count // ROWS, tile)
 
 
 def index_neighbours(rows, offsets, lanes, is_near, inside):
@@ -41,60 +52,96 @@
         is_near[n // group, some, :] = jnp.broadcast_to(near[n : n + 1, :], (rows, atoms))
 
 
-def couple(rows, blocked, unroll, own, other, lanes, is_near, links, work, keep):
-    gathered_a, gathered_b, total = work
-    groups = NB * rows // ROWS
-    pairs = total.shape[0]
-    steps = NORB // blocked
+def couple(own, other, lanes, is_near, links, gathered_a, gathered_b, total):
+    groups, pairs = links.shape[:2]
+    steps = NORB // BLOCKED
     chunk = pairs // steps
-    buffers = (gathered_a, gathered_b)
-
-    def gather(g, first, count):
-        target = buffers[g % 2]
+
+    def gather(target, g, step):
         lane, mine = lanes[g], is_near[g] != 0
-        for at in range(count):
-            pair = first + at
-            rows_at = pl.ds(pl.multiple_of(pair * ROWS, ROWS), ROWS)
-            inner = jnp.take_along_axis(own[rows_at, :], lane, axis=1, mode="promise_in_bounds")
-            outer = jnp.take_along_axis(other[rows_at, :], lane, axis=1, mode="promise_in_bounds")
+        for at in range(chunk):
+            pair = step * chunk + at
+            inner = jnp.take_along_axis(own[eight(pair), :], lane, axis=1, mode="promise_in_bounds")
+            outer = jnp.take_along_axis(other[eight(pair), :], lane, axis=1, mode="promise_in_bounds")
             target[pair] = jnp.where(mine, inner, outer)
 
-    lax.fori_loop(0, steps, lambda step, _: gather(0, step * chunk, chunk), None)
-    for g in range(groups):
-        source = buffers[g % 2]
-
-        def block_row(step, _):
-            first = step * blocked
-            inner = [[None] * NORB for _ in range(blocked)]
+    def group_sums(g, source, target):
+        following = jnp.minimum(g + 1, groups - 1)
+
+        def block_row(step):
+            first = step * BLOCKED
+            inner = [[None] * NORB for _ in range(BLOCKED)]
             for j in range(NORB):
-                left = [links[g, (first + b) * NORB + j] for b in range(blocked)]
+                left = [links[g, (first + b) * NORB + j] for b in range(BLOCKED)]
                 for l in range(NORB):
                     value = source[j * NORB + l]
-                    for b in range(blocked):
+                    for b in range(BLOCKED):
                         term = left[b] * value
                         inner[b][l] = term if j == 0 else inner[b][l] + term
             for k in range(NORB):
-                sums = [None] * blocked
+                at = [(first + b) * NORB + k for b in range(BLOCKED)]
+                sums = [total[at[b]] for b in range(BLOCKED)]
                 for l in range(NORB):
                     right = links[g, k * NORB + l]
-                    for b in range(blocked):
-                        term = inner[b][l] * right
-                        sums[b] = term if l == 0 else sums[b] + term
-                for b in range(blocked):
-                    at = (first + b) * NORB + k
-                    value = sums[b] if g == 0 else total[at] + sums[b]
-                    if g < groups - 1:
-                        total[at] = value
-                    else:
-                        width = ROWS // 2
-                        while width >= rows:
-                            value = value + pltpu.roll(value, width, 0)
-                            width //= 2
-                        keep(at, value[:rows])
-            if g < groups - 1:
-                gather(g + 1, step * chunk, chunk)
-
-        lax.fori_loop(0, steps, block_row, None, unroll=unroll)
+                    for b in range(BLOCKED):
+                        sums[b] = sums[b] + inner[b][l] * right
+                for b in range(BLOCKED):
+                    total[at[b]] = sums[b]
+            gather(target, following, step)
+
+        each(steps, block_row)
+
+    def clear(step):
+        for at in range(chunk):
+            total[step * chunk + at] = jnp.zeros(total.shape[1:], jnp.float32)
+        gather(gathered_a, 0, step)
+
+    def two_groups(half):
+        group_sums(half * 2, gathered_a, gathered_b)
+        group_sums(half * 2 + 1, gathered_b, gathered_a)
+
+    each(steps, clear)
+    each(groups // 2, two_groups)
+    if groups % 2:
+        group_sums(groups - 1, gathered_a, gathered_b)
+
+
+def couple_kernel(rows, own, *refs):
+    far, (lanes, is_near, links, out, other, *work) = refs[:-8], refs[-8:]
+    pairs = links.shape[1]
+    total = work[-1]
+    if len(far) == 1:
+
+        def widen(tile):
+            for pair in range(ROWS):
+                value = far[0][tile * ROWS + pair]
+                for at in range(0, ROWS, rows):
+                    some = pl.ds((tile * ROWS + pair) * ROWS + at, rows)
+                    other[some, :] = value
+
+        each(pairs // ROWS, widen)
+    else:
+        energies = rows // len(far)
+
+        def reader(row):
+            source, energy = far[row % rows // energies], row % energies
+            return row, lambda at: source[energy, pl.ds(at, ROWS), :]
+
+        spread_rows(other, 0, [reader(row) for row in range(ROWS)], pairs)
+    couple(own, other, lanes, is_near, links, *work)
+
+    def finish(tile):
+        for at in range(ROWS):
+            value = total[tile * ROWS + at]
+            width = ROWS // 2
+            while width >= rows:
+                value = value + pltpu.roll(value, width, 0)
+                width //= 2
+            out[tile * ROWS + at] = value[:rows]
+
+    each(pairs // ROWS, finish)
+    for at in range(pairs, out.shape[0]):
+        out[at] = jnp.zeros(out.shape[1:], jnp.float32)
 
 
 def mix_weights(mixing, shifts, coupled, occupied):
@@ -103,12 +150,17 @@
     row = lax.broadcasted_iota(jnp.int32, (ROWS, LANES), 0)
     emitted = jnp.zeros((ROWS, LANES), jnp.float32)
     absorbed = jnp.zeros((ROWS, LANES), jnp.float32)
-    for mode in range(shifts.shape[0]):
+
+    def add_mode(mode, weights):
+        emitted, absorbed = weights
         hit = lane == shifts[mode]
         absorb = coupled[mode] * occupied[mode]
         emit = coupled[mode] * (occupied[mode] + 1.0)
-        emitted = emitted + jnp.where(hit, emit, 0.0)
-        absorbed = absorbed + jnp.where(hit, absorb, 0.0)
+        return emitted + jnp.where(hit, emit, 0.0), absorbed + jnp.where(hit, absorb, 0.0)
+
+    emitted, absorbed = lax.fori_loop(
+        0, shifts.shape[0], add_mode, (emitted, absorbed), unroll=8
+    )
     for at in range(0, total, ROWS):
         for first in range(0, total, LANES):
             width = min(LANES, total - first)
@@ -142,89 +194,87 @@
 
     copies[0].wait()
     copies[1].wait()
-    for row in range(ROWS):
+
+    def own_reader(row):
         function, energy = row % rows // energies, row % energies
-        read = lambda at, size: free[function, energy, at : at + size, :]
-        spread_rows(start, 0, row, read, 0, pairs)
+        return row, lambda at: free[function, energy, pl.ds(at, ROWS), :]
+
+    spread_rows(start, 0, [own_reader(row) for row in range(ROWS)], pairs)
     copies[2].wait()
-    for row in range(ROWS):
-        skipped = row // rows * share
-        read = lambda at, size: retarded[row % energies, at : at + size, :]
-        spread_rows(left, 0, row, read, skipped, share)
-        spread_rows(right, 0, row, read, 0, pairs)
+
+    def factor_reader(row, skipped):
+        return row, lambda at: retarded[row % energies, pl.ds(skipped + at, ROWS), :]
+
+    spread_rows(left, 0, [factor_reader(row, row // rows * share) for row in range(ROWS)], share)
+    spread_rows(right, 0, [factor_reader(row, 0) for row in range(ROWS)], pairs)
     for copy in copies[3:7]:
         copy.wait()
     mix_weights(mixing, shifts, coupled, occupied)
     index_neighbours(rows, offsets, lanes, is_near, inside)
-    for n in range(NB):
-        copies[7 + n].wait()
-        valid = inside[n : n + 1, :]
-        for row in range(rows):
-            read = lambda at, size: coupling[n, at : at + size, :] * valid
-            spread_rows(links, n // group * pairs, n % group * rows + row, read, 0, pairs)
-
-
-def couple_kernel(rows, blocked, unroll, own, *refs):
-    far, (lanes, is_near, links, out, other, *work) = refs[:-8], refs[-8:]
-    pairs = links.shape[1]
-    if len(far) == 1:
-        for pair in range(pairs):
-            value = far[0][pair]
-            for at in range(0, ROWS, rows):
-                other[pair * ROWS + at : pair * ROWS + at + rows, :] = value
-    else:
-        energies = rows // len(far)
-        for row in range(ROWS):
-            source = far[row % rows // energies]
-            read = lambda at, size: source[row % energies, at : at + size, :]
-            spread_rows(other, 0, row, read, 0, pairs)
-
-    def keep(at, value):
-        out[at] = value
-
-    couple(rows, blocked, unroll, own, other, lanes, is_near, links, work, keep)
-    for at in range(pairs, out.shape[0]):
-        out[at] = jnp.zeros(out.shape[1:], jnp.float32)
+    for copy in copies[7:]:
+        copy.wait()
+
+    def expand(n):
+        valid = inside[pl.ds(n, 1), :]
+        read = lambda at: coupling[n, pl.ds(at, ROWS), :] * valid
+        first = n % group * rows
+        spread_rows(
+            links, n // group * pairs, [(first + row, read) for row in range(rows)], pairs
+        )
+
+    each(NB, expand)
 
 
 def mix_kernel(fused, mixing, blocks, out, before, after):
     parts, share, rows, atoms = blocks.shape
     energies = rows // fused
+
+    def place(pair):
+        lanes = pl.ds(pl.multiple_of(pair * atoms, atoms), atoms)
+        for part in range(parts):
+            held = slice(part * energies, (part + 1) * energies)
+            value = blocks[part, pair]
+            for f in range(fused):
+                before[f, held, lanes] = value[f * energies : (f + 1) * energies]
+
+    def replace(pair):
+        lanes = pl.ds(pl.multiple_of(pair * atoms, atoms), atoms)
+        for part in range(parts):
+            held = slice(part * energies, (part + 1) * energies)
+            for f in range(fused):
+                out[part, pair, f * energies : (f + 1) * energies, :] = after[f, held, lanes]
+
+    each(share, place)
     for f in range(fused):
-        some = slice(f * energies, (f + 1) * energies)
-        for part in range(parts):
-            for pair in range(share):
-                before[part * energies : (part + 1) * energies, pair * atoms : (pair + 1) * atoms] = (
-                    blocks[part, pair, some, :]
-                )
-        after[...] = jnp.dot(
-            mixing[f], before[...], precision=TOP_RANK, preferred_element_type=jnp.float32
+        after[f] = jnp.dot(
+            mixing[f], before[f], precision=TOP_RANK, preferred_element_type=jnp.float32
         )
-        for part in range(parts):
-            for pair in range(share):
-                out[part, pair, some, :] = after[
-                    part * energies : (part + 1) * energies, pair * atoms : (pair + 1) * atoms
-                ]
-
-
-def dress(rows, sigma, left, right, copied, keep):
-    parts = ROWS // rows
-    for pair in range(NORB * NORB):
-        value = sigma[pair]
-        for part in range(parts):
-            copied[pair, part * rows : (part + 1) * rows, :] = value
-    for i in range(NORB // parts):
-        inner = [None] * NORB
-        for j in range(NORB):
-            factor = left[i * NORB + j]
-            for l in range(NORB):
-                term = factor * copied[j * NORB + l]
-                inner[l] = term if j == 0 else inner[l] + term
-        for k in range(NORB):
-            value = inner[0] * right[k * NORB]
-            for l in range(1, NORB):
-                value = value + inner[l] * right[k * NORB + l]
-            keep(i * NORB + k, value)
+    each(share, replace)
+
+
+def widen_sigma(rows, sigma, copied):
+    def widen(tile):
+        for at in range(ROWS):
+            pair = tile * ROWS + at
+            value = sigma[pair]
+            for first in range(0, ROWS, rows):
+                copied[pair, first : first + rows, :] = value
+
+    each(copied.shape[0] // ROWS, widen)
+
+
+def dress_row(i, left, right, copied, keep):
+    inner = [None] * NORB
+    for j in range(NORB):
+        factor = left[i * NORB + j]
+        for l in range(NORB):
+            term = factor * copied[j * NORB + l]
+            inner[l] = term if j == 0 else inner[l] + term
+    for k in range(NORB):
+        value = inner[0] * right[k * NORB]
+        for l in range(1, NORB):
+            value = value + inner[l] * right[k * NORB + l]
+        keep(i * NORB + k, value)
 
 
 def dress_between_kernel(rows, sigma, left, right, free, own, compact, copied):
@@ -241,11 +291,12 @@
                 piece = piece + pltpu.roll(piece, width, 0)
                 width //= 2
             pair = part * share + at
-            piece = piece + free[pair * ROWS : (pair + 1) * ROWS, :]
-            own[pair * ROWS : (pair + 1) * ROWS, :] = piece
+            piece = piece + free[eight(pair), :]
+            own[eight(pair), :] = piece
             compact[pair] = piece[:rows]
 
-    dress(rows, sigma, left, right, copied, keep)
+    widen_sigma(rows, sigma, copied)
+    each(share // NORB, lambda i: dress_row(i, left, right, copied, keep))
 
 
 def dress_last_kernel(*refs):
@@ -257,37 +308,41 @@
     parts = ROWS // rows
     share = left.shape[0]
     stage = 2 * NORB
-    copies = []
+    stages = share // stage
 
     def keep(at, value):
-        dressed[at * ROWS : (at + 1) * ROWS, :] = value
-        if (at + 1) % stage and at + 1 < share:
-            return
-        done = at // stage * stage
+        dressed[eight(at), :] = value
+
+    def departure(done, function, part):
+        some = pl.ds(pl.multiple_of(part * share + done * stage, ROWS), stage)
+        return pltpu.make_async_copy(
+            out.at[function, :, some, :],
+            out_hbm[function].at[:, some, :],
+            leaving.at[(done * 2 + function) * parts + part],
+        )
+
+    def dress_stage(done):
+        for at in range(stage // NORB):
+            dress_row(done * (stage // NORB) + at, left, right, copied, keep)
         for row in range(ROWS):
             function, energy, part = row % rows // energies, row % energies, row // rows
-            for begin in range(done, at + 1, ROWS):
-                size = min(ROWS, at + 1 - begin)
-                first = part * share + begin
-                piece = dressed[pl.ds(begin * ROWS + row, size, stride=ROWS), :]
-                out[function, energy, first : first + size, :] = (
-                    free[function][energy, first : first + size, :] + piece
-                )
+            for at in range(0, stage, ROWS):
+                begin = done * stage + at
+                some = pl.ds(pl.multiple_of(part * share + begin, ROWS), ROWS)
+                piece = dressed[pl.ds(begin * ROWS + row, ROWS, stride=ROWS), :]
+                out[function, energy, some, :] = free[function][energy, some, :] + piece
         for function in range(2):
             for part in range(parts):
-                some = pl.ds(part * share + done, at + 1 - done)
-                copies.append(
-                    pltpu.make_async_copy(
-                        out.at[function, :, some, :],
-                        out_hbm[function].at[:, some, :],
-                        leaving.at[len(copies)],
-                    )
-                )
-                copies[-1].start()
-
-    dress(rows, sigma, left, right, copied, keep)
-    for copy in copies:
-        copy.wait()
+                departure(done, function, part).start()
+
+    def await_stage(done):
+        for function in range(2):
+            for part in range(parts):
+                departure(done, function, part).wait()
+
+    widen_sigma(rows, sigma, copied)
+    each(stages, dress_stage)
+    each(stages, await_stage)
 
 
 def call(kernel, outs, scratch, flops, *operands, spaces=None, targets=None):
@@ -384,7 +439,7 @@
             )
             halos = [beside(compact)]
         (coupled,) = call(
-            functools.partial(couple_kernel, rows, *((3, 1) if step == 0 else (2, 2))),
+            functools.partial(couple_kernel, rows),
             [every],
             [held(*wide)] + [held(*deep)] * 3,
             NB * flops,
@@ -398,7 +453,7 @@
         (mixed,) = call(
             functools.partial(mix_kernel, 2),
             [gathered.shape],
-            [held(total, share * atoms)] * 2,
+            [held(2, total, share * atoms)] * 2,
             2 * total * gathered.size,
             mixing,
             gathered,

time: 83.5 us -> 84.1 us (level)
  transfers between devices with their start and end apart: 3 -> 3, of which waited for: 1 -> 1; matrix products, arithmetic and copies ran while one was open for 0% -> 0% of each run, Pallas kernels for 3% -> 4%
where the time goes in v8:
time: 84.1 us; the launch traced here: 83.8 us
  blocking collectives  60.2 us (72%)
  Pallas kernels  20.7 us (25%)
  waiting for transfers between devices  1.57 us (2%)
    all_to_all x2, blocking collectives, body(): lax.all_to_all(coupled.reshape(parts, share, rows, atoms), 'energy', 0, 0)  33.2 us
    all_to_all x2, blocking collectives, body(): sigma = lax.all_to_all(mixed, 'energy', 0, 0).reshape(every)  26.9 us
    pallas_call x7, Pallas kernels, call(): pl.pallas_call(kernel, out_shape=shapes, in_specs=spaces or [vmem] * len(...  20.7 us
  transfers between devices with their start and end apart: 3, of which 1 were waited for; matrix products, arithmetic and copies ran while one was open for 0% of the time, Pallas kernels for 4%

profile of v8, /device:TPU:0, one launch (start us, length us, event | category | flops | bytes accessed | tf_op | source)
XLA Modules:
  0.0 83.8 jit_solution(5604112856730755757)
XLA Ops:
  0.6 0.5 collective-permute-start
  1.1 0.1 collective-permute-start.1
  1.2 3.6 %shard_map.95 = (f32[1152,128]{1,0:T(8,128)S(1)}, f32[576,128]{1,0:T(8,128)S(1)}, f32[1152,128]{1,0:T(8,128)S(1)}, f32[2,32,32]{2,1,0:T(8,128)S(1)}, f32[6912,12...) custom-call(f32[2,144,128]{2,1,0:T(8,128)} %refs_3_.3, f32[2,144,128]{2,1,0:T(8,128)} %refs_4_.3, ...), custom_call_target="tpu_custom_call" | custom-call | flops 884736 | bytes 6404864 | tf_op jit(solution)/shard_map/pallas_call | solution.py:355
  4.8 0.0 collective-permute-done.refs_0_
  4.8 0.0 collective-permute-done.1.refs_1_
  4.8 6.8 %shard_map.96 = f32[144,4,128]{2,1,0:T(4,128)S(1)} custom-call(f32[1152,128]{1,0:T(8,128)S(1)} %get-tuple-element.12.own.free, f32[2,144,128]{2,1,0:T(8,128)S(1)} %collective-permute-done.refs_0_, f32[2,144,128]{2,1,0:T(8,128)S(1)} %collective-permute-done.1.refs_1_, s32[6,8,128]{2,1,0:T(8,128)S(1)} %get-tuple-element.13.refs_2_.refs_1_, ...), custom_call_target="tpu_custom_call" | custom-call | flops 42467328 | bytes 4767744 | tf_op jit(solution)/shard_map/pallas_call | solution.py:355
  11.7 19.0 %all_to_all.20.blocks = f32[16,9,4,128]{3,2,1,0:T(4,128)S(1)} all-to-all(f32[16,9,4,128]{3,2,1,0:T(4,128)S(1)} %bitcast.12), channel_id=1, replica_groups=mesh['energy'=16,'slab'=2] {'energy'}, dimensions={0} | all-to-all | bytes 589824 | tf_op jit(solution)/shard_map/all_to_all | solution.py:452
  30.7 0.7 shard_map.97
  31.4 13.5 %all_to_all.21 = f32[16,9,4,128]{3,2,1,0:T(4,128)S(1)} all-to-all(f32[16,9,4,128]{3,2,1,0:T(4,128)S(1)} %shard_map.97), channel_id=1, replica_groups=mesh['energy'=16,'slab'=2] {'energy'}, dimensions={0} | all-to-all | bytes 589824 | tf_op jit(solution)/shard_map/all_to_all | solution.py:461
  44.8 0.8 shard_map.98
  45.6 0.0 copy-start
  45.6 0.0 copy-start.1
  45.6 0.1 collective-permute-start.2
  45.7 1.6 %collective-permute-done.2.refs_0_ = f32[144,4,128]{2,1,0:T(4,128)S(1)} collective-permute-done((f32[144,4,128]{2,1,0:T(4,128)S(1)}, f32[144,4,128]{2,1,0:T(4,128)S(1)}, u32[]{:S(2)}, u32[]{:S(2)}) %collective-permute-start.2) | collective-permute-done | bytes 294944 | tf_op jit(solution)/shard_map/ppermute | solution.py:371
  47.3 6.8 %shard_map.99 = f32[144,4,128]{2,1,0:T(4,128)S(1)} custom-call(f32[1152,128]{1,0:T(8,128)S(1)} %get-tuple-element.18.own, f32[144,4,128]{2,1,0:T(4,128)S(1)} %collective-permute-done.2.refs_0_, s32[6,8,128]{2,1,0:T(8,128)S(1)} %get-tuple-element.13.refs_2_.refs_1_, s32[6,8,128]{2,1,0:T(8,128)S(1)} %get-tuple-element.14.refs_3_.refs_2_, ...), custom_call_target="tpu_custom_call" | custom-call | flops 42467328 | bytes 4767744 | tf_op jit(solution)/shard_map/pallas_call | solution.py:355
  54.1 14.2 %all_to_all.22.blocks = f32[16,9,4,128]{3,2,1,0:T(4,128)S(1)} all-to-all(f32[16,9,4,128]{3,2,1,0:T(4,128)S(1)} %bitcast.11), channel_id=1, replica_groups=mesh['energy'=16,'slab'=2] {'energy'}, dimensions={0} | all-to-all | bytes 589824 | tf_op jit(solution)/shard_map/all_to_all | solution.py:452
  68.3 0.7 shard_map.100
  69.0 13.5 %all_to_all.23 = f32[16,9,4,128]{3,2,1,0:T(4,128)S(1)} all-to-all(f32[16,9,4,128]{3,2,1,0:T(4,128)S(1)} %shard_map.100), channel_id=1, replica_groups=mesh['energy'=16,'slab'=2] {'energy'}, dimensions={0} | all-to-all | bytes 589824 | tf_op jit(solution)/shard_map/all_to_all | solution.py:461
  82.4 0.0 copy-done
  82.4 0.0 copy-done.1
  82.4 1.4 %shard_map.101 = (f32[2,144,128]{2,1,0:T(8,128)}, f32[2,144,128]{2,1,0:T(8,128)}) custom-call(f32[144,4,128]{2,1,0:T(4,128)S(1)} %bitcast.16, f32[72,8,128]{2,1,0:T(8,128)S(1)} %bitcast.15, f32[144,8,128]{2,1,0:T(8,128)S(1)} %bitcast.10, f32[2,144,128]{2,1,0:T(8,128)S(1)} %copy-done, f32[2,144,128]{2,1,0:T(8,128)S(1)} %copy-done.1), custom_call_target="tpu_custom_call" | custom-call | flops 3538944 | bytes 1769472 | tf_op jit(solution)/shard_map/pallas_call | solution.py:355
Async XLA Ops:
  0.6 4.2 %collective-permute-start = (f32[2,144,128]{2,1,0:T(8,128)}, f32[2,144,128]{2,1,0:T(8,128)S(1)}, u32[]{:S(2)}, u32[]{:S(2)}) collective-permute-start(f32[2,144,128]{2,1,0:T(8,128)} %refs_3_.3), channel_id=1, source_target_pairs={{0,1},{1,0},{2,3},{3,2},{4,5},{5,4},{6,7},{7,6},{8,9},{9,8},{10,11... | collective-permute-start | bytes 442376 | tf_op jit(solution)/shard_map/ppermute | solution.py:371
  1.1 3.7 %collective-permute-start.1 = (f32[2,144,128]{2,1,0:T(8,128)}, f32[2,144,128]{2,1,0:T(8,128)S(1)}, u32[]{:S(2)}, u32[]{:S(2)}) collective-permute-start(f32[2,144,128]{2,1,0:T(8,128)} %refs_4_.3), channel_id=1, source_target_pairs={{0,1},{1,0},{2,3},{3,2},{4,5},{5,4},{6,7},{7,6},{8,9},{9,8},{10,11... | collective-permute-start | bytes 442376 | tf_op jit(solution)/shard_map/ppermute | solution.py:371
  45.6 36.8 %copy-start = (f32[2,144,128]{2,1,0:T(8,128)S(1)}, f32[2,144,128]{2,1,0:T(8,128)}, u32[]{:S(2)}) copy-start(f32[2,144,128]{2,1,0:T(8,128)} %refs_3_.3) | copy-start | bytes 442372
  45.6 36.8 %copy-start.1 = (f32[2,144,128]{2,1,0:T(8,128)S(1)}, f32[2,144,128]{2,1,0:T(8,128)}, u32[]{:S(2)}) copy-start(f32[2,144,128]{2,1,0:T(8,128)} %refs_4_.3) | copy-start | bytes 442372
  45.6 1.6 %collective-permute-start.2 = (f32[144,4,128]{2,1,0:T(4,128)S(1)}, f32[144,4,128]{2,1,0:T(4,128)S(1)}, u32[]{:S(2)}, u32[]{:S(2)}) collective-permute-start(f32[144,4,128]{2,1,0:T(4,128)S(1)} %get-tuple-element.19), channel_id=1, source_target_pairs={{0,1},{1,0},{2,3},{3,2},{4,5},{5,4},{6,7},{7,6},{8,9},{9,8},{10,11... | collective-permute-start | bytes 884744 | tf_op jit(solution)/shard_map/ppermute | solution.py:371

commit v9 on v7

--- a/solution.py
+++ b/solution.py
@@ -13,9 +13,18 @@
 ITERS = 2
 ROWS = 8
 LANES = 128
+BLOCKED = 2
 
 TOP_RANK = lax.Precision.HIGHEST
 PARAMS = pltpu.CompilerParams(vmem_limit_bytes=24 * 1024 * 1024)
+
+
+def each(count, step):
+    lax.fori_loop(0, count, lambda at, _: step(at), None)
+
+
+def eight(at):
+    return pl.ds(pl.multiple_of(at * ROWS, ROWS), ROWS)
 
 
 def spread_rows(target, base, row, source, first, count):
@@ -23,6 +32,15 @@
         size = min(ROWS, count - at)
         rows = pl.ds((base + at) * ROWS + row, size, stride=ROWS)
         target[rows, :] = source(first + at, size)
+
+
+def exchanged(shares):
+    parts, slabs = lax.axis_size("energy"), lax.axis_size("slab")
+    groups = [
+        [device * slabs + slab for device in range(parts)][:: -1 if slab % 2 else 1]
+        for slab in range(slabs)
+    ]
+    return lax.all_to_all(shares, ("energy", "slab"), 0, 0, axis_index_groups=groups)
 
 
 def index_neighbours(rows, offsets, lanes, is_near, inside):
@@ -41,63 +59,61 @@
         is_near[n // group, some, :] = jnp.broadcast_to(near[n : n + 1, :], (rows, atoms))
 
 
-def couple(rows, blocked, unroll, own, other, lanes, is_near, links, work, keep):
-    gathered_a, gathered_b, total = work
-    groups = NB * rows // ROWS
-    pairs = total.shape[0]
-    steps = NORB // blocked
+def couple(own, other, lanes, is_near, links, gathered_a, gathered_b, total):
+    groups, pairs = links.shape[:2]
+    steps = NORB // BLOCKED
     chunk = pairs // steps
-    buffers = (gathered_a, gathered_b)
-
-    def gather(g, first, count):
-        target = buffers[g % 2]
+
+    def gather(target, g, step):
         lane, mine = lanes[g], is_near[g] != 0
-        for at in range(count):
-            pair = first + at
-            rows_at = pl.ds(pl.multiple_of(pair * ROWS, ROWS), ROWS)
-            inner = jnp.take_along_axis(own[rows_at, :], lane, axis=1, mode="promise_in_bounds")
-            outer = jnp.take_along_axis(other[rows_at, :], lane, axis=1, mode="promise_in_bounds")
+        for at in range(chunk):
+            pair = step * chunk + at
+            inner = jnp.take_along_axis(own[eight(pair), :], lane, axis=1, mode="promise_in_bounds")
+            outer = jnp.take_along_axis(other[eight(pair), :], lane, axis=1, mode="promise_in_bounds")
             target[pair] = jnp.where(mine, inner, outer)
 
-    lax.fori_loop(0, steps, lambda step, _: gather(0, step * chunk, chunk), None)
-    for g in range(groups):
-        source = buffers[g % 2]
-
-        def block_row(step, _):
-            first = step * blocked
-            inner = [[None] * NORB for _ in range(blocked)]
+    def group_sums(g, source, target):
+        following = jnp.minimum(g + 1, groups - 1)
+
+        def block_row(step):
+            first = step * BLOCKED
+            inner = [[None] * NORB for _ in range(BLOCKED)]
             for j in range(NORB):
-                left = [links[g, (first + b) * NORB + j] for b in range(blocked)]
+                left = [links[g, (first + b) * NORB + j] for b in range(BLOCKED)]
                 for l in range(NORB):
                     value = source[j * NORB + l]
-                    for b in range(blocked):
+                    for b in range(BLOCKED):
                         term = left[b] * value
                         inner[b][l] = term if j == 0 else inner[b][l] + term
             for k in range(NORB):
-                sums = [None] * blocked
+                at = [(first + b) * NORB + k for b in range(BLOCKED)]
+                sums = [total[at[b]] for b in range(BLOCKED)]
                 for l in range(NORB):
                     right = links[g, k * NORB + l]
-                    for b in range(blocked):
-                        term = inner[b][l] * right
-                        sums[b] = term if l == 0 else sums[b] + term
-                for b in range(blocked):
-                    at = (first + b) * NORB + k
-                    value = sums[b] if g == 0 else total[at] + sums[b]
-                    if g < groups - 1:
-                        total[at] = value
-                    else:
-                        width = ROWS // 2
-                        while width >= rows:
-                            value = value + pltpu.roll(value, width, 0)
-                            width //= 2
-                        keep(at, value[:rows])
-            if g < groups - 1:
-                gather(g + 1, step * chunk, chunk)
-
-        lax.fori_loop(0, steps, block_row, None, unroll=unroll)
-
-
-def mix_weights(mixing, shifts, coupled, occupied):
+                    for b in range(BLOCKED):
+                        sums[b] = sums[b] + inner[b][l] * right
+                for b in range(BLOCKED):
+                    total[at[b]] = sums[b]
+            gather(target, following, step)
+
+        each(steps, block_row)
+
+    def clear(step):
+        for at in range(chunk):
+            total[step * chunk + at] = jnp.zeros(total.shape[1:], jnp.float32)
+        gather(gathered_a, 0, step)
+
+    def two_groups(half):
+        group_sums(half * 2, gathered_a, gathered_b)
+        group_sums(half * 2 + 1, gathered_b, gathered_a)
+
+    each(steps, clear)
+    each(groups // 2, two_groups)
+    if groups % 2:
+        group_sums(groups - 1, gathered_a, gathered_b)
+
+
+def mix_weights(mixing, energies, shifts, coupled, occupied):
     total = mixing.shape[1]
     lane = lax.broadcasted_iota(jnp.int32, (ROWS, LANES), 1)
     row = lax.broadcasted_iota(jnp.int32, (ROWS, LANES), 0)
@@ -112,7 +128,9 @@
     for at in range(0, total, ROWS):
         for first in range(0, total, LANES):
             width = min(LANES, total - first)
-            gap = lane + first - (row + at)
+            apart = (lane + first) // energies - (row + at) // energies
+            apart = jnp.where(lax.axis_index("slab") % 2 == 1, -apart, apart)
+            gap = apart * energies + (lane + first) % energies - (row + at) % energies
             far = jnp.minimum(jnp.abs(gap), LANES - 1)
             emit = jnp.take_along_axis(emitted, far, axis=1, mode="promise_in_bounds")
             absorb = jnp.take_along_axis(absorbed, far, axis=1, mode="promise_in_bounds")
@@ -154,7 +172,7 @@
         spread_rows(right, 0, row, read, 0, pairs)
     for copy in copies[3:7]:
         copy.wait()
-    mix_weights(mixing, shifts, coupled, occupied)
+    mix_weights(mixing, energies, shifts, coupled, occupied)
     index_neighbours(rows, offsets, lanes, is_near, inside)
     for n in range(NB):
         copies[7 + n].wait()
@@ -164,9 +182,10 @@
             spread_rows(links, n // group * pairs, n % group * rows + row, read, 0, pairs)
 
 
-def couple_kernel(rows, blocked, unroll, own, *refs):
+def couple_kernel(rows, own, *refs):
     far, (lanes, is_near, links, out, other, *work) = refs[:-8], refs[-8:]
     pairs = links.shape[1]
+    total = work[-1]
     if len(far) == 1:
         for pair in range(pairs):
             value = far[0][pair]
@@ -178,11 +197,14 @@
             source = far[row % rows // energies]
             read = lambda at, size: source[row % energies, at : at + size, :]
             spread_rows(other, 0, row, read, 0, pairs)
-
-    def keep(at, value):
-        out[at] = value
-
-    couple(rows, blocked, unroll, own, other, lanes, is_near, links, work, keep)
+    couple(own, other, lanes, is_near, links, *work)
+    for pair in range(pairs):
+        value = total[pair]
+        width = ROWS // 2
+        while width >= rows:
+            value = value + pltpu.roll(value, width, 0)
+            width //= 2
+        out[pair] = value[:rows]
     for at in range(pairs, out.shape[0]):
         out[at] = jnp.zeros(out.shape[1:], jnp.float32)
 
@@ -384,7 +406,7 @@
             )
             halos = [beside(compact)]
         (coupled,) = call(
-            functools.partial(couple_kernel, rows, *((3, 1) if step == 0 else (2, 2))),
+            functools.partial(couple_kernel, rows),
             [every],
             [held(*wide)] + [held(*deep)] * 3,
             NB * flops,
@@ -394,7 +416,7 @@
             is_near,
             links,
         )
-        gathered = lax.all_to_all(coupled.reshape(parts, share, rows, atoms), "energy", 0, 0)
+        gathered = exchanged(coupled.reshape(parts, share, rows, atoms))
         (mixed,) = call(
             functools.partial(mix_kernel, 2),
             [gathered.shape],
@@ -403,7 +425,7 @@
             mixing,
             gathered,
         )
-        sigma = lax.all_to_all(mixed, "energy", 0, 0).reshape(every)
+        sigma = exchanged(mixed).reshape(every)
     stages = -(-thin[0] // (ROWS * 2 * NORB))
     return call(
         dress_last_kernel,

time: 83.5 us -> 81.2 us (0.972)
  Pallas kernels: 20.1 us -> 18.4 us
    pallas_call x7, Pallas kernels: 20.1 us -> 18.4 us  [call(): pl.pallas_call(kernel, out_shape=shapes, in_specs=spaces or [vmem] * len(...]
where the time goes in v9:
time: 81.2 us; the launch traced here: 80.9 us
  blocking collectives  59.5 us (73%)
  Pallas kernels  18.4 us (23%)
  waiting for transfers between devices  1.57 us (2%)
    all_to_all x4, blocking collectives, exchanged(): lax.all_to_all(shares, ('energy', 'slab'), 0, 0, axis_index_groups=groups)  59.5 us
    pallas_call x7, Pallas kernels, call(): pl.pallas_call(kernel, out_shape=shapes, in_specs=spaces or [vmem] * len(...  18.4 us
  transfers between devices with their start and end apart: 3, of which 1 were waited for; matrix products, arithmetic and copies ran while one was open for 0% of the time, Pallas kernels for 3%

profile of v9, /device:TPU:0, one launch (start us, length us, event | category | flops | bytes accessed | tf_op | source)
XLA Modules:
  0.0 80.9 jit_solution(13003374239650841559)
XLA Ops:
  0.6 0.5 collective-permute-start
  1.1 0.1 collective-permute-start.1
  1.2 2.2 %shard_map.95 = (f32[1152,128]{1,0:T(8,128)S(1)}, f32[576,128]{1,0:T(8,128)S(1)}, f32[1152,128]{1,0:T(8,128)S(1)}, f32[2,32,32]{2,1,0:T(8,128)S(1)}, f32[6912,12...) custom-call(f32[2,144,128]{2,1,0:T(8,128)} %refs_3_.3, f32[2,144,128]{2,1,0:T(8,128)} %refs_4_.3, ...), custom_call_target="tpu_custom_call" | custom-call | flops 884736 | bytes 6404864 | tf_op jit(solution)/shard_map/pallas_call | solution.py:322
  3.4 0.0 collective-permute-done.refs_0_
  3.4 0.0 collective-permute-done.1.refs_1_
  3.4 6.7 %shard_map.96 = f32[144,4,128]{2,1,0:T(4,128)S(1)} custom-call(f32[1152,128]{1,0:T(8,128)S(1)} %get-tuple-element.12.own.free, f32[2,144,128]{2,1,0:T(8,128)S(1)} %collective-permute-done.refs_0_, f32[2,144,128]{2,1,0:T(8,128)S(1)} %collective-permute-done.1.refs_1_, s32[6,8,128]{2,1,0:T(8,128)S(1)} %get-tuple-element.13.refs_2_.refs_1_, ...), custom_call_target="tpu_custom_call" | custom-call | flops 42467328 | bytes 4767744 | tf_op jit(solution)/shard_map/pallas_call | solution.py:322
  10.1 16.8 %all_to_all.20.blocks = f32[16,9,4,128]{3,2,1,0:T(4,128)S(1)} all-to-all(f32[16,9,4,128]{3,2,1,0:T(4,128)S(1)} %bitcast.12), channel_id=1, replica_groups={{0,2,4,6,8,10,12,14,16,18,20,22,24,26,28,30},{31,29,27,25,23,21,19,17,1..., dimensions={0} | all-to-all | bytes 589824 | tf_op jit(solution)/shard_map/all_to_all | solution.py:43
  26.9 0.5 shard_map.97
  27.5 14.4 %all_to_all.21 = f32[16,9,4,128]{3,2,1,0:T(4,128)S(1)} all-to-all(f32[16,9,4,128]{3,2,1,0:T(4,128)S(1)} %shard_map.97), channel_id=1, replica_groups={{0,2,4,6,8,10,12,14,16,18,20,22,24,26,28,30},{31,29,27,25,23,21,19,17,1..., dimensions={0} | all-to-all | bytes 589824 | tf_op jit(solution)/shard_map/all_to_all | solution.py:43
  41.8 0.6 shard_map.98
  42.4 0.0 copy-start
  42.5 0.0 copy-start.1
  42.5 0.1 collective-permute-start.2
  42.5 1.6 %collective-permute-done.2.refs_0_ = f32[144,4,128]{2,1,0:T(4,128)S(1)} collective-permute-done((f32[144,4,128]{2,1,0:T(4,128)S(1)}, f32[144,4,128]{2,1,0:T(4,128)S(1)}, u32[]{:S(2)}, u32[]{:S(2)}) %collective-permute-start.2) | collective-permute-done | bytes 294944 | tf_op jit(solution)/shard_map/ppermute | solution.py:338
  44.1 6.6 %shard_map.99 = f32[144,4,128]{2,1,0:T(4,128)S(1)} custom-call(f32[1152,128]{1,0:T(8,128)S(1)} %get-tuple-element.18.own, f32[144,4,128]{2,1,0:T(4,128)S(1)} %collective-permute-done.2.refs_0_, s32[6,8,128]{2,1,0:T(8,128)S(1)} %get-tuple-element.13.refs_2_.refs_1_, s32[6,8,128]{2,1,0:T(8,128)S(1)} %get-tuple-element.14.refs_3_.refs_2_, ...), custom_call_target="tpu_custom_call" | custom-call | flops 42467328 | bytes 4767744 | tf_op jit(solution)/shard_map/pallas_call | solution.py:322
  50.7 13.6 %all_to_all.22.blocks = f32[16,9,4,128]{3,2,1,0:T(4,128)S(1)} all-to-all(f32[16,9,4,128]{3,2,1,0:T(4,128)S(1)} %bitcast.11), channel_id=1, replica_groups={{0,2,4,6,8,10,12,14,16,18,20,22,24,26,28,30},{31,29,27,25,23,21,19,17,1..., dimensions={0} | all-to-all | bytes 589824 | tf_op jit(solution)/shard_map/all_to_all | solution.py:43
  64.4 0.5 shard_map.100
  64.9 14.7 %all_to_all.23 = f32[16,9,4,128]{3,2,1,0:T(4,128)S(1)} all-to-all(f32[16,9,4,128]{3,2,1,0:T(4,128)S(1)} %shard_map.100), channel_id=1, replica_groups={{0,2,4,6,8,10,12,14,16,18,20,22,24,26,28,30},{31,29,27,25,23,21,19,17,1..., dimensions={0} | all-to-all | bytes 589824 | tf_op jit(solution)/shard_map/all_to_all | solution.py:43
  79.6 0.0 copy-done
  79.6 0.0 copy-done.1
  79.6 1.3 %shard_map.101 = (f32[2,144,128]{2,1,0:T(8,128)}, f32[2,144,128]{2,1,0:T(8,128)}) custom-call(f32[144,4,128]{2,1,0:T(4,128)S(1)} %bitcast.16, f32[72,8,128]{2,1,0:T(8,128)S(1)} %bitcast.15, f32[144,8,128]{2,1,0:T(8,128)S(1)} %bitcast.10, f32[2,144,128]{2,1,0:T(8,128)S(1)} %copy-done, f32[2,144,128]{2,1,0:T(8,128)S(1)} %copy-done.1), custom_call_target="tpu_custom_call" | custom-call | flops 3538944 | bytes 1769472 | tf_op jit(solution)/shard_map/pallas_call | solution.py:322
Async XLA Ops:
  0.6 2.8 %collective-permute-start = (f32[2,144,128]{2,1,0:T(8,128)}, f32[2,144,128]{2,1,0:T(8,128)S(1)}, u32[]{:S(2)}, u32[]{:S(2)}) collective-permute-start(f32[2,144,128]{2,1,0:T(8,128)} %refs_3_.3), channel_id=1, source_target_pairs={{0,1},{1,0},{2,3},{3,2},{4,5},{5,4},{6,7},{7,6},{8,9},{9,8},{10,11... | collective-permute-start | bytes 442376 | tf_op jit(solution)/shard_map/ppermute | solution.py:338
  1.1 2.3 %collective-permute-start.1 = (f32[2,144,128]{2,1,0:T(8,128)}, f32[2,144,128]{2,1,0:T(8,128)S(1)}, u32[]{:S(2)}, u32[]{:S(2)}) collective-permute-start(f32[2,144,128]{2,1,0:T(8,128)} %refs_4_.3), channel_id=1, source_target_pairs={{0,1},{1,0},{2,3},{3,2},{4,5},{5,4},{6,7},{7,6},{8,9},{9,8},{10,11... | collective-permute-start | bytes 442376 | tf_op jit(solution)/shard_map/ppermute | solution.py:338
  42.4 37.1 %copy-start = (f32[2,144,128]{2,1,0:T(8,128)S(1)}, f32[2,144,128]{2,1,0:T(8,128)}, u32[]{:S(2)}) copy-start(f32[2,144,128]{2,1,0:T(8,128)} %refs_3_.3) | copy-start | bytes 442372
  42.5 37.1 %copy-start.1 = (f32[2,144,128]{2,1,0:T(8,128)S(1)}, f32[2,144,128]{2,1,0:T(8,128)}, u32[]{:S(2)}) copy-start(f32[2,144,128]{2,1,0:T(8,128)} %refs_4_.3) | copy-start | bytes 442372
  42.5 1.6 %collective-permute-start.2 = (f32[144,4,128]{2,1,0:T(4,128)S(1)}, f32[144,4,128]{2,1,0:T(4,128)S(1)}, u32[]{:S(2)}, u32[]{:S(2)}) collective-permute-start(f32[144,4,128]{2,1,0:T(4,128)S(1)} %get-tuple-element.19), channel_id=1, source_target_pairs={{0,1},{1,0},{2,3},{3,2},{4,5},{5,4},{6,7},{7,6},{8,9},{9,8},{10,11... | collective-permute-start | bytes 884744 | tf_op jit(solution)/shard_map/ppermute | solution.py:338

commit v10 on v9

--- a/solution.py
+++ b/solution.py
@@ -1,4 +1,5 @@
 import functools
+import math
 
 import jax
 import jax.numpy as jnp
@@ -34,10 +35,17 @@
         target[rows, :] = source(first + at, size)
 
 
+def standing(place, parts, odd):
+    root = math.isqrt(parts)
+    root = root if parts % root == 0 else 1
+    place = place + odd * (parts - 1 - 2 * place)
+    return place % root * (parts // root) + place // root
+
+
 def exchanged(shares):
     parts, slabs = lax.axis_size("energy"), lax.axis_size("slab")
     groups = [
-        [device * slabs + slab for device in range(parts)][:: -1 if slab % 2 else 1]
+        [standing(place, parts, slab % 2) * slabs + slab for place in range(parts)]
         for slab in range(slabs)
     ]
     return lax.all_to_all(shares, ("energy", "slab"), 0, 0, axis_index_groups=groups)
@@ -115,6 +123,11 @@
 
 def mix_weights(mixing, energies, shifts, coupled, occupied):
     total = mixing.shape[1]
+    parts, odd = total // energies, lax.axis_index("slab") % 2
+
+    def energy_at(index):
+        return standing(index // energies, parts, odd) * energies + index % energies
+
     lane = lax.broadcasted_iota(jnp.int32, (ROWS, LANES), 1)
     row = lax.broadcasted_iota(jnp.int32, (ROWS, LANES), 0)
     emitted = jnp.zeros((ROWS, LANES), jnp.float32)
@@ -128,9 +141,7 @@
     for at in range(0, total, ROWS):
         for first in range(0, total, LANES):
             width = min(LANES, total - first)
-            apart = (lane + first) // energies - (row + at) // energies
-            apart = jnp.where(lax.axis_index("slab") % 2 == 1, -apart, apart)
-            gap = apart * energies + (lane + first) % energies - (row + at) % energies
+            gap = energy_at(lane + first) - energy_at(row + at)
             far = jnp.minimum(jnp.abs(gap), LANES - 1)
             emit = jnp.take_along_axis(emitted, far, axis=1, mode="promise_in_bounds")
             absorb = jnp.take_along_axis(absorbed, far, axis=1, mode="promise_in_bounds")

time: 81.2 us -> 80.5 us (level)
  no operation moved by 1% of the time
where the time goes in v10:
time: 80.5 us; the launch traced here: 80.2 us
  blocking collectives  58.8 us (73%)
  Pallas kernels  18.4 us (23%)
  waiting for transfers between devices  1.57 us (2%)
    all_to_all x4, blocking collectives, exchanged(): lax.all_to_all(shares, ('energy', 'slab'), 0, 0, axis_index_groups=groups)  58.8 us
    pallas_call x7, Pallas kernels, call(): pl.pallas_call(kernel, out_shape=shapes, in_specs=spaces or [vmem] * len(...  18.4 us
  transfers between devices with their start and end apart: 3, of which 1 were waited for; matrix products, arithmetic and copies ran while one was open for 0% of the time, Pallas kernels for 3%

profile of v10, /device:TPU:0, one launch (start us, length us, event | category | flops | bytes accessed | tf_op | source)
XLA Modules:
  0.0 80.2 jit_solution(3783072958629958491)
XLA Ops:
  0.6 0.5 collective-permute-start
  1.1 0.1 collective-permute-start.1
  1.2 2.2 %shard_map.95 = (f32[1152,128]{1,0:T(8,128)S(1)}, f32[576,128]{1,0:T(8,128)S(1)}, f32[1152,128]{1,0:T(8,128)S(1)}, f32[2,32,32]{2,1,0:T(8,128)S(1)}, f32[6912,12...) custom-call(f32[2,144,128]{2,1,0:T(8,128)} %refs_3_.3, f32[2,144,128]{2,1,0:T(8,128)} %refs_4_.3, ...), custom_call_target="tpu_custom_call" | custom-call | flops 884736 | bytes 6404864 | tf_op jit(solution)/shard_map/pallas_call | solution.py:333
  3.4 0.0 collective-permute-done.refs_0_
  3.4 0.0 collective-permute-done.1.refs_1_
  3.4 6.7 %shard_map.96 = f32[144,4,128]{2,1,0:T(4,128)S(1)} custom-call(f32[1152,128]{1,0:T(8,128)S(1)} %get-tuple-element.12.own.free, f32[2,144,128]{2,1,0:T(8,128)S(1)} %collective-permute-done.refs_0_, f32[2,144,128]{2,1,0:T(8,128)S(1)} %collective-permute-done.1.refs_1_, s32[6,8,128]{2,1,0:T(8,128)S(1)} %get-tuple-element.13.refs_2_.refs_1_, ...), custom_call_target="tpu_custom_call" | custom-call | flops 42467328 | bytes 4767744 | tf_op jit(solution)/shard_map/pallas_call | solution.py:333
  10.1 17.4 %all_to_all.20.blocks = f32[16,9,4,128]{3,2,1,0:T(4,128)S(1)} all-to-all(f32[16,9,4,128]{3,2,1,0:T(4,128)S(1)} %bitcast.12), channel_id=1, replica_groups={{0,8,16,24,2,10,18,26,4,12,20,28,6,14,22,30},{31,23,15,7,29,21,13,5,27,..., dimensions={0} | all-to-all | bytes 589824 | tf_op jit(solution)/shard_map/all_to_all | solution.py:51
  27.5 0.5 shard_map.97
  28.1 13.3 %all_to_all.21 = f32[16,9,4,128]{3,2,1,0:T(4,128)S(1)} all-to-all(f32[16,9,4,128]{3,2,1,0:T(4,128)S(1)} %shard_map.97), channel_id=1, replica_groups={{0,8,16,24,2,10,18,26,4,12,20,28,6,14,22,30},{31,23,15,7,29,21,13,5,27,..., dimensions={0} | all-to-all | bytes 589824 | tf_op jit(solution)/shard_map/all_to_all | solution.py:51
  41.4 0.6 shard_map.98
  42.0 0.0 copy-start
  42.0 0.0 copy-start.1
  42.0 0.1 collective-permute-start.2
  42.1 1.6 %collective-permute-done.2.refs_0_ = f32[144,4,128]{2,1,0:T(4,128)S(1)} collective-permute-done((f32[144,4,128]{2,1,0:T(4,128)S(1)}, f32[144,4,128]{2,1,0:T(4,128)S(1)}, u32[]{:S(2)}, u32[]{:S(2)}) %collective-permute-start.2) | collective-permute-done | bytes 294944 | tf_op jit(solution)/shard_map/ppermute | solution.py:349
  43.6 6.6 %shard_map.99 = f32[144,4,128]{2,1,0:T(4,128)S(1)} custom-call(f32[1152,128]{1,0:T(8,128)S(1)} %get-tuple-element.18.own, f32[144,4,128]{2,1,0:T(4,128)S(1)} %collective-permute-done.2.refs_0_, s32[6,8,128]{2,1,0:T(8,128)S(1)} %get-tuple-element.13.refs_2_.refs_1_, s32[6,8,128]{2,1,0:T(8,128)S(1)} %get-tuple-element.14.refs_3_.refs_2_, ...), custom_call_target="tpu_custom_call" | custom-call | flops 42467328 | bytes 4767744 | tf_op jit(solution)/shard_map/pallas_call | solution.py:333
  50.3 14.2 %all_to_all.22.blocks = f32[16,9,4,128]{3,2,1,0:T(4,128)S(1)} all-to-all(f32[16,9,4,128]{3,2,1,0:T(4,128)S(1)} %bitcast.11), channel_id=1, replica_groups={{0,8,16,24,2,10,18,26,4,12,20,28,6,14,22,30},{31,23,15,7,29,21,13,5,27,..., dimensions={0} | all-to-all | bytes 589824 | tf_op jit(solution)/shard_map/all_to_all | solution.py:51
  64.4 0.5 shard_map.100
  65.0 13.9 %all_to_all.23 = f32[16,9,4,128]{3,2,1,0:T(4,128)S(1)} all-to-all(f32[16,9,4,128]{3,2,1,0:T(4,128)S(1)} %shard_map.100), channel_id=1, replica_groups={{0,8,16,24,2,10,18,26,4,12,20,28,6,14,22,30},{31,23,15,7,29,21,13,5,27,..., dimensions={0} | all-to-all | bytes 589824 | tf_op jit(solution)/shard_map/all_to_all | solution.py:51
  78.9 0.0 copy-done
  78.9 0.0 copy-done.1
  78.9 1.3 %shard_map.101 = (f32[2,144,128]{2,1,0:T(8,128)}, f32[2,144,128]{2,1,0:T(8,128)}) custom-call(f32[144,4,128]{2,1,0:T(4,128)S(1)} %bitcast.16, f32[72,8,128]{2,1,0:T(8,128)S(1)} %bitcast.15, f32[144,8,128]{2,1,0:T(8,128)S(1)} %bitcast.10, f32[2,144,128]{2,1,0:T(8,128)S(1)} %copy-done, f32[2,144,128]{2,1,0:T(8,128)S(1)} %copy-done.1), custom_call_target="tpu_custom_call" | custom-call | flops 3538944 | bytes 1769472 | tf_op jit(solution)/shard_map/pallas_call | solution.py:333
Async XLA Ops:
  0.6 2.8 %collective-permute-start = (f32[2,144,128]{2,1,0:T(8,128)}, f32[2,144,128]{2,1,0:T(8,128)S(1)}, u32[]{:S(2)}, u32[]{:S(2)}) collective-permute-start(f32[2,144,128]{2,1,0:T(8,128)} %refs_3_.3), channel_id=1, source_target_pairs={{0,1},{1,0},{2,3},{3,2},{4,5},{5,4},{6,7},{7,6},{8,9},{9,8},{10,11... | collective-permute-start | bytes 442376 | tf_op jit(solution)/shard_map/ppermute | solution.py:349
  1.1 2.3 %collective-permute-start.1 = (f32[2,144,128]{2,1,0:T(8,128)}, f32[2,144,128]{2,1,0:T(8,128)S(1)}, u32[]{:S(2)}, u32[]{:S(2)}) collective-permute-start(f32[2,144,128]{2,1,0:T(8,128)} %refs_4_.3), channel_id=1, source_target_pairs={{0,1},{1,0},{2,3},{3,2},{4,5},{5,4},{6,7},{7,6},{8,9},{9,8},{10,11... | collective-permute-start | bytes 442376 | tf_op jit(solution)/shard_map/ppermute | solution.py:349
  42.0 37.0 %copy-start = (f32[2,144,128]{2,1,0:T(8,128)S(1)}, f32[2,144,128]{2,1,0:T(8,128)}, u32[]{:S(2)}) copy-start(f32[2,144,128]{2,1,0:T(8,128)} %refs_3_.3) | copy-start | bytes 442372
  42.0 36.9 %copy-start.1 = (f32[2,144,128]{2,1,0:T(8,128)S(1)}, f32[2,144,128]{2,1,0:T(8,128)}, u32[]{:S(2)}) copy-start(f32[2,144,128]{2,1,0:T(8,128)} %refs_4_.3) | copy-start | bytes 442372
  42.0 1.6 %collective-permute-start.2 = (f32[144,4,128]{2,1,0:T(4,128)S(1)}, f32[144,4,128]{2,1,0:T(4,128)S(1)}, u32[]{:S(2)}, u32[]{:S(2)}) collective-permute-start(f32[144,4,128]{2,1,0:T(4,128)S(1)} %get-tuple-element.19), channel_id=1, source_target_pairs={{0,1},{1,0},{2,3},{3,2},{4,5},{5,4},{6,7},{7,6},{8,9},{9,8},{10,11... | collective-permute-start | bytes 884744 | tf_op jit(solution)/shard_map/ppermute | solution.py:349

commit v11 on v10

--- a/solution.py
+++ b/solution.py
@@ -14,7 +14,7 @@
 ITERS = 2
 ROWS = 8
 LANES = 128
-BLOCKED = 2
+TALL, BROAD = 4, 6
 
 TOP_RANK = lax.Precision.HIGHEST
 PARAMS = pltpu.CompilerParams(vmem_limit_bytes=24 * 1024 * 1024)
@@ -67,58 +67,81 @@
         is_near[n // group, some, :] = jnp.broadcast_to(near[n : n + 1, :], (rows, atoms))
 
 
-def couple(own, other, lanes, is_near, links, gathered_a, gathered_b, total):
+def couple(own, other, lanes, is_near, links, gathered_a, gathered_b, inner_a, inner_b, total):
     groups, pairs = links.shape[:2]
-    steps = NORB // BLOCKED
+    across = NORB // BROAD
+    steps = NORB // TALL * across
     chunk = pairs // steps
+    gathered, inner = (gathered_a, gathered_b), (inner_a, inner_b)
 
     def gather(target, g, step):
         lane, mine = lanes[g], is_near[g] != 0
         for at in range(chunk):
             pair = step * chunk + at
-            inner = jnp.take_along_axis(own[eight(pair), :], lane, axis=1, mode="promise_in_bounds")
-            outer = jnp.take_along_axis(other[eight(pair), :], lane, axis=1, mode="promise_in_bounds")
-            target[pair] = jnp.where(mine, inner, outer)
-
-    def group_sums(g, source, target):
-        following = jnp.minimum(g + 1, groups - 1)
-
-        def block_row(step):
-            first = step * BLOCKED
-            inner = [[None] * NORB for _ in range(BLOCKED)]
-            for j in range(NORB):
-                left = [links[g, (first + b) * NORB + j] for b in range(BLOCKED)]
-                for l in range(NORB):
-                    value = source[j * NORB + l]
-                    for b in range(BLOCKED):
-                        term = left[b] * value
-                        inner[b][l] = term if j == 0 else inner[b][l] + term
-            for k in range(NORB):
-                at = [(first + b) * NORB + k for b in range(BLOCKED)]
-                sums = [total[at[b]] for b in range(BLOCKED)]
-                for l in range(NORB):
-                    right = links[g, k * NORB + l]
-                    for b in range(BLOCKED):
-                        sums[b] = sums[b] + inner[b][l] * right
-                for b in range(BLOCKED):
-                    total[at[b]] = sums[b]
-            gather(target, following, step)
-
-        each(steps, block_row)
+            near = jnp.take_along_axis(own[eight(pair), :], lane, axis=1, mode="promise_in_bounds")
+            far = jnp.take_along_axis(other[eight(pair), :], lane, axis=1, mode="promise_in_bounds")
+            target[pair] = jnp.where(mine, near, far)
+
+    def corner(step):
+        return step // across * TALL, step % across * BROAD
+
+    def left_stage(g, source, target, step):
+        top, side = corner(step)
+        sums = [[None] * BROAD for _ in range(TALL)]
+        for j in range(NORB):
+            left = [links[g, (top + i) * NORB + j] for i in range(TALL)]
+            right = [source[j * NORB + side + l] for l in range(BROAD)]
+            for i in range(TALL):
+                for l in range(BROAD):
+                    term = left[i] * right[l]
+                    sums[i][l] = term if j == 0 else sums[i][l] + term
+        for i in range(TALL):
+            for l in range(BROAD):
+                target[(top + i) * NORB + side + l] = sums[i][l]
+
+    def right_stage(g, source, step):
+        top, side = corner(step)
+        places = [[(top + i) * NORB + side + k for k in range(BROAD)] for i in range(TALL)]
+        sums = [[total[place] for place in row] for row in places]
+        for l in range(NORB):
+            left = [source[(top + i) * NORB + l] for i in range(TALL)]
+            right = [links[g, (side + k) * NORB + l] for k in range(BROAD)]
+            for i in range(TALL):
+                for k in range(BROAD):
+                    sums[i][k] = sums[i][k] + left[i] * right[k]
+        for i in range(TALL):
+            for k in range(BROAD):
+                total[places[i][k]] = sums[i][k]
 
     def clear(step):
         for at in range(chunk):
             total[step * chunk + at] = jnp.zeros(total.shape[1:], jnp.float32)
         gather(gathered_a, 0, step)
 
+    def first_group(step):
+        left_stage(0, gathered_a, inner_a, step)
+        gather(gathered_b, min(1, groups - 1), step)
+
+    def group_steps(g, odd):
+        following = jnp.minimum(g + 1, groups - 1)
+
+        def block(step):
+            right_stage(g - 1, inner[1 - odd], step)
+            left_stage(g, gathered[odd], inner[odd], step)
+            gather(gathered[1 - odd], following, step)
+
+        each(steps, block)
+
     def two_groups(half):
-        group_sums(half * 2, gathered_a, gathered_b)
-        group_sums(half * 2 + 1, gathered_b, gathered_a)
+        group_steps(half * 2 + 1, 1)
+        group_steps(half * 2 + 2, 0)
 
     each(steps, clear)
-    each(groups // 2, two_groups)
-    if groups % 2:
-        group_sums(groups - 1, gathered_a, gathered_b)
+    each(steps, first_group)
+    each((groups - 1) // 2, two_groups)
+    if groups % 2 == 0:
+        group_steps(groups - 1, 1)
+    each(steps, lambda step: right_stage(groups - 1, inner[(groups - 1) % 2], step))
 
 
 def mix_weights(mixing, energies, shifts, coupled, occupied):
@@ -159,8 +182,8 @@
     rows = 2 * energies
     group = ROWS // rows
     share = left.shape[0] // ROWS
-    moves = [(free_hbm[f], free.at[f]) for f in range(2)] + [(retarded_hbm, retarded)]
-    moves += list(zip(modes_hbm, (shifts, coupled, occupied))) + [(offsets_hbm, offsets)]
+    moves = list(zip(modes_hbm, (shifts, coupled, occupied))) + [(offsets_hbm, offsets)]
+    moves += [(free_hbm[f], free.at[f]) for f in range(2)] + [(retarded_hbm, retarded)]
     moves += [(coupling_hbm.at[n], coupling.at[n]) for n in range(NB)]
     copies = [
         pltpu.make_async_copy(source, target, sems.at[at])
@@ -169,22 +192,22 @@
     for copy in copies:
         copy.start()
 
-    copies[0].wait()
-    copies[1].wait()
+    for copy in copies[:4]:
+        copy.wait()
+    mix_weights(mixing, energies, shifts, coupled, occupied)
+    index_neighbours(rows, offsets, lanes, is_near, inside)
+    copies[4].wait()
+    copies[5].wait()
     for row in range(ROWS):
         function, energy = row % rows // energies, row % energies
         read = lambda at, size: free[function, energy, at : at + size, :]
         spread_rows(start, 0, row, read, 0, pairs)
-    copies[2].wait()
+    copies[6].wait()
     for row in range(ROWS):
         skipped = row // rows * share
         read = lambda at, size: retarded[row % energies, at : at + size, :]
         spread_rows(left, 0, row, read, skipped, share)
         spread_rows(right, 0, row, read, 0, pairs)
-    for copy in copies[3:7]:
-        copy.wait()
-    mix_weights(mixing, energies, shifts, coupled, occupied)
-    index_neighbours(rows, offsets, lanes, is_near, inside)
     for n in range(NB):
         copies[7 + n].wait()
         valid = inside[n : n + 1, :]
@@ -194,7 +217,7 @@
 
 
 def couple_kernel(rows, own, *refs):
-    far, (lanes, is_near, links, out, other, *work) = refs[:-8], refs[-8:]
+    far, (lanes, is_near, links, out, other, *work) = refs[:-10], refs[-10:]
     pairs = links.shape[1]
     total = work[-1]
     if len(far) == 1:
@@ -419,7 +442,7 @@
         (coupled,) = call(
             functools.partial(couple_kernel, rows),
             [every],
-            [held(*wide)] + [held(*deep)] * 3,
+            [held(*wide)] + [held(*deep)] * 5,
             NB * flops,
             own,
             *halos,

time: 80.5 us -> 81.7 us (1.015)
  Pallas kernels: 18.4 us -> 19.6 us
    pallas_call x7, Pallas kernels: 18.4 us -> 19.6 us  [call(): pl.pallas_call(kernel, out_shape=shapes, in_specs=spaces or [vmem] * len(...]
  transfers between devices with their start and end apart: 3 -> 3, of which waited for: 1 -> 1; matrix products, arithmetic and copies ran while one was open for 0% -> 0% of each run, Pallas kernels for 3% -> 2%
where the time goes in v11:
time: 81.7 us; the launch traced here: 81.4 us
  blocking collectives  58.8 us (72%)
  Pallas kernels  19.6 us (24%)
  waiting for transfers between devices  1.57 us (2%)
    all_to_all x4, blocking collectives, exchanged(): lax.all_to_all(shares, ('energy', 'slab'), 0, 0, axis_index_groups=groups)  58.8 us
    pallas_call x7, Pallas kernels, call(): pl.pallas_call(kernel, out_shape=shapes, in_specs=spaces or [vmem] * len(...  19.6 us
  transfers between devices with their start and end apart: 3, of which 1 were waited for; matrix products, arithmetic and copies ran while one was open for 0% of the time, Pallas kernels for 2%

profile of v11, /device:TPU:0, one launch (start us, length us, event | category | flops | bytes accessed | tf_op | source)
XLA Modules:
  0.0 81.4 jit_solution(18079494939392988301)
XLA Ops:
  0.6 0.5 collective-permute-start
  1.1 0.1 collective-permute-start.1
  1.2 1.9 %shard_map.95 = (f32[1152,128]{1,0:T(8,128)S(1)}, f32[576,128]{1,0:T(8,128)S(1)}, f32[1152,128]{1,0:T(8,128)S(1)}, f32[2,32,32]{2,1,0:T(8,128)S(1)}, f32[6912,12...) custom-call(f32[2,144,128]{2,1,0:T(8,128)} %refs_3_.3, f32[2,144,128]{2,1,0:T(8,128)} %refs_4_.3, ...), custom_call_target="tpu_custom_call" | custom-call | flops 884736 | bytes 6404864 | tf_op jit(solution)/shard_map/pallas_call | solution.py:356
  3.2 0.0 collective-permute-done.refs_0_
  3.2 0.0 collective-permute-done.1.refs_1_
  3.2 7.4 %shard_map.96 = f32[144,4,128]{2,1,0:T(4,128)S(1)} custom-call(f32[1152,128]{1,0:T(8,128)S(1)} %get-tuple-element.12.own.free, f32[2,144,128]{2,1,0:T(8,128)S(1)} %collective-permute-done.refs_0_, f32[2,144,128]{2,1,0:T(8,128)S(1)} %collective-permute-done.1.refs_1_, s32[6,8,128]{2,1,0:T(8,128)S(1)} %get-tuple-element.13.refs_2_.refs_1_, ...), custom_call_target="tpu_custom_call" | custom-call | flops 42467328 | bytes 4767744 | tf_op jit(solution)/shard_map/pallas_call | solution.py:356
  10.6 17.4 %all_to_all.20.blocks = f32[16,9,4,128]{3,2,1,0:T(4,128)S(1)} all-to-all(f32[16,9,4,128]{3,2,1,0:T(4,128)S(1)} %bitcast.12), channel_id=1, replica_groups={{0,8,16,24,2,10,18,26,4,12,20,28,6,14,22,30},{31,23,15,7,29,21,13,5,27,..., dimensions={0} | all-to-all | bytes 589824 | tf_op jit(solution)/shard_map/all_to_all | solution.py:51
  28.0 0.5 shard_map.97
  28.5 13.3 %all_to_all.21 = f32[16,9,4,128]{3,2,1,0:T(4,128)S(1)} all-to-all(f32[16,9,4,128]{3,2,1,0:T(4,128)S(1)} %shard_map.97), channel_id=1, replica_groups={{0,8,16,24,2,10,18,26,4,12,20,28,6,14,22,30},{31,23,15,7,29,21,13,5,27,..., dimensions={0} | all-to-all | bytes 589824 | tf_op jit(solution)/shard_map/all_to_all | solution.py:51
  41.8 0.6 shard_map.98
  42.5 0.0 copy-start
  42.5 0.0 copy-start.1
  42.5 0.1 collective-permute-start.2
  42.6 1.6 %collective-permute-done.2.refs_0_ = f32[144,4,128]{2,1,0:T(4,128)S(1)} collective-permute-done((f32[144,4,128]{2,1,0:T(4,128)S(1)}, f32[144,4,128]{2,1,0:T(4,128)S(1)}, u32[]{:S(2)}, u32[]{:S(2)}) %collective-permute-start.2) | collective-permute-done | bytes 294944 | tf_op jit(solution)/shard_map/ppermute | solution.py:372
  44.1 7.4 %shard_map.99 = f32[144,4,128]{2,1,0:T(4,128)S(1)} custom-call(f32[1152,128]{1,0:T(8,128)S(1)} %get-tuple-element.18.own, f32[144,4,128]{2,1,0:T(4,128)S(1)} %collective-permute-done.2.refs_0_, s32[6,8,128]{2,1,0:T(8,128)S(1)} %get-tuple-element.13.refs_2_.refs_1_, s32[6,8,128]{2,1,0:T(8,128)S(1)} %get-tuple-element.14.refs_3_.refs_2_, ...), custom_call_target="tpu_custom_call" | custom-call | flops 42467328 | bytes 4767744 | tf_op jit(solution)/shard_map/pallas_call | solution.py:356
  51.5 14.1 %all_to_all.22.blocks = f32[16,9,4,128]{3,2,1,0:T(4,128)S(1)} all-to-all(f32[16,9,4,128]{3,2,1,0:T(4,128)S(1)} %bitcast.11), channel_id=1, replica_groups={{0,8,16,24,2,10,18,26,4,12,20,28,6,14,22,30},{31,23,15,7,29,21,13,5,27,..., dimensions={0} | all-to-all | bytes 589824 | tf_op jit(solution)/shard_map/all_to_all | solution.py:51
  65.6 0.5 shard_map.100
  66.1 14.0 %all_to_all.23 = f32[16,9,4,128]{3,2,1,0:T(4,128)S(1)} all-to-all(f32[16,9,4,128]{3,2,1,0:T(4,128)S(1)} %shard_map.100), channel_id=1, replica_groups={{0,8,16,24,2,10,18,26,4,12,20,28,6,14,22,30},{31,23,15,7,29,21,13,5,27,..., dimensions={0} | all-to-all | bytes 589824 | tf_op jit(solution)/shard_map/all_to_all | solution.py:51
  80.1 0.0 copy-done
  80.1 0.0 copy-done.1
  80.1 1.3 %shard_map.101 = (f32[2,144,128]{2,1,0:T(8,128)}, f32[2,144,128]{2,1,0:T(8,128)}) custom-call(f32[144,4,128]{2,1,0:T(4,128)S(1)} %bitcast.16, f32[72,8,128]{2,1,0:T(8,128)S(1)} %bitcast.15, f32[144,8,128]{2,1,0:T(8,128)S(1)} %bitcast.10, f32[2,144,128]{2,1,0:T(8,128)S(1)} %copy-done, f32[2,144,128]{2,1,0:T(8,128)S(1)} %copy-done.1), custom_call_target="tpu_custom_call" | custom-call | flops 3538944 | bytes 1769472 | tf_op jit(solution)/shard_map/pallas_call | solution.py:356
Async XLA Ops:
  0.6 2.5 %collective-permute-start = (f32[2,144,128]{2,1,0:T(8,128)}, f32[2,144,128]{2,1,0:T(8,128)S(1)}, u32[]{:S(2)}, u32[]{:S(2)}) collective-permute-start(f32[2,144,128]{2,1,0:T(8,128)} %refs_3_.3), channel_id=1, source_target_pairs={{0,1},{1,0},{2,3},{3,2},{4,5},{5,4},{6,7},{7,6},{8,9},{9,8},{10,11... | collective-permute-start | bytes 442376 | tf_op jit(solution)/shard_map/ppermute | solution.py:372
  1.1 2.0 %collective-permute-start.1 = (f32[2,144,128]{2,1,0:T(8,128)}, f32[2,144,128]{2,1,0:T(8,128)S(1)}, u32[]{:S(2)}, u32[]{:S(2)}) collective-permute-start(f32[2,144,128]{2,1,0:T(8,128)} %refs_4_.3), channel_id=1, source_target_pairs={{0,1},{1,0},{2,3},{3,2},{4,5},{5,4},{6,7},{7,6},{8,9},{9,8},{10,11... | collective-permute-start | bytes 442376 | tf_op jit(solution)/shard_map/ppermute | solution.py:372
  42.5 37.6 %copy-start = (f32[2,144,128]{2,1,0:T(8,128)S(1)}, f32[2,144,128]{2,1,0:T(8,128)}, u32[]{:S(2)}) copy-start(f32[2,144,128]{2,1,0:T(8,128)} %refs_3_.3) | copy-start | bytes 442372
  42.5 37.6 %copy-start.1 = (f32[2,144,128]{2,1,0:T(8,128)S(1)}, f32[2,144,128]{2,1,0:T(8,128)}, u32[]{:S(2)}) copy-start(f32[2,144,128]{2,1,0:T(8,128)} %refs_4_.3) | copy-start | bytes 442372
  42.5 1.6 %collective-permute-start.2 = (f32[144,4,128]{2,1,0:T(4,128)S(1)}, f32[144,4,128]{2,1,0:T(4,128)S(1)}, u32[]{:S(2)}, u32[]{:S(2)}) collective-permute-start(f32[144,4,128]{2,1,0:T(4,128)S(1)} %get-tuple-element.19), channel_id=1, source_target_pairs={{0,1},{1,0},{2,3},{3,2},{4,5},{5,4},{6,7},{7,6},{8,9},{9,8},{10,11... | collective-permute-start | bytes 884744 | tf_op jit(solution)/shard_map/ppermute | solution.py:372

commit v12 on v10

--- a/solution.py
+++ b/solution.py
@@ -15,6 +15,7 @@
 ROWS = 8
 LANES = 128
 BLOCKED = 2
+BROAD = 6
 
 TOP_RANK = lax.Precision.HIGHEST
 PARAMS = pltpu.CompilerParams(vmem_limit_bytes=24 * 1024 * 1024)
@@ -93,15 +94,18 @@
                     for b in range(BLOCKED):
                         term = left[b] * value
                         inner[b][l] = term if j == 0 else inner[b][l] + term
-            for k in range(NORB):
-                at = [(first + b) * NORB + k for b in range(BLOCKED)]
-                sums = [total[at[b]] for b in range(BLOCKED)]
+            for side in range(0, NORB, BROAD):
+                at = [
+                    (b, (first + b) * NORB + k, k)
+                    for k in range(side, side + BROAD)
+                    for b in range(BLOCKED)
+                ]
+                sums = [total[place] for _, place, _ in at]
                 for l in range(NORB):
-                    right = links[g, k * NORB + l]
-                    for b in range(BLOCKED):
-                        sums[b] = sums[b] + inner[b][l] * right
-                for b in range(BLOCKED):
-                    total[at[b]] = sums[b]
+                    right = {k: links[g, k * NORB + l] for k in range(side, side + BROAD)}
+                    sums = [x + inner[b][l] * right[k] for x, (b, _, k) in zip(sums, at)]
+                for x, (_, place, _) in zip(sums, at):
+                    total[place] = x
             gather(target, following, step)
 
         each(steps, block_row)
@@ -122,11 +126,12 @@
 
 
 def mix_weights(mixing, energies, shifts, coupled, occupied):
-    total = mixing.shape[1]
-    parts, odd = total // energies, lax.axis_index("slab") % 2
+    total = mixing.shape[0]
+    rows = 2 * energies
+    parts, odd = total // rows, lax.axis_index("slab") % 2
 
     def energy_at(index):
-        return standing(index // energies, parts, odd) * energies + index % energies
+        return standing(index // rows, parts, odd) * energies + index % energies
 
     lane = lax.broadcasted_iota(jnp.int32, (ROWS, LANES), 1)
     row = lax.broadcasted_iota(jnp.int32, (ROWS, LANES), 0)
@@ -146,8 +151,10 @@
             emit = jnp.take_along_axis(emitted, far, axis=1, mode="promise_in_bounds")
             absorb = jnp.take_along_axis(absorbed, far, axis=1, mode="promise_in_bounds")
             some = slice(first, first + width)
-            mixing[0, at : at + ROWS, some] = jnp.where(gap > 0, emit, absorb)[:, :width]
-            mixing[1, at : at + ROWS, some] = jnp.where(gap > 0, absorb, emit)[:, :width]
+            function = (row + at) % rows // energies
+            weight = jnp.where((gap > 0) == (function == 0), emit, absorb)
+            weight = jnp.where((lane + first) % rows // energies == function, weight, 0.0)
+            mixing[at : at + ROWS, some] = weight[:, :width]
 
 
 def prep_kernel(*refs):
@@ -159,8 +166,8 @@
     rows = 2 * energies
     group = ROWS // rows
     share = left.shape[0] // ROWS
-    moves = [(free_hbm[f], free.at[f]) for f in range(2)] + [(retarded_hbm, retarded)]
-    moves += list(zip(modes_hbm, (shifts, coupled, occupied))) + [(offsets_hbm, offsets)]
+    moves = list(zip(modes_hbm, (shifts, coupled, occupied))) + [(offsets_hbm, offsets)]
+    moves += [(free_hbm[f], free.at[f]) for f in range(2)] + [(retarded_hbm, retarded)]
     moves += [(coupling_hbm.at[n], coupling.at[n]) for n in range(NB)]
     copies = [
         pltpu.make_async_copy(source, target, sems.at[at])
@@ -169,22 +176,22 @@
     for copy in copies:
         copy.start()
 
-    copies[0].wait()
-    copies[1].wait()
+    for copy in copies[:4]:
+        copy.wait()
+    mix_weights(mixing, energies, shifts, coupled, occupied)
+    index_neighbours(rows, offsets, lanes, is_near, inside)
+    copies[4].wait()
+    copies[5].wait()
     for row in range(ROWS):
         function, energy = row % rows // energies, row % energies
         read = lambda at, size: free[function, energy, at : at + size, :]
         spread_rows(start, 0, row, read, 0, pairs)
-    copies[2].wait()
+    copies[6].wait()
     for row in range(ROWS):
         skipped = row // rows * share
         read = lambda at, size: retarded[row % energies, at : at + size, :]
         spread_rows(left, 0, row, read, skipped, share)
         spread_rows(right, 0, row, read, 0, pairs)
-    for copy in copies[3:7]:
-        copy.wait()
-    mix_weights(mixing, energies, shifts, coupled, occupied)
-    index_neighbours(rows, offsets, lanes, is_near, inside)
     for n in range(NB):
         copies[7 + n].wait()
         valid = inside[n : n + 1, :]
@@ -220,24 +227,19 @@
         out[at] = jnp.zeros(out.shape[1:], jnp.float32)
 
 
-def mix_kernel(fused, mixing, blocks, out, before, after):
+def mix_kernel(mixing, blocks, out, before, after):
     parts, share, rows, atoms = blocks.shape
-    energies = rows // fused
-    for f in range(fused):
-        some = slice(f * energies, (f + 1) * energies)
-        for part in range(parts):
-            for pair in range(share):
-                before[part * energies : (part + 1) * energies, pair * atoms : (pair + 1) * atoms] = (
-                    blocks[part, pair, some, :]
-                )
-        after[...] = jnp.dot(
-            mixing[f], before[...], precision=TOP_RANK, preferred_element_type=jnp.float32
-        )
-        for part in range(parts):
-            for pair in range(share):
-                out[part, pair, some, :] = after[
-                    part * energies : (part + 1) * energies, pair * atoms : (pair + 1) * atoms
-                ]
+    for part in range(parts):
+        for pair in range(share):
+            lanes = slice(pair * atoms, (pair + 1) * atoms)
+            before[part * rows : (part + 1) * rows, lanes] = blocks[part, pair]
+    after[...] = jnp.dot(
+        mixing[...], before[...], precision=TOP_RANK, preferred_element_type=jnp.float32
+    )
+    for part in range(parts):
+        for pair in range(share):
+            lanes = slice(pair * atoms, (pair + 1) * atoms)
+            out[part, pair] = after[part * rows : (part + 1) * rows, lanes]
 
 
 def dress(rows, sigma, left, right, copied, keep):
@@ -372,7 +374,7 @@
     groups = NB * rows // ROWS
     parts = lax.axis_size("energy")
     share = -(-pairs // parts)
-    total = energies * parts
+    total = rows * parts
     away = pl.BlockSpec(memory_space=pltpu.HBM)
     held = lambda *dims: pltpu.VMEM(dims, jnp.float32)
     wide = (pairs * ROWS, atoms)
@@ -389,7 +391,7 @@
     constants = (retarded, *phonons, neighbour_offsets, coupling)
     own, left, right, mixing, links, lanes, is_near = call(
         prep_kernel,
-        [wide, thin, wide, (2, total, total), (groups * wide[0], atoms), index, index],
+        [wide, thin, wide, (total, total), (groups * wide[0], atoms), index, index],
         [held(2, *retarded.shape), held(*retarded.shape)]
         + [pltpu.SMEM(x.shape, x.dtype) for x in phonons]
         + [pltpu.VMEM(neighbour_offsets.shape, jnp.int32)]
@@ -429,7 +431,7 @@
         )
         gathered = exchanged(coupled.reshape(parts, share, rows, atoms))
         (mixed,) = call(
-            functools.partial(mix_kernel, 2),
+            mix_kernel,
             [gathered.shape],
             [held(total, share * atoms)] * 2,
             2 * total * gathered.size,

time: 80.5 us -> 80.2 us (level)
  transfers between devices with their start and end apart: 3 -> 3, of which waited for: 1 -> 1; matrix products, arithmetic and copies ran while one was open for 0% -> 0% of each run, Pallas kernels for 3% -> 2%
where the time goes in v12:
time: 80.2 us; the launch traced here: 79.9 us
  blocking collectives  58.8 us (73%)
  Pallas kernels  18.1 us (23%)
  waiting for transfers between devices  1.57 us (2%)
    all_to_all x4, blocking collectives, exchanged(): lax.all_to_all(shares, ('energy', 'slab'), 0, 0, axis_index_groups=groups)  58.8 us
    pallas_call x7, Pallas kernels, call(): pl.pallas_call(kernel, out_shape=shapes, in_specs=spaces or [vmem] * len(...  18.1 us
  transfers between devices with their start and end apart: 3, of which 1 were waited for; matrix products, arithmetic and copies ran while one was open for 0% of the time, Pallas kernels for 2%

profile of v12, /device:TPU:0, one launch (start us, length us, event | category | flops | bytes accessed | tf_op | source)
XLA Modules:
  0.0 79.9 jit_solution(4278470249128371162)
XLA Ops:
  0.6 0.5 collective-permute-start
  1.1 0.1 collective-permute-start.1
  1.2 1.9 %shard_map.95 = (f32[1152,128]{1,0:T(8,128)S(1)}, f32[576,128]{1,0:T(8,128)S(1)}, f32[1152,128]{1,0:T(8,128)S(1)}, f32[64,64]{1,0:T(8,128)S(1)}, f32[6912,128]{1...) custom-call(f32[2,144,128]{2,1,0:T(8,128)} %refs_3_.3, f32[2,144,128]{2,1,0:T(8,128)} %refs_4_.3, ...), custom_call_target="tpu_custom_call" | custom-call | flops 884736 | bytes 6413056 | tf_op jit(solution)/shard_map/pallas_call | solution.py:335
  3.2 0.0 collective-permute-done.refs_0_
  3.2 0.0 collective-permute-done.1.refs_1_
  3.2 6.7 %shard_map.96 = f32[144,4,128]{2,1,0:T(4,128)S(1)} custom-call(f32[1152,128]{1,0:T(8,128)S(1)} %get-tuple-element.12.own.free, f32[2,144,128]{2,1,0:T(8,128)S(1)} %collective-permute-done.refs_0_, f32[2,144,128]{2,1,0:T(8,128)S(1)} %collective-permute-done.1.refs_1_, s32[6,8,128]{2,1,0:T(8,128)S(1)} %get-tuple-element.13.refs_2_.refs_1_, ...), custom_call_target="tpu_custom_call" | custom-call | flops 42467328 | bytes 4767744 | tf_op jit(solution)/shard_map/pallas_call | solution.py:335
  9.9 17.4 %all_to_all.20.blocks = f32[16,9,4,128]{3,2,1,0:T(4,128)S(1)} all-to-all(f32[16,9,4,128]{3,2,1,0:T(4,128)S(1)} %bitcast.12), channel_id=1, replica_groups={{0,8,16,24,2,10,18,26,4,12,20,28,6,14,22,30},{31,23,15,7,29,21,13,5,27,..., dimensions={0} | all-to-all | bytes 589824 | tf_op jit(solution)/shard_map/all_to_all | solution.py:52
  27.3 0.4 shard_map.97
  27.8 13.3 %all_to_all.21 = f32[16,9,4,128]{3,2,1,0:T(4,128)S(1)} all-to-all(f32[16,9,4,128]{3,2,1,0:T(4,128)S(1)} %shard_map.97), channel_id=1, replica_groups={{0,8,16,24,2,10,18,26,4,12,20,28,6,14,22,30},{31,23,15,7,29,21,13,5,27,..., dimensions={0} | all-to-all | bytes 589824 | tf_op jit(solution)/shard_map/all_to_all | solution.py:52
  41.1 0.6 shard_map.98
  41.7 0.0 copy-start
  41.7 0.0 copy-start.1
  41.7 0.1 collective-permute-start.2
  41.8 1.6 %collective-permute-done.2.refs_0_ = f32[144,4,128]{2,1,0:T(4,128)S(1)} collective-permute-done((f32[144,4,128]{2,1,0:T(4,128)S(1)}, f32[144,4,128]{2,1,0:T(4,128)S(1)}, u32[]{:S(2)}, u32[]{:S(2)}) %collective-permute-start.2) | collective-permute-done | bytes 294944 | tf_op jit(solution)/shard_map/ppermute | solution.py:351
  43.4 6.7 %shard_map.99 = f32[144,4,128]{2,1,0:T(4,128)S(1)} custom-call(f32[1152,128]{1,0:T(8,128)S(1)} %get-tuple-element.18.own, f32[144,4,128]{2,1,0:T(4,128)S(1)} %collective-permute-done.2.refs_0_, s32[6,8,128]{2,1,0:T(8,128)S(1)} %get-tuple-element.13.refs_2_.refs_1_, s32[6,8,128]{2,1,0:T(8,128)S(1)} %get-tuple-element.14.refs_3_.refs_2_, ...), custom_call_target="tpu_custom_call" | custom-call | flops 42467328 | bytes 4767744 | tf_op jit(solution)/shard_map/pallas_call | solution.py:335
  50.0 14.2 %all_to_all.22.blocks = f32[16,9,4,128]{3,2,1,0:T(4,128)S(1)} all-to-all(f32[16,9,4,128]{3,2,1,0:T(4,128)S(1)} %bitcast.11), channel_id=1, replica_groups={{0,8,16,24,2,10,18,26,4,12,20,28,6,14,22,30},{31,23,15,7,29,21,13,5,27,..., dimensions={0} | all-to-all | bytes 589824 | tf_op jit(solution)/shard_map/all_to_all | solution.py:52
  64.2 0.4 shard_map.100
  64.6 13.9 %all_to_all.23 = f32[16,9,4,128]{3,2,1,0:T(4,128)S(1)} all-to-all(f32[16,9,4,128]{3,2,1,0:T(4,128)S(1)} %shard_map.100), channel_id=1, replica_groups={{0,8,16,24,2,10,18,26,4,12,20,28,6,14,22,30},{31,23,15,7,29,21,13,5,27,..., dimensions={0} | all-to-all | bytes 589824 | tf_op jit(solution)/shard_map/all_to_all | solution.py:52
  78.6 0.0 copy-done
  78.6 0.0 copy-done.1
  78.6 1.3 %shard_map.101 = (f32[2,144,128]{2,1,0:T(8,128)}, f32[2,144,128]{2,1,0:T(8,128)}) custom-call(f32[144,4,128]{2,1,0:T(4,128)S(1)} %bitcast.16, f32[72,8,128]{2,1,0:T(8,128)S(1)} %bitcast.15, f32[144,8,128]{2,1,0:T(8,128)S(1)} %bitcast.10, f32[2,144,128]{2,1,0:T(8,128)S(1)} %copy-done, f32[2,144,128]{2,1,0:T(8,128)S(1)} %copy-done.1), custom_call_target="tpu_custom_call" | custom-call | flops 3538944 | bytes 1769472 | tf_op jit(solution)/shard_map/pallas_call | solution.py:335
Async XLA Ops:
  0.6 2.5 %collective-permute-start = (f32[2,144,128]{2,1,0:T(8,128)}, f32[2,144,128]{2,1,0:T(8,128)S(1)}, u32[]{:S(2)}, u32[]{:S(2)}) collective-permute-start(f32[2,144,128]{2,1,0:T(8,128)} %refs_3_.3), channel_id=1, source_target_pairs={{0,1},{1,0},{2,3},{3,2},{4,5},{5,4},{6,7},{7,6},{8,9},{9,8},{10,11... | collective-permute-start | bytes 442376 | tf_op jit(solution)/shard_map/ppermute | solution.py:351
  1.1 2.0 %collective-permute-start.1 = (f32[2,144,128]{2,1,0:T(8,128)}, f32[2,144,128]{2,1,0:T(8,128)S(1)}, u32[]{:S(2)}, u32[]{:S(2)}) collective-permute-start(f32[2,144,128]{2,1,0:T(8,128)} %refs_4_.3), channel_id=1, source_target_pairs={{0,1},{1,0},{2,3},{3,2},{4,5},{5,4},{6,7},{7,6},{8,9},{9,8},{10,11... | collective-permute-start | bytes 442376 | tf_op jit(solution)/shard_map/ppermute | solution.py:351
  41.7 36.9 %copy-start = (f32[2,144,128]{2,1,0:T(8,128)S(1)}, f32[2,144,128]{2,1,0:T(8,128)}, u32[]{:S(2)}) copy-start(f32[2,144,128]{2,1,0:T(8,128)} %refs_3_.3) | copy-start | bytes 442372
  41.7 36.9 %copy-start.1 = (f32[2,144,128]{2,1,0:T(8,128)S(1)}, f32[2,144,128]{2,1,0:T(8,128)}, u32[]{:S(2)}) copy-start(f32[2,144,128]{2,1,0:T(8,128)} %refs_4_.3) | copy-start | bytes 442372
  41.7 1.6 %collective-permute-start.2 = (f32[144,4,128]{2,1,0:T(4,128)S(1)}, f32[144,4,128]{2,1,0:T(4,128)S(1)}, u32[]{:S(2)}, u32[]{:S(2)}) collective-permute-start(f32[144,4,128]{2,1,0:T(4,128)S(1)} %get-tuple-element.19), channel_id=1, source_target_pairs={{0,1},{1,0},{2,3},{3,2},{4,5},{5,4},{6,7},{7,6},{8,9},{9,8},{10,11... | collective-permute-start | bytes 884744 | tf_op jit(solution)/shard_map/ppermute | solution.py:351

commit v13 on v12

--- a/solution.py
+++ b/solution.py
@@ -36,17 +36,16 @@
         target[rows, :] = source(first + at, size)
 
 
-def standing(place, parts, odd):
+def standing(place, parts):
     root = math.isqrt(parts)
     root = root if parts % root == 0 else 1
-    place = place + odd * (parts - 1 - 2 * place)
     return place % root * (parts // root) + place // root
 
 
 def exchanged(shares):
     parts, slabs = lax.axis_size("energy"), lax.axis_size("slab")
     groups = [
-        [standing(place, parts, slab % 2) * slabs + slab for place in range(parts)]
+        [standing(place, parts) * slabs + slab for place in range(parts)]
         for slab in range(slabs)
     ]
     return lax.all_to_all(shares, ("energy", "slab"), 0, 0, axis_index_groups=groups)
@@ -128,10 +127,10 @@
 def mix_weights(mixing, energies, shifts, coupled, occupied):
     total = mixing.shape[0]
     rows = 2 * energies
-    parts, odd = total // rows, lax.axis_index("slab") % 2
+    parts = total // rows
 
     def energy_at(index):
-        return standing(index // rows, parts, odd) * energies + index % energies
+        return standing(index // rows, parts) * energies + index % energies
 
     lane = lax.broadcasted_iota(jnp.int32, (ROWS, LANES), 1)
     row = lax.broadcasted_iota(jnp.int32, (ROWS, LANES), 0)

time: 80.2 us -> 82.6 us (1.030)
  blocking collectives: 58.8 us -> 61.3 us
    all_to_all x4, blocking collectives: 58.8 us -> 61.3 us  [exchanged(): lax.all_to_all(shares, ('energy', 'slab'), 0, 0, axis_index_groups=groups)]
where the time goes in v13:
time: 82.6 us; the launch traced here: 82.3 us
  blocking collectives  61.3 us (74%)
  Pallas kernels  18.1 us (22%)
  waiting for transfers between devices  1.57 us (2%)
    all_to_all x4, blocking collectives, exchanged(): lax.all_to_all(shares, ('energy', 'slab'), 0, 0, axis_index_groups=groups)  61.3 us
    pallas_call x7, Pallas kernels, call(): pl.pallas_call(kernel, out_shape=shapes, in_specs=spaces or [vmem] * len(...  18.1 us
  transfers between devices with their start and end apart: 3, of which 1 were waited for; matrix products, arithmetic and copies ran while one was open for 0% of the time, Pallas kernels for 2%

profile of v13, /device:TPU:0, one launch (start us, length us, event | category | flops | bytes accessed | tf_op | source)
XLA Modules:
  0.0 82.3 jit_solution(2264121440135518573)
XLA Ops:
  0.6 0.5 collective-permute-start
  1.1 0.1 collective-permute-start.1
  1.2 1.9 %shard_map.95 = (f32[1152,128]{1,0:T(8,128)S(1)}, f32[576,128]{1,0:T(8,128)S(1)}, f32[1152,128]{1,0:T(8,128)S(1)}, f32[64,64]{1,0:T(8,128)S(1)}, f32[6912,128]{1...) custom-call(f32[2,144,128]{2,1,0:T(8,128)} %refs_3_.3, f32[2,144,128]{2,1,0:T(8,128)} %refs_4_.3, ...), custom_call_target="tpu_custom_call" | custom-call | flops 884736 | bytes 6413056 | tf_op jit(solution)/shard_map/pallas_call | solution.py:334
  3.2 0.0 collective-permute-done.refs_0_
  3.2 0.0 collective-permute-done.1.refs_1_
  3.2 6.7 %shard_map.96 = f32[144,4,128]{2,1,0:T(4,128)S(1)} custom-call(f32[1152,128]{1,0:T(8,128)S(1)} %get-tuple-element.12.own.free, f32[2,144,128]{2,1,0:T(8,128)S(1)} %collective-permute-done.refs_0_, f32[2,144,128]{2,1,0:T(8,128)S(1)} %collective-permute-done.1.refs_1_, s32[6,8,128]{2,1,0:T(8,128)S(1)} %get-tuple-element.13.refs_2_.refs_1_, ...), custom_call_target="tpu_custom_call" | custom-call | flops 42467328 | bytes 4767744 | tf_op jit(solution)/shard_map/pallas_call | solution.py:334
  9.9 19.6 %all_to_all.20.blocks = f32[16,9,4,128]{3,2,1,0:T(4,128)S(1)} all-to-all(f32[16,9,4,128]{3,2,1,0:T(4,128)S(1)} %bitcast.12), channel_id=1, replica_groups={{0,8,16,24,2,10,18,26,4,12,20,28,6,14,22,30},{1,9,17,25,3,11,19,27,5,13..., dimensions={0} | all-to-all | bytes 589824 | tf_op jit(solution)/shard_map/all_to_all | solution.py:51
  29.5 0.4 shard_map.97
  30.0 13.5 %all_to_all.21 = f32[16,9,4,128]{3,2,1,0:T(4,128)S(1)} all-to-all(f32[16,9,4,128]{3,2,1,0:T(4,128)S(1)} %shard_map.97), channel_id=1, replica_groups={{0,8,16,24,2,10,18,26,4,12,20,28,6,14,22,30},{1,9,17,25,3,11,19,27,5,13..., dimensions={0} | all-to-all | bytes 589824 | tf_op jit(solution)/shard_map/all_to_all | solution.py:51
  43.5 0.6 shard_map.98
  44.1 0.0 copy-start
  44.1 0.0 copy-start.1
  44.1 0.1 collective-permute-start.2
  44.2 1.6 %collective-permute-done.2.refs_0_ = f32[144,4,128]{2,1,0:T(4,128)S(1)} collective-permute-done((f32[144,4,128]{2,1,0:T(4,128)S(1)}, f32[144,4,128]{2,1,0:T(4,128)S(1)}, u32[]{:S(2)}, u32[]{:S(2)}) %collective-permute-start.2) | collective-permute-done | bytes 294944 | tf_op jit(solution)/shard_map/ppermute | solution.py:350
  45.7 6.7 %shard_map.99 = f32[144,4,128]{2,1,0:T(4,128)S(1)} custom-call(f32[1152,128]{1,0:T(8,128)S(1)} %get-tuple-element.18.own, f32[144,4,128]{2,1,0:T(4,128)S(1)} %collective-permute-done.2.refs_0_, s32[6,8,128]{2,1,0:T(8,128)S(1)} %get-tuple-element.13.refs_2_.refs_1_, s32[6,8,128]{2,1,0:T(8,128)S(1)} %get-tuple-element.14.refs_3_.refs_2_, ...), custom_call_target="tpu_custom_call" | custom-call | flops 42467328 | bytes 4767744 | tf_op jit(solution)/shard_map/pallas_call | solution.py:334
  52.4 14.5 %all_to_all.22.blocks = f32[16,9,4,128]{3,2,1,0:T(4,128)S(1)} all-to-all(f32[16,9,4,128]{3,2,1,0:T(4,128)S(1)} %bitcast.11), channel_id=1, replica_groups={{0,8,16,24,2,10,18,26,4,12,20,28,6,14,22,30},{1,9,17,25,3,11,19,27,5,13..., dimensions={0} | all-to-all | bytes 589824 | tf_op jit(solution)/shard_map/all_to_all | solution.py:51
  66.9 0.4 shard_map.100
  67.3 13.7 %all_to_all.23 = f32[16,9,4,128]{3,2,1,0:T(4,128)S(1)} all-to-all(f32[16,9,4,128]{3,2,1,0:T(4,128)S(1)} %shard_map.100), channel_id=1, replica_groups={{0,8,16,24,2,10,18,26,4,12,20,28,6,14,22,30},{1,9,17,25,3,11,19,27,5,13..., dimensions={0} | all-to-all | bytes 589824 | tf_op jit(solution)/shard_map/all_to_all | solution.py:51
  81.0 0.0 copy-done
  81.0 0.0 copy-done.1
  81.0 1.3 %shard_map.101 = (f32[2,144,128]{2,1,0:T(8,128)}, f32[2,144,128]{2,1,0:T(8,128)}) custom-call(f32[144,4,128]{2,1,0:T(4,128)S(1)} %bitcast.16, f32[72,8,128]{2,1,0:T(8,128)S(1)} %bitcast.15, f32[144,8,128]{2,1,0:T(8,128)S(1)} %bitcast.10, f32[2,144,128]{2,1,0:T(8,128)S(1)} %copy-done, f32[2,144,128]{2,1,0:T(8,128)S(1)} %copy-done.1), custom_call_target="tpu_custom_call" | custom-call | flops 3538944 | bytes 1769472 | tf_op jit(solution)/shard_map/pallas_call | solution.py:334
Async XLA Ops:
  0.6 2.5 %collective-permute-start = (f32[2,144,128]{2,1,0:T(8,128)}, f32[2,144,128]{2,1,0:T(8,128)S(1)}, u32[]{:S(2)}, u32[]{:S(2)}) collective-permute-start(f32[2,144,128]{2,1,0:T(8,128)} %refs_3_.3), channel_id=1, source_target_pairs={{0,1},{1,0},{2,3},{3,2},{4,5},{5,4},{6,7},{7,6},{8,9},{9,8},{10,11... | collective-permute-start | bytes 442376 | tf_op jit(solution)/shard_map/ppermute | solution.py:350
  1.1 2.0 %collective-permute-start.1 = (f32[2,144,128]{2,1,0:T(8,128)}, f32[2,144,128]{2,1,0:T(8,128)S(1)}, u32[]{:S(2)}, u32[]{:S(2)}) collective-permute-start(f32[2,144,128]{2,1,0:T(8,128)} %refs_4_.3), channel_id=1, source_target_pairs={{0,1},{1,0},{2,3},{3,2},{4,5},{5,4},{6,7},{7,6},{8,9},{9,8},{10,11... | collective-permute-start | bytes 442376 | tf_op jit(solution)/shard_map/ppermute | solution.py:350
  44.1 36.9 %copy-start = (f32[2,144,128]{2,1,0:T(8,128)S(1)}, f32[2,144,128]{2,1,0:T(8,128)}, u32[]{:S(2)}) copy-start(f32[2,144,128]{2,1,0:T(8,128)} %refs_3_.3) | copy-start | bytes 442372
  44.1 36.9 %copy-start.1 = (f32[2,144,128]{2,1,0:T(8,128)S(1)}, f32[2,144,128]{2,1,0:T(8,128)}, u32[]{:S(2)}) copy-start(f32[2,144,128]{2,1,0:T(8,128)} %refs_4_.3) | copy-start | bytes 442372
  44.1 1.6 %collective-permute-start.2 = (f32[144,4,128]{2,1,0:T(4,128)S(1)}, f32[144,4,128]{2,1,0:T(4,128)S(1)}, u32[]{:S(2)}, u32[]{:S(2)}) collective-permute-start(f32[144,4,128]{2,1,0:T(4,128)S(1)} %get-tuple-element.19), channel_id=1, source_target_pairs={{0,1},{1,0},{2,3},{3,2},{4,5},{5,4},{6,7},{7,6},{8,9},{9,8},{10,11... | collective-permute-start | bytes 884744 | tf_op jit(solution)/shard_map/ppermute | solution.py:350

commit v14 on v13

--- a/solution.py
+++ b/solution.py
@@ -36,16 +36,17 @@
         target[rows, :] = source(first + at, size)
 
 
-def standing(place, parts):
+def standing(place, parts, even):
     root = math.isqrt(parts)
     root = root if parts % root == 0 else 1
+    place = place + even * (parts - 1 - 2 * place)
     return place % root * (parts // root) + place // root
 
 
 def exchanged(shares):
     parts, slabs = lax.axis_size("energy"), lax.axis_size("slab")
     groups = [
-        [standing(place, parts) * slabs + slab for place in range(parts)]
+        [standing(place, parts, 1 - slab % 2) * slabs + slab for place in range(parts)]
         for slab in range(slabs)
     ]
     return lax.all_to_all(shares, ("energy", "slab"), 0, 0, axis_index_groups=groups)
@@ -127,10 +128,10 @@
 def mix_weights(mixing, energies, shifts, coupled, occupied):
     total = mixing.shape[0]
     rows = 2 * energies
-    parts = total // rows
+    parts, even = total // rows, 1 - lax.axis_index("slab") % 2
 
     def energy_at(index):
-        return standing(index // rows, parts) * energies + index % energies
+        return standing(index // rows, parts, even) * energies + index % energies
 
     lane = lax.broadcasted_iota(jnp.int32, (ROWS, LANES), 1)
     row = lax.broadcasted_iota(jnp.int32, (ROWS, LANES), 0)

time: 82.6 us -> 81 us (0.981)
  blocking collectives: 61.3 us -> 58.7 us
  starting transfers between devices: 0.67 us -> 1.81 us
    all_to_all x4, blocking collectives: 61.3 us -> 58.7 us  [exchanged(): lax.all_to_all(shares, ('energy', 'slab'), 0, 0, axis_index_groups=groups)]
    ppermute x3, starting transfers between devices: 0.67 us -> 1.81 us  [beside(): return lax.ppermute(block, 'slab', [(0, 1), (1, 0)])]
where the time goes in v14:
time: 81 us; the launch traced here: 80.5 us
  blocking collectives  58.7 us (72%)
  Pallas kernels  18.1 us (22%)
  starting transfers between devices  1.81 us (2%)
  waiting for transfers between devices  1.21 us (1%)
    all_to_all x4, blocking collectives, exchanged(): lax.all_to_all(shares, ('energy', 'slab'), 0, 0, axis_index_groups=groups)  58.7 us
    pallas_call x7, Pallas kernels, call(): pl.pallas_call(kernel, out_shape=shapes, in_specs=spaces or [vmem] * len(...  18.1 us
    ppermute x3, starting transfers between devices, beside(): return lax.ppermute(block, 'slab', [(0, 1), (1, 0)])  1.81 us
  transfers between devices with their start and end apart: 3, of which 1 were waited for; matrix products, arithmetic and copies ran while one was open for 0% of the time, Pallas kernels for 2%

profile of v14, /device:TPU:0, one launch (start us, length us, event | category | flops | bytes accessed | tf_op | source)
XLA Modules:
  0.0 80.5 jit_solution(7931202477525013152)
XLA Ops:
  0.6 0.5 collective-permute-start
  1.1 0.1 collective-permute-start.1
  1.2 1.9 %shard_map.95 = (f32[1152,128]{1,0:T(8,128)S(1)}, f32[576,128]{1,0:T(8,128)S(1)}, f32[1152,128]{1,0:T(8,128)S(1)}, f32[64,64]{1,0:T(8,128)S(1)}, f32[6912,128]{1...) custom-call(f32[2,144,128]{2,1,0:T(8,128)} %refs_3_.3, f32[2,144,128]{2,1,0:T(8,128)} %refs_4_.3, ...), custom_call_target="tpu_custom_call" | custom-call | flops 884736 | bytes 6413056 | tf_op jit(solution)/shard_map/pallas_call | solution.py:335
  3.2 0.0 collective-permute-done.refs_0_
  3.2 0.0 collective-permute-done.1.refs_1_
  3.2 6.7 %shard_map.96 = f32[144,4,128]{2,1,0:T(4,128)S(1)} custom-call(f32[1152,128]{1,0:T(8,128)S(1)} %get-tuple-element.12.own.free, f32[2,144,128]{2,1,0:T(8,128)S(1)} %collective-permute-done.refs_0_, f32[2,144,128]{2,1,0:T(8,128)S(1)} %collective-permute-done.1.refs_1_, s32[6,8,128]{2,1,0:T(8,128)S(1)} %get-tuple-element.13.refs_2_.refs_1_, ...), custom_call_target="tpu_custom_call" | custom-call | flops 42467328 | bytes 4767744 | tf_op jit(solution)/shard_map/pallas_call | solution.py:335
  9.9 17.8 %all_to_all.20.blocks = f32[16,9,4,128]{3,2,1,0:T(4,128)S(1)} all-to-all(f32[16,9,4,128]{3,2,1,0:T(4,128)S(1)} %bitcast.12), channel_id=1, replica_groups={{30,22,14,6,28,20,12,4,26,18,10,2,24,16,8,0},{1,9,17,25,3,11,19,27,5,13..., dimensions={0} | all-to-all | bytes 589824 | tf_op jit(solution)/shard_map/all_to_all | solution.py:52
  27.7 0.4 shard_map.97
  28.2 13.4 %all_to_all.21 = f32[16,9,4,128]{3,2,1,0:T(4,128)S(1)} all-to-all(f32[16,9,4,128]{3,2,1,0:T(4,128)S(1)} %shard_map.97), channel_id=1, replica_groups={{30,22,14,6,28,20,12,4,26,18,10,2,24,16,8,0},{1,9,17,25,3,11,19,27,5,13..., dimensions={0} | all-to-all | bytes 589824 | tf_op jit(solution)/shard_map/all_to_all | solution.py:52
  41.6 0.6 shard_map.98
  42.2 0.0 copy-start
  42.2 0.0 copy-start.1
  42.2 1.2 %collective-permute-start.2 = (f32[144,4,128]{2,1,0:T(4,128)S(1)}, f32[144,4,128]{2,1,0:T(4,128)S(1)}, u32[]{:S(2)}, u32[]{:S(2)}) collective-permute-start(f32[144,4,128]{2,1,0:T(4,128)S(1)} %get-tuple-element.19), channel_id=1, source_target_pairs={{0,1},{1,0},{2,3},{3,2},{4,5},{5,4},{6,7},{7,6},{8,9},{9,8},{10,11... | collective-permute-start | bytes 884744 | tf_op jit(solution)/shard_map/ppermute | solution.py:351
  43.4 1.2 %collective-permute-done.2.refs_0_ = f32[144,4,128]{2,1,0:T(4,128)S(1)} collective-permute-done((f32[144,4,128]{2,1,0:T(4,128)S(1)}, f32[144,4,128]{2,1,0:T(4,128)S(1)}, u32[]{:S(2)}, u32[]{:S(2)}) %collective-permute-start.2) | collective-permute-done | bytes 294944 | tf_op jit(solution)/shard_map/ppermute | solution.py:351
  44.6 6.7 %shard_map.99 = f32[144,4,128]{2,1,0:T(4,128)S(1)} custom-call(f32[1152,128]{1,0:T(8,128)S(1)} %get-tuple-element.18.own, f32[144,4,128]{2,1,0:T(4,128)S(1)} %collective-permute-done.2.refs_0_, s32[6,8,128]{2,1,0:T(8,128)S(1)} %get-tuple-element.13.refs_2_.refs_1_, s32[6,8,128]{2,1,0:T(8,128)S(1)} %get-tuple-element.14.refs_3_.refs_2_, ...), custom_call_target="tpu_custom_call" | custom-call | flops 42467328 | bytes 4767744 | tf_op jit(solution)/shard_map/pallas_call | solution.py:335
  51.3 13.5 %all_to_all.22.blocks = f32[16,9,4,128]{3,2,1,0:T(4,128)S(1)} all-to-all(f32[16,9,4,128]{3,2,1,0:T(4,128)S(1)} %bitcast.11), channel_id=1, replica_groups={{30,22,14,6,28,20,12,4,26,18,10,2,24,16,8,0},{1,9,17,25,3,11,19,27,5,13..., dimensions={0} | all-to-all | bytes 589824 | tf_op jit(solution)/shard_map/all_to_all | solution.py:52
  64.8 0.4 shard_map.100
  65.3 13.9 %all_to_all.23 = f32[16,9,4,128]{3,2,1,0:T(4,128)S(1)} all-to-all(f32[16,9,4,128]{3,2,1,0:T(4,128)S(1)} %shard_map.100), channel_id=1, replica_groups={{30,22,14,6,28,20,12,4,26,18,10,2,24,16,8,0},{1,9,17,25,3,11,19,27,5,13..., dimensions={0} | all-to-all | bytes 589824 | tf_op jit(solution)/shard_map/all_to_all | solution.py:52
  79.2 0.0 copy-done
  79.2 0.0 copy-done.1
  79.2 1.3 %shard_map.101 = (f32[2,144,128]{2,1,0:T(8,128)}, f32[2,144,128]{2,1,0:T(8,128)}) custom-call(f32[144,4,128]{2,1,0:T(4,128)S(1)} %bitcast.16, f32[72,8,128]{2,1,0:T(8,128)S(1)} %bitcast.15, f32[144,8,128]{2,1,0:T(8,128)S(1)} %bitcast.10, f32[2,144,128]{2,1,0:T(8,128)S(1)} %copy-done, f32[2,144,128]{2,1,0:T(8,128)S(1)} %copy-done.1), custom_call_target="tpu_custom_call" | custom-call | flops 3538944 | bytes 1769472 | tf_op jit(solution)/shard_map/pallas_call | solution.py:335
Async XLA Ops:
  0.6 2.5 %collective-permute-start = (f32[2,144,128]{2,1,0:T(8,128)}, f32[2,144,128]{2,1,0:T(8,128)S(1)}, u32[]{:S(2)}, u32[]{:S(2)}) collective-permute-start(f32[2,144,128]{2,1,0:T(8,128)} %refs_3_.3), channel_id=1, source_target_pairs={{0,1},{1,0},{2,3},{3,2},{4,5},{5,4},{6,7},{7,6},{8,9},{9,8},{10,11... | collective-permute-start | bytes 442376 | tf_op jit(solution)/shard_map/ppermute | solution.py:351
  1.1 2.0 %collective-permute-start.1 = (f32[2,144,128]{2,1,0:T(8,128)}, f32[2,144,128]{2,1,0:T(8,128)S(1)}, u32[]{:S(2)}, u32[]{:S(2)}) collective-permute-start(f32[2,144,128]{2,1,0:T(8,128)} %refs_4_.3), channel_id=1, source_target_pairs={{0,1},{1,0},{2,3},{3,2},{4,5},{5,4},{6,7},{7,6},{8,9},{9,8},{10,11... | collective-permute-start | bytes 442376 | tf_op jit(solution)/shard_map/ppermute | solution.py:351
  42.2 37.0 %copy-start = (f32[2,144,128]{2,1,0:T(8,128)S(1)}, f32[2,144,128]{2,1,0:T(8,128)}, u32[]{:S(2)}) copy-start(f32[2,144,128]{2,1,0:T(8,128)} %refs_3_.3) | copy-start | bytes 442372
  42.2 37.0 %copy-start.1 = (f32[2,144,128]{2,1,0:T(8,128)S(1)}, f32[2,144,128]{2,1,0:T(8,128)}, u32[]{:S(2)}) copy-start(f32[2,144,128]{2,1,0:T(8,128)} %refs_4_.3) | copy-start | bytes 442372
  42.2 2.4 %collective-permute-start.2 = (f32[144,4,128]{2,1,0:T(4,128)S(1)}, f32[144,4,128]{2,1,0:T(4,128)S(1)}, u32[]{:S(2)}, u32[]{:S(2)}) collective-permute-start(f32[144,4,128]{2,1,0:T(4,128)S(1)} %get-tuple-element.19), channel_id=1, source_target_pairs={{0,1},{1,0},{2,3},{3,2},{4,5},{5,4},{6,7},{7,6},{8,9},{9,8},{10,11... | collective-permute-start | bytes 884744 | tf_op jit(solution)/shard_map/ppermute | solution.py:351
